TPU v7x, 32 devices: a whole 2x2x4 slice. The times are simulated.
32 devices in a mesh: groups: 2 (over x), cells: 4 (over y, core), blocks: 4 (over z).
Axes of the slice: x: 2, y: 2, z: 4, core: 2. Of those that a mesh axis runs over, the one named last changes fastest.
Arguments:
- expression: bfloat16 [8192, 4096], P(('groups', 'cells'), 'blocks'), parts along dimension 0, as said below
Outputs:
- adjacency: float32 [8192, 4096], P(('groups', 'blocks'), 'cells'), parts along dimension 0
There are 2 independent parts, one for each index of `groups`. A program takes and returns all parts, laid end to end along the dimension named above; each array names one. Nothing has to cross between parts.
Inputs may be any that keep to these rules, and one draw needn't show every extreme that they name: `expression`: every gene has a nonzero noise part, so every variance is positive.
All inputs are finite; a program needn't handle non-finite values.
Results may differ from a plain program's by a relative error of at most 0.0003.
Values sent between devices are 32-bit elements; how exact they have to be, the bound alone decides.
No kernel may reach another device: no remote copies, remote signals or barrier semaphores. Data moves between devices by JAX's collectives and lax.ppermute only.
A program may use at most 128 MiB of HBM per device.

v0:
```python
import jax
import jax.numpy as jnp
from jax import lax
from jax.sharding import PartitionSpec as P


def from_behind(shard, axis, by):
    peers = lax.axis_size(axis)
    return lax.ppermute(shard, axis, [(i, (i + by) % peers) for i in range(peers)])


def cross_gram(left, right):
    return lax.dot_general(
        left,
        right,
        (((0,), (0,)), ((), ())),
        preferred_element_type=jnp.float32,
        precision=lax.Precision.HIGHEST,
    )


def local(expression):
    rows, width = expression.shape
    cell_count = lax.axis_size("cells")
    block_count = lax.axis_size("blocks")
    genes = width * block_count
    values = expression.astype(jnp.float32)
    column_total = lax.psum(jnp.sum(values, axis=0), "cells")
    mean = column_total / (rows * cell_count)
    centred = values - mean[None, :]
    row_variance = lax.psum(jnp.sum(centred * centred, axis=0), "cells")
    every_variance = lax.all_gather(row_variance, "blocks", axis=0, tiled=True)
    mine = lax.axis_index("blocks")
    partial_value = jnp.zeros((width, genes), jnp.float32)
    current = centred
    for step in range(block_count):
        if step > 0:
            current = from_behind(current, "blocks", 1)
        source = (mine - step) % block_count
        partial_value = lax.dynamic_update_slice_in_dim(
            partial_value, cross_gram(centred, current), source * width, 1
        )
    tile = lax.psum_scatter(partial_value, "cells", scatter_dimension=1, tiled=True)
    column_start = lax.axis_index("cells") * tile.shape[1]
    column_variance = lax.dynamic_slice_in_dim(every_variance, column_start, tile.shape[1])
    ratio = tile / jnp.sqrt(row_variance[:, None] * column_variance[None, :])
    return ((1.0 + ratio) / 2.0) ** 6


def solution(mesh):
    placed = (P(("groups", "cells"), "blocks"),)
    return jax.shard_map(
        local,
        mesh=mesh,
        in_specs=placed,
        out_specs=P(("groups", "blocks"), "cells"),
        check_vma=False,
    )
```

profile of v0, /device:TPU:5, one launch (start us, length us, event | category | flops | bytes accessed | tf_op | source)
XLA Modules:
  0.0 450.7 jit_solution(7566980970017823094)
XLA Ops:
  6.5 0.0 reduce-scatter.2.cloned.1.call-start
  6.5 2.0 convert_reduce_fusion
  8.5 5.7 %psum.14 = f32[1024]{0:T(1024)S(1)} all-reduce(f32[1024]{0:T(1024)S(1)} %convert_reduce_fusion), channel_id=1, replica_groups=mesh['groups'=2,'cells'=4,'blocks'=4] {'cells'}, use_global_device_ids=true, to_apply=%region_1.0 | all-reduce | flops 1024 | bytes 8192 | tf_op jit(solution)/shard_map/psum | solution.py:28
  14.2 2.4 multiply_reduce_fusion
  16.6 1.3 collective-permute-start
  17.9 92.0 %collective-permute-done = f32[1024,1024]{1,0:T(8,128)S(1)} collective-permute-done((f32[1024,1024]{1,0:T(8,128)S(1)}, f32[1024,1024]{1,0:T(8,128)S(1)}, u32[]{:S(2)}, u32[]{:S(2)}) %collective-permute-start) | collective-permute-done | bytes 4194336 | tf_op jit(solution)/shard_map/ppermute | solution.py:9
  110.0 0.0 copy-start.1
  110.0 2.0 copy-done.1
  112.0 0.0 collective-permute-start.1
  112.0 92.4 %collective-permute-done.1 = f32[1024,1024]{1,0:T(8,128)} collective-permute-done((f32[1024,1024]{1,0:T(8,128)S(1)}, f32[1024,1024]{1,0:T(8,128)}, u32[]{:S(2)}, u32[]{:S(2)}) %collective-permute-start.1) | collective-permute-done | bytes 4194336 | tf_op jit(solution)/shard_map/ppermute | solution.py:9
  204.4 0.0 collective-permute-start.2
  204.4 7.8 %broadcast_in_dim.2 = f32[1024,4096]{1,0:T(8,128)} broadcast(f32[]{:T(128)} %constant.43.clone.1), dimensions={} | broadcast | bytes 16777220 | tf_op jit(solution)/shard_map/broadcast_in_dim | solution.py:34
  212.3 0.0 copy-done
  212.3 15.1 %fusion.7 = f32[1024,4096]{1,0:T(8,128)} fusion(f32[1024,4096]{1,0:T(8,128)} %broadcast_in_dim.2, s32[]{:T(128)S(6)} %select_n.35, bf16[1024,1024]{1,0:T(8,128)(2,1)S(1)} %copy-done, f32[1024]{0:T(1024)S(1)} %broadcast_multiply_fusion), kind=kOutput, calls=%fused_computation.11 | convolution fusion | flops 12886999040 | bytes 6295556 | tf_op jit(solution)/shard_map/dot_general | solution.py:13
  227.4 0.0 copy-done.2
  227.4 14.8 %fusion.4 = f32[1024,4096]{1,0:T(8,128)} fusion(f32[1024,4096]{1,0:T(8,128)} %fusion.7, s32[]{:T(128)S(6)} %select_n.37, f32[1024,1024]{1,0:T(8,128)S(1)} %copy-done.2, bf16[1024,1024]{1,0:T(8,128)(2,1)S(1)} %copy-done, f32[1024]{0:T(1024)S(1)} %broadcast_multiply_fusion), kind=kOutput, calls=%fused_computation.8 | convolution fusion | flops 12886999040 | bytes 10489860 | tf_op jit(solution)/shard_map/dot_general | solution.py:13
  242.2 16.4 %fusion.5 = f32[1024,4096]{1,0:T(8,128)} fusion(f32[1024,4096]{1,0:T(8,128)} %fusion.4, s32[]{:T(128)S(6)} %select_n.39, f32[1024,1024]{1,0:T(8,128)} %collective-permute-done.1, bf16[1024,1024]{1,0:T(8,128)(2,1)S(1)} %copy-done, f32[1024]{0:T(1024)S(1)} %broadcast_multiply_fusion), kind=kOutput, calls=%fused_computation.9 | convolution fusion | flops 12886999040 | bytes 10489860 | tf_op jit(solution)/shard_map/dot_general | solution.py:13
  258.7 37.5 %collective-permute-done.2 = f32[1024,1024]{1,0:T(8,128)} collective-permute-done((f32[1024,1024]{1,0:T(8,128)}, f32[1024,1024]{1,0:T(8,128)}, u32[]{:S(2)}, u32[]{:S(2)}) %collective-permute-start.2) | collective-permute-done | bytes 4194336 | tf_op jit(solution)/shard_map/ppermute | solution.py:9
  296.2 16.4 %fusion.6 = f32[1024,4096]{1,0:T(8,128)} fusion(f32[1024,4096]{1,0:T(8,128)} %fusion.5, s32[]{:T(128)S(6)} %select_n.41, f32[1024,1024]{1,0:T(8,128)} %collective-permute-done.2, bf16[1024,1024]{1,0:T(8,128)(2,1)S(1)} %copy-done, f32[1024]{0:T(1024)S(1)} %broadcast_multiply_fusion), kind=kOutput, calls=%fused_computation.10 | convolution fusion | flops 12886999040 | bytes 10489860 | tf_op jit(solution)/shard_map/dot_general | solution.py:13
  312.6 0.0 reduce-scatter.2.cloned.1.call-update
  312.6 8.4 %psum.15 = f32[1024]{0:T(1024)S(1)} all-reduce(f32[1024]{0:T(1024)S(1)} %get-tuple-element.5), channel_id=1, replica_groups=mesh['groups'=2,'cells'=4,'blocks'=4] {'cells'}, use_global_device_ids=true, to_apply=%region_4.5 | all-reduce | flops 1024 | bytes 8192 | tf_op jit(solution)/shard_map/psum | solution.py:31
  321.0 10.2 %all_gather.3 = f32[4096]{0:T(1024)S(1)} all-gather(f32[1024]{0:T(1024)S(1)} %psum.15), channel_id=1, replica_groups=mesh['groups'=2,'cells'=4,'blocks'=4] {'blocks'}, dimensions={0}, use_global_device_ids=true | all-gather | bytes 20480 | tf_op jit(solution)/shard_map/all_gather | solution.py:32
  331.2 107.2 %reduce-scatter.2.cloned.1.call-done = f32[1024,1024]{1,0:T(8,128)} async-done(((f32[1024,4096]{1,0:T(8,128)}), f32[1024,1024]{1,0:T(8,128)}) %reduce-scatter.2.cloned.1.call-update) | async-done | bytes 4194320 | tf_op jit(solution)/shard_map/reduce_scatter | solution.py:43
  438.5 5.4 %multiply_multiply_fusion = f32[1024,1024]{1,0:T(8,128)} fusion(f32[1024,1024]{1,0:T(8,128)} %reduce-scatter.2.cloned.1.call-done, f32[1024]{0:T(1024)S(1)} %dynamic_slice.3, f32[1024]{0:T(1024)S(1)} %psum.15), kind=kLoop, calls=%fused_computation | loop fusion | flops 7340032 | bytes 8396800 | tf_op jit(solution)/shard_map/mul | solution.py:47
  (4 shorter events, 0.0 us)
Async XLA Ops:
  6.5 431.9 %reduce-scatter.2.cloned.1.call-start = ((), (), s32[]{:S(2)}) async-start(), calls=%async_computation.1 | async-start | bytes 20971520 | tf_op jit(solution)/shard_map/reduce_scatter | solution.py:43
  16.6 93.4 %collective-permute-start = (f32[1024,1024]{1,0:T(8,128)S(1)}, f32[1024,1024]{1,0:T(8,128)S(1)}, u32[]{:S(2)}, u32[]{:S(2)}) collective-permute-start(f32[1024,1024]{1,0:T(8,128)S(1)} %get-tuple-element.6), channel_id=1, source_target_pairs={{0,1},{1,2},{2,3},{3,0},{4,5},{5,6},{6,7},{7,4},{8,9},{9,10},{10,1... | collective-permute-start | bytes 12582920 | tf_op jit(solution)/shard_map/ppermute | solution.py:9
  110.0 2.0 copy-start.1
  112.0 92.4 %collective-permute-start.1 = (f32[1024,1024]{1,0:T(8,128)S(1)}, f32[1024,1024]{1,0:T(8,128)}, u32[]{:S(2)}, u32[]{:S(2)}) collective-permute-start(f32[1024,1024]{1,0:T(8,128)S(1)} %collective-permute-done), channel_id=1, source_target_pairs={{0,1},{1,2},{2,3},{3,0},{4,5},{5,6},{6,7},{7,4},{8,9},{9,10},{10,1... | collective-permute-start | bytes 12582920 | tf_op jit(solution)/shard_map/ppermute | solution.py:9
  204.4 91.7 %collective-permute-start.2 = (f32[1024,1024]{1,0:T(8,128)}, f32[1024,1024]{1,0:T(8,128)}, u32[]{:S(2)}, u32[]{:S(2)}) collective-permute-start(f32[1024,1024]{1,0:T(8,128)} %collective-permute-done.1), channel_id=1, source_target_pairs={{0,1},{1,2},{2,3},{3,0},{4,5},{5,6},{6,7},{7,4},{8,9},{9,10},{10,1... | collective-permute-start | bytes 12582920 | tf_op jit(solution)/shard_map/ppermute | solution.py:9
  204.4 7.8 %copy-start = (bf16[1024,1024]{1,0:T(8,128)(2,1)S(1)}, bf16[1024,1024]{1,0:T(8,128)(2,1)}, u32[]{:S(2)}) copy-start(bf16[1024,1024]{1,0:T(8,128)(2,1)} %param.1) | copy-start | bytes 6291460
  212.3 15.1 %copy-start.2 = (f32[1024,1024]{1,0:T(8,128)S(1)}, f32[1024,1024]{1,0:T(8,128)}, u32[]{:S(2)}) copy-start(f32[1024,1024]{1,0:T(8,128)} %copy-done.1) | copy-start | bytes 12582916
Sparse Core Ops, SparseCore 0:
  312.7 125.6 reduce-scatter.1
where the time goes:
time: 454 us; the launch traced here: 451 us
  waiting for transfers between devices  329 us (72%)
  matrix products  62.8 us (14%)
  blocking collectives  24.4 us (5%)
  between operations  13.4 us (3%)
  local copies, waits for them, and re-layouts  9.84 us (2%)
  other arithmetic  9.74 us (2%)
    ppermute x3, waiting for transfers between devices, from_behind(): lax.ppermute(shard, axis, [(i, (i + by) % peers) for i in range(peers)])  222 us
    reduce_scatter x1, waiting for transfers between devices, local(): lax.psum_scatter(partial_value, 'cells', scatter_dimension=1, tiled=True)  107 us
    dot_general x4, matrix products, cross_gram(): lax.dot_general(left, right, (((0,), (0,)), ((), ())), preferred_element_...  62.8 us
    all_gather x1, blocking collectives, local(): every_variance = lax.all_gather(row_variance, 'blocks', axis=0, tiled=True)  10.2 us
  transfers between devices with their start and end apart: 4, of which 4 were waited for; matrix products, arithmetic and copies ran while one was open for 12% of the time, Pallas kernels for 0%

commit v1 on v0

v1 whole, which is shorter than its diff:
```python
import functools

import jax
import jax.numpy as jnp
from jax import lax
from jax.experimental import pallas as pl
from jax.experimental.pallas import tpu as pltpu
from jax.sharding import PartitionSpec as P

BOTH = ("cells", "blocks")
TILE = 256
FAR_WIDTHS = (2, 1, 1)
f32, bf16 = jnp.float32, jnp.bfloat16
ANYWHERE = pl.BlockSpec(memory_space=pl.ANY)


def call(kernel, *, grid, in_specs, out_specs, out_shape, scratch=(), scalars=0, aliases=None):
    return pl.pallas_call(
        kernel,
        grid_spec=pltpu.PrefetchScalarGridSpec(
            num_scalar_prefetch=scalars,
            grid=grid,
            in_specs=in_specs,
            out_specs=out_specs,
            scratch_shapes=scratch,
        ),
        out_shape=out_shape,
        input_output_aliases=aliases or {},
        cost_estimate=pl.CostEstimate(flops=1, bytes_accessed=1, transcendentals=0),
        compiler_params=pltpu.CompilerParams(vmem_limit_bytes=48 << 20),
    )


def shape(*dims):
    return jax.ShapeDtypeStruct(dims, f32)


def split(value):
    high = value.astype(bf16)
    return high, (value - high.astype(f32)).astype(bf16)


def centre_kernel(x_ref, centred_ref, turned_ref, mean_ref, spread_ref):
    value = x_ref[...].astype(f32)
    mean = jnp.sum(value, axis=0, keepdims=True) / value.shape[0]
    value = value - mean
    centred_ref[...] = value
    turned_ref[...] = value.T
    mean_ref[...] = mean
    spread_ref[...] = jnp.sum(value * value, axis=0, keepdims=True)


def centre(expression):
    rows, width = expression.shape
    column = pl.BlockSpec((rows, TILE), lambda g: (0, g))
    line = pl.BlockSpec((1, TILE), lambda g: (0, g))
    return call(
        centre_kernel,
        grid=(width // TILE,),
        in_specs=[column],
        out_specs=[column, pl.BlockSpec((TILE, rows), lambda g: (g, 0)), line, line],
        out_shape=[shape(rows, width), shape(width, rows), shape(1, width), shape(1, width)],
    )(expression)


def copy_kernel(from_ref, *refs):
    refs[-1][...] = from_ref[...]


def columns(source, start, size, *earlier):
    rows = source.shape[0]
    return call(
        copy_kernel,
        grid=(rows // TILE,),
        in_specs=[pl.BlockSpec((TILE, size), lambda i: (i, start // size))]
        + [ANYWHERE] * len(earlier),
        out_specs=pl.BlockSpec((TILE, size), lambda i: (i, 0)),
        out_shape=shape(rows, size),
    )(source, *earlier)


def three(left, right, contract):
    def dot(a, b):
        return lax.dot_general(a, b, (contract, ((), ())), preferred_element_type=f32)

    (left_high, left_low), (right_high, right_low) = left, right
    return dot(left_high, right_high) + (dot(left_high, right_low) + dot(left_low, right_high))


def spans(width):
    return [slice(start, min(start + 512, width)) for start in range(0, width, 512)]


def own_kernel(turned_ref, out_ref, high_ref, low_ref):
    step = pl.program_id(0)

    @pl.when(step == 0)
    def _():
        high_ref[...], low_ref[...] = split(turned_ref[...])

    rows = pl.ds(pl.multiple_of(step * TILE, TILE), TILE)
    left = high_ref[rows], low_ref[rows]
    for span in spans(out_ref.shape[1]):
        out_ref[:, span] = three(left, (high_ref[span], low_ref[span]), ((1,), (1,)))


def own_gram(turned):
    width, cells = turned.shape
    whole = pl.BlockSpec((width, cells), lambda i: (0, 0))
    out_sum, *parts = call(
        own_kernel,
        grid=(width // TILE,),
        in_specs=[whole],
        out_specs=[pl.BlockSpec((TILE, width), lambda i: (i, 0)), whole, whole],
        out_shape=[shape(width, width)] + [jax.ShapeDtypeStruct((width, cells), bf16)] * 2,
    )(turned)
    return out_sum, parts


def pair_kernel(left_high, left_low, right_high, right_low, *refs):
    out_ref = refs[-1]
    left = left_high[...], left_low[...]
    for span in spans(out_ref.shape[1]):
        out_ref[:, span] = three(left, (right_high[span], right_low[span]), ((1,), (1,)))


def pair_gram(own, pair, *earlier):
    width, cells = own[0].shape
    whole = pl.BlockSpec((width, cells), lambda i: (0, 0))
    return call(
        pair_kernel,
        grid=(width // TILE,),
        in_specs=[pl.BlockSpec((TILE, cells), lambda i: (i, 0))] * 2
        + [whole] * 2
        + [ANYWHERE] * len(earlier),
        out_specs=pl.BlockSpec((TILE, width), lambda i: (i, 0)),
        out_shape=shape(width, width),
    )(*own, *pair, *earlier)


def both_kernel(pair_is_split, core_ref, own_high, own_low, *refs):
    right_high, right_low = refs[-2:]
    if pair_is_split:
        pair_high, pair_low, right_ref = refs[:3]
        out_ref = refs[-3]
        pair = pair_high[...], pair_low[...]
    else:
        pair_ref, right_ref = refs[:2]
        out_ref, pair_high, pair_low = refs[-5:-2]
        pair = split(pair_ref[...])
        pair_high[...], pair_low[...] = pair

    @pl.when(pl.program_id(0) == 0)
    def _():
        right_high[...], right_low[...] = split(right_ref[...])

    core = core_ref[0]
    for span in spans(out_ref.shape[2]):
        right = right_high[:, span], right_low[:, span]
        out_ref[core, :, span] = three((own_high[...], own_low[...]), right, ((1,), (0,)))
        out_ref[1 - core, :, span] = three(pair, right, ((1,), (0,)))


def both_grams(core, own, pair, right, *earlier):
    width, cells = own[0].shape
    size = right.shape[1]
    left = pl.BlockSpec((TILE, cells), lambda i, core: (i, 0))
    is_split = len(pair) == 2
    extra = 0 if is_split else 2
    out = call(
        functools.partial(both_kernel, is_split),
        scalars=1,
        grid=(width // TILE,),
        in_specs=[left] * (2 + len(pair))
        + [pl.BlockSpec((cells, size), lambda i, core: (0, 0))]
        + [ANYWHERE] * len(earlier),
        out_specs=[pl.BlockSpec((2, TILE, size), lambda i, core: (0, i, 0))] + [left] * extra,
        out_shape=[shape(2, width, size)]
        + [jax.ShapeDtypeStruct((width, cells), bf16)] * extra,
        scratch=[pltpu.VMEM((cells, size), bf16)] * 2,
    )(core, *own, *pair, right, *earlier)
    return out[0], (pair if is_split else out[1:])


def power_six(ratio):
    half = (1.0 + ratio) * 0.5
    square = half * half
    return square * square * square


def finish_kernel(flags, *refs):
    own, own_far, pair, pair_far, mid, mid_first, mid_second, far, far_first, far_second = refs[:10]
    rs, cs, offset = refs[10:13]
    out_ref = refs[-1]
    for kind, (left, other, right) in enumerate(
        ((own, own, own_far), (pair, pair, pair_far), (mid, mid_second, mid_first), (far, far_second, far_first))
    ):
        for outer in range(2) if kind > 1 else (None,):
            now = flags[0] == kind
            if outer is not None:
                now &= flags[1] == outer

            @pl.when(now)
            def _():
                tile = (other if outer else left)[...] + right[...]
                out_ref[...] = power_six(tile * rs[...] * cs[...] + offset[...])


def finish(flags, near, mid, far, scales, before, start, mid_start):
    (row_scale, column_scale, offset), (width, size) = scales, far[0].shape

    def spec(column, kinds, outer=None):
        def index(i, flags):
            used = flags[0] == kinds
            if outer is not None:
                used &= flags[1] == outer
            return jnp.where(used, i, 0), column

        return pl.BlockSpec((TILE, size), index)

    column, mid_column = start // size, (start - mid_start) // size
    here = pl.BlockSpec((TILE, size), lambda i, flags: (i, column))
    in_specs = [spec(column, 0)] * 2 + [spec(column, 1)] * 2
    in_specs += [spec(mid_column, 2, 0), spec(mid_column, 2), spec(mid_column, 2, 1)]
    in_specs += [spec(0, 3, 0), spec(0, 3), spec(0, 3, 1)]
    in_specs += [
        pl.BlockSpec((TILE, 1), lambda i, flags: (i, 0)),
        pl.BlockSpec((1, size), lambda i, flags: (0, column)),
        here,
    ]
    operands = [flags, *near, *mid, *far, row_scale, column_scale, offset]
    aliases = {}
    if before is not None:
        aliases = {len(operands): 0}
        in_specs.append(ANYWHERE)
        operands.append(before)
    return call(
        finish_kernel,
        scalars=1,
        grid=(width // TILE,),
        in_specs=in_specs,
        out_specs=here,
        out_shape=shape(*offset.shape),
        aliases=aliases,
    )(*operands)


def cross_gram(left, right):
    return lax.dot_general(
        left,
        right,
        (((0,), (0,)), ((), ())),
        preferred_element_type=f32,
        precision=lax.Precision.HIGH,
    )


def pieces(width, shares):
    unit = width // sum(shares)
    starts = [unit * sum(shares[:i]) for i in range(len(shares))]
    return [(start, unit * share) for start, share in zip(starts, shares)]


def local_statistics(values):
    mean = jnp.sum(values, axis=0) / values.shape[0]
    shifted = values - mean[None, :]
    return shifted, mean, jnp.sum(shifted * shifted, axis=0)


def statistics(rows, mean, spread):
    shards = lax.all_gather(jnp.stack([mean, spread]), "cells")
    away = shards[:, 0] - jnp.mean(shards[:, 0], axis=0)[None, :]
    variance = jnp.sum(shards[:, 1], axis=0) + rows * jnp.sum(away * away, axis=0)
    return away, variance


def on_a_line(expression):
    rows, width = expression.shape
    z = lax.axis_index("blocks")
    k = lax.axis_index("cells")
    mid_of, far_of = (2, 2, 1, 1), (3, 3, 0, 0)
    own_owner, pair_owner = (0, 1, 2, 3), (1, 0, 3, 2)
    mid_id, far_id = jnp.where(z < 2, 2, 1), jnp.where(z < 2, 3, 0)
    outer = (z == 0) | (z == 3)
    kind = jnp.where(k == z, 0, jnp.where(k == (z ^ 1), 1, jnp.where(k == mid_id, 2, 3)))
    flags = jnp.stack([kind, outer.astype(kind.dtype)]).astype(jnp.int32)
    mid_core, far_core = (mid_id % 2).astype(jnp.int32)[None], (far_id % 2).astype(jnp.int32)[None]

    def between(part, pairs, name):
        with jax.named_scope(name):
            return lax.ppermute(part, BOTH, [(a * 4 + b, c * 4 + d) for (a, b), (c, d) in pairs])

    def along(part, pairs, name):
        with jax.named_scope(name):
            return lax.ppermute(part, "blocks", pairs)

    def to_core(part, owner, name):
        pairs = [(2 * y + owner[b] % 2, b) for y in range(2) for b in range(4)]
        return part + between(part, [((i ^ 1, b), (i, b)) for i, b in pairs], name)

    def to_lane(part, owner, name):
        return between(part, [((owner[b] ^ 2, b), (owner[b], b)) for b in range(4)], name)

    def over_cores(parts):
        got = lax.all_to_all(parts, "cells", 0, 0, axis_index_groups=[[0, 1], [2, 3]], tiled=True)
        return got[0] + got[1]

    def onward(part, owner, name):
        first = [((owner[b] ^ 2, b), (owner[b], b)) for b in (1, 2)]
        first += [((owner[b] ^ 3, b), (owner[b], b ^ 1)) for b in (1, 2)]
        second = [((owner[b] ^ 1, b), (owner[b], b ^ 1)) for b in (1, 2)]
        return between(part, first, name + "_first"), between(part, second, name + "_second")

    centred, turned, mean, spread = centre(expression)
    mid_got = along(centred, [(1, 2), (2, 1)], "mid_block")
    pair_got = along(turned, [(0, 1), (1, 0), (2, 3), (3, 2)], "pair_block")
    far = pieces(width, FAR_WIDTHS)

    def send_far(part, *earlier):
        value = columns(centred, *far[part], *earlier)
        return along(value, [(0, 2), (3, 1)], "far_block")

    own_sum, own = own_gram(turned)
    far_got = [send_far(0, own_sum)]
    own_sum = to_core(own_sum, own_owner, "own_core")
    own_far = to_lane(own_sum, own_owner, "own_lane")
    away, variance = statistics(rows, mean[0], spread[0])
    mine = jnp.concatenate([away, variance[None, :], jnp.zeros((3, width), f32)])
    column = jnp.where(k == z, mine, 0.0)
    for by in (1, 2, 3):
        column += between(mine, [((i, i), (i, (i + by) % 4)) for i in range(4)], "moments")
    far_got.append(send_far(1, column))

    parts, pair = both_grams(mid_core, own, (pair_got,), mid_got, own_far, column)
    mid_sum = over_cores(parts)
    mid = (mid_sum, *onward(mid_sum, mid_of, "mid_sum"))
    pair_sum = pair_gram(own, pair, parts)
    last = (mid_sum, pair_sum)
    far_got.append(send_far(2, pair_sum))
    pair_sum = to_core(pair_sum, pair_owner, "pair_core")
    pair_far = to_lane(pair_sum, pair_owner, "pair_lane")
    fars = []
    waits = [(), mid[1:], (pair_far,)]
    for got, wait in zip(far_got, waits):
        parts, _ = both_grams(far_core, own, pair, got, *last, *wait)
        far_sum = over_cores(parts)
        last = (far_sum,)
        fars.append((far_sum, *onward(far_sum, far_of, "far_sum")))

    row_scale = 1.0 / jnp.sqrt(variance)
    column_scale = 1.0 / jnp.sqrt(column[4])
    offset = rows * lax.dot_general(
        away * row_scale[None, :],
        column[:4] * column_scale[None, :],
        (((0,), (0,)), ((), ())),
        precision=lax.Precision.HIGHEST,
    )
    scales = (row_scale[:, None], column_scale[None, :], offset)
    result = None
    for tile, (start, size) in zip(fars, far):
        near = (own_sum, own_far, pair_sum, pair_far)
        result = finish(flags, near, mid, tile, scales, result, start, 0)
    return result


def on_a_ring(expression):
    rows, width = expression.shape
    block_count = lax.axis_size("blocks")
    shifted, mean, spread = local_statistics(expression.astype(jnp.float32))
    away, variance = statistics(rows, mean, spread)
    centred = shifted + lax.dynamic_index_in_dim(away, lax.axis_index("cells"), 0)
    every_variance = lax.all_gather(variance, "blocks", axis=0, tiled=True)
    mine = lax.axis_index("blocks")
    partial_value = jnp.zeros((width, width * block_count), jnp.float32)
    current = centred
    for step in range(block_count):
        if step > 0:
            ring = [(i, (i + 1) % block_count) for i in range(block_count)]
            current = lax.ppermute(current, "blocks", ring)
        source = (mine - step) % block_count
        partial_value = lax.dynamic_update_slice_in_dim(
            partial_value, cross_gram(centred, current), source * width, 1
        )
    tile = lax.psum_scatter(partial_value, "cells", scatter_dimension=1, tiled=True)
    column_start = lax.axis_index("cells") * tile.shape[1]
    column_variance = lax.dynamic_slice_in_dim(every_variance, column_start, tile.shape[1])
    row_scale, column_scale = 1.0 / jnp.sqrt(variance), 1.0 / jnp.sqrt(column_variance)
    return power_six(tile * row_scale[:, None] * column_scale[None, :])


def solution(mesh):
    line = mesh.shape["cells"] == 4 and mesh.shape["blocks"] == 4
    return jax.shard_map(
        on_a_line if line else on_a_ring,
        mesh=mesh,
        in_specs=(P(("groups", "cells"), "blocks"),),
        out_specs=P(("groups", "blocks"), "cells"),
        check_vma=False,
    )
```

time: 454 us -> 328 us (0.72)
  waiting for transfers between devices: 329 us -> 118 us
  Pallas kernels: 0 us -> 94.4 us
  matrix products: 62.8 us -> 5.14 us
  starting transfers between devices: 1.35 us -> 42.6 us
  blocking collectives: 24.4 us -> 39 us
  between operations: 13.4 us -> 0.39 us
  other arithmetic: 9.74 us -> 15.9 us
    reduce_scatter x1 -> x0, waiting for transfers between devices: 107 us -> none  [local(): lax.psum_scatter(partial_value, 'cells', scatter_dimension=1, tiled=True)]
    ppermute x3 -> x20, waiting for transfers between devices: 222 us -> 118 us  [the longest x15 77.7 us: between(): lax.ppermute(part, BOTH, [(a * 4 + b, c * 4 + d) for (a, b), (c, d) in pa...]
    pallas_call x0 -> x13, Pallas kernels: none -> 94.4 us  [the longest x4 43.3 us: both_grams(): call(functools.partial(both_kernel, is_split), scalars=1, grid=(width //...]
    dot_general x4 -> x1, matrix products: 62.8 us -> 5.14 us  [on_a_line(): lax.dot_general(away * row_scale[None, :], column[:4] * column_scale[None...]
    ppermute x3 -> x20, starting transfers between devices: 1.35 us -> 42.6 us  [the longest x15 25.7 us: between(): lax.ppermute(part, BOTH, [(a * 4 + b, c * 4 + d) for (a, b), (c, d) in pa...]
    all_to_all x0 -> x4, blocking collectives: none -> 33 us  [over_cores(): lax.all_to_all(parts, 'cells', 0, 0, axis_index_groups=[[0, 1], [2, 3]],...]
    add x0 -> x7, other arithmetic: none -> 15.7 us  [the longest x2 10.7 us: to_core(): return part + between(part, [((i ^ 1, b), (i, b)) for i, b in pairs], name)]
    psum x2 -> x0, blocking collectives: 14.1 us -> none  [the longest x1 8.4 us: local(): row_variance = lax.psum(jnp.sum(centred * centred, axis=0), 'cells')]
  transfers between devices with their start and end apart: 4 -> 20, of which waited for: 4 -> 4; matrix products, arithmetic and copies ran while one was open for 12% -> 7% of each run, Pallas kernels for 0% -> 13%
where the time goes in v1:
time: 328 us; the launch traced here: 321 us
  waiting for transfers between devices  118 us (36%)
  Pallas kernels  94.4 us (29%)
  starting transfers between devices  42.6 us (13%)
  blocking collectives  39 us (12%)
  other arithmetic  15.9 us (5%)
  local copies, waits for them, and re-layouts  5.92 us (2%)
  matrix products  5.14 us (2%)
    ppermute x15, waiting for transfers between devices, between(): lax.ppermute(part, BOTH, [(a * 4 + b, c * 4 + d) for (a, b), (c, d) in pa...  77.7 us
    pallas_call x4, Pallas kernels, both_grams(): call(functools.partial(both_kernel, is_split), scalars=1, grid=(width //...  43.3 us
    ppermute x5, waiting for transfers between devices, along(): return lax.ppermute(part, 'blocks', pairs)  40.2 us
    all_to_all x4, blocking collectives, over_cores(): lax.all_to_all(parts, 'cells', 0, 0, axis_index_groups=[[0, 1], [2, 3]],...  33 us
    ppermute x15, starting transfers between devices, between(): lax.ppermute(part, BOTH, [(a * 4 + b, c * 4 + d) for (a, b), (c, d) in pa...  25.7 us
    ppermute x5, starting transfers between devices, along(): return lax.ppermute(part, 'blocks', pairs)  16.8 us
    pallas_call x3, Pallas kernels, finish(): call(finish_kernel, scalars=1, grid=(width // TILE,), in_specs=in_specs,...  16.7 us
    pallas_call x1, Pallas kernels, own_gram(): call(own_kernel, grid=(width // TILE,), in_specs=[whole], out_specs=[pl.B...  11.3 us
  transfers between devices with their start and end apart: 20, of which 4 were waited for; matrix products, arithmetic and copies ran while one was open for 7% of the time, Pallas kernels for 13%

profile of v1, /device:TPU:5, one launch (start us, length us, event | category | flops | bytes accessed | tf_op | source)
XLA Modules:
  0.0 321.3 jit_solution(12786334774077009875)
XLA Ops:
  1.6 4.2 %shard_map.17 = (f32[1024,1024]{1,0:T(8,128)}, f32[1024,1024]{1,0:T(8,128)}, f32[1,1024]{1,0:T(1,128)S(1)}, f32[1,1024]{1,0:T(1,128)S(1)}) custom-call(bf16[1024,1024]{1,0:T(8,128)(2,1)S(1)} %copy-done.9), custom_call_target="tpu_custom_call" | custom-call | flops 1 | bytes 1 | tf_op jit(solution)/shard_map/pallas_call | solution.py:57
  5.8 11.3 %shard_map.18 = (f32[1024,1024]{1,0:T(8,128)}, bf16[1024,1024]{1,0:T(8,128)(2,1)S(1)}, bf16[1024,1024]{1,0:T(8,128)(2,1)S(1)}) custom-call(f32[1024,1024]{1,0:T(8,128)} %get-tuple-element.15.turned_ref), custom_call_target="tpu_custom_call" | custom-call | flops 1 | bytes 1 | tf_op jit(solution)/shard_map/pallas_call | solution.py:110
  22.7 4.0 %collective-permute-done = f32[1024,1024]{1,0:T(8,128)S(1)} collective-permute-done((f32[1024,1024]{1,0:T(8,128)}, f32[1024,1024]{1,0:T(8,128)S(1)}, u32[]{:S(2)}, u32[]{:S(2)}) %collective-permute-start) | collective-permute-done | bytes 4194336 | tf_op jit(solution)/shard_map/own_core/ppermute | solution.py:291
  26.7 5.1 %add.66.refs_0_ = f32[1024,1024]{1,0:T(8,128)} add(f32[1024,1024]{1,0:T(8,128)} %get-tuple-element.16.refs_0_, f32[1024,1024]{1,0:T(8,128)S(1)} %collective-permute-done) | non-fusion elementwise | flops 1048576 | bytes 12582912 | tf_op jit(solution)/shard_map/add | solution.py:299
  34.5 6.0 %all-gather.1 = f32[4,2,1024]{2,1,0:T(2,128)S(1)} all-gather(f32[1,2,1024]{2,1,0:T(2,128)S(1)} %maximum_bitcast_fusion), channel_id=2, replica_groups=mesh['groups'=2,'cells'=4,'blocks'=4] {'cells'}, dimensions={0}, use_global_device_ids=true | all-gather | bytes 40960 | tf_op jit(solution)/shard_map/all_gather | solution.py:271
  43.4 73.7 %collective-permute-done.4 = f32[8,1024]{1,0:T(8,128)S(1)} collective-permute-done((f32[8,1024]{1,0:T(8,128)S(1)}, f32[8,1024]{1,0:T(8,128)S(1)}, u32[]{:S(2)}, u32[]{:S(2)}) %collective-permute-start.4) | collective-permute-done | bytes 32800 | tf_op jit(solution)/shard_map/moments/ppermute | solution.py:291
  117.2 19.7 %shard_map.19 = (f32[2,1024,1024]{2,1,0:T(8,128)}, bf16[1024,1024]{1,0:T(8,128)(2,1)S(1)}, bf16[1024,1024]{1,0:T(8,128)(2,1)S(1)}) custom-call(s32[1]{0:T(128)} %bitcast.2.core_ref, bf16[1024,1024]{1,0:T(8,128)(2,1)} %copy-done, bf16[1024,1024]{1,0:T(8,128)(2,1)} %copy-done.2, f32[1024,1024]{1,0:T(8,128)} %collective-permute-done.2.refs_0_, ...), custom_call_target="tpu_custom_call" | custom-call | flops 1 | bytes 1 | tf_op jit(solution)/shard_map/pallas_call | solution.py:170
  139.6 10.7 %shard_map.20.refs_0_.refs_4_ = f32[1024,1024]{1,0:T(8,128)} custom-call(bf16[1024,1024]{1,0:T(8,128)(2,1)S(1)} %copy-done.1, bf16[1024,1024]{1,0:T(8,128)(2,1)S(1)} %copy-done.3, bf16[1024,1024]{1,0:T(8,128)(2,1)} %copy-done.5, bf16[1024,1024]{1,0:T(8,128)(2,1)} %copy-done.6, f32[2,1024,1024]{2,1,0:T(8,128)} %get-tuple-element.24.refs_0_), custom_call_target="tpu_custom_call" | custom-call | flops 1 | bytes 1 | tf_op jit(solution)/shard_map/pallas_call | solution.py:130
  151.6 13.7 %all_to_all.20 = f32[2,1024,1024]{2,1,0:T(8,128)S(1)} all-to-all(f32[2,1024,1024]{2,1,0:T(8,128)S(1)} %copy-done.11), channel_id=1, replica_groups={{0,4},{8,12},{1,5},{9,13},{2,6},{10,14},{3,7},{11,15},{16,20},{24,28},{..., dimensions={0} | all-to-all | bytes 16777216 | tf_op jit(solution)/shard_map/all_to_all | solution.py:305
  177.5 5.6 %collective-permute-start.13 = (f32[1024,512]{1,0:T(8,128)}, f32[1024,512]{1,0:T(8,128)}, u32[]{:S(2)}, u32[]{:S(2)}) collective-permute-start(f32[1024,512]{1,0:T(8,128)} %shard_map.23), channel_id=1, source_target_pairs={{0,2},{3,1},{4,6},{7,5},{8,10},{11,9},{12,14},{15,13},{16,18},{19,... | collective-permute-start | bytes 6291464 | tf_op jit(solution)/shard_map/far_block/ppermute | solution.py:295
  183.1 5.6 %add.73.refs_2_ = f32[1024,1024]{1,0:T(8,128)} add(f32[1024,1024]{1,0:T(8,128)S(1)} %copy-done.10, f32[1024,1024]{1,0:T(8,128)} %collective-permute-done.7) | non-fusion elementwise | flops 1048576 | bytes 12582912 | tf_op jit(solution)/shard_map/add | solution.py:299
  195.5 31.9 %collective-permute-done.13.refs_2_ = f32[1024,512]{1,0:T(8,128)} collective-permute-done((f32[1024,512]{1,0:T(8,128)}, f32[1024,512]{1,0:T(8,128)}, u32[]{:S(2)}, u32[]{:S(2)}) %collective-permute-start.13) | collective-permute-done | bytes 2097184 | tf_op jit(solution)/shard_map/far_block/ppermute | solution.py:295
  227.4 10.7 %shard_map.24 = f32[2,1024,512]{2,1,0:T(8,128)} custom-call(s32[1]{0:T(128)} %bitcast.7.core_ref, bf16[1024,1024]{1,0:T(8,128)(2,1)S(1)} %copy-done.1, bf16[1024,1024]{1,0:T(8,128)(2,1)S(1)} %copy-done.4, bf16[1024,1024]{1,0:T(8,128)(2,1)} %copy-done.5, bf16[1024,1024]{1,0:T(8,128)(2,1)} %copy-done.6, f32[1024,512]{1,0:T(8,128)} %collective-permute-done.13.refs_2_, ...), custom_call_target="tpu_custom_call" | custom-call | flops 1 | bytes 1 | tf_op jit(solution)/shard_map/pallas_call | solution.py:170
  238.1 8.6 %all_to_all.21 = f32[2,1024,512]{2,1,0:T(8,128)S(1)} all-to-all(f32[2,1024,512]{2,1,0:T(8,128)} %shard_map.24), channel_id=1, replica_groups={{0,4},{8,12},{1,5},{9,13},{2,6},{10,14},{3,7},{11,15},{16,20},{24,28},{..., dimensions={0} | all-to-all | bytes 8388608 | tf_op jit(solution)/shard_map/all_to_all | solution.py:305
  251.8 7.2 %collective-permute-start.11 = (f32[1024,256]{1,0:T(8,128)S(1)}, f32[1024,256]{1,0:T(8,128)S(1)}, u32[]{:S(2)}, u32[]{:S(2)}) collective-permute-start(f32[1024,256]{1,0:T(8,128)S(1)} %shard_map.21), channel_id=1, source_target_pairs={{0,2},{3,1},{4,6},{7,5},{8,10},{11,9},{12,14},{15,13},{16,18},{19,... | collective-permute-start | bytes 3145736 | tf_op jit(solution)/shard_map/far_block/ppermute | solution.py:295
  260.3 6.3 %shard_map.25 = f32[2,1024,256]{2,1,0:T(8,128)S(1)} custom-call(s32[1]{0:T(128)} %bitcast.7.core_ref, bf16[1024,1024]{1,0:T(8,128)(2,1)S(1)} %copy-done.1, bf16[1024,1024]{1,0:T(8,128)(2,1)} %copy-done.2, bf16[1024,1024]{1,0:T(8,128)(2,1)} %copy-done.5, bf16[1024,1024]{1,0:T(8,128)(2,1)} %copy-done.6, f32[1024,256]{1,0:T(8,128)S(1)} %collective-permute-done.12.refs_2_, ...), custom_call_target="tpu_custom_call" | custom-call | flops 1 | bytes 1 | tf_op jit(solution)/shard_map/pallas_call | solution.py:170
  266.6 5.2 %all_to_all.22 = f32[2,1024,256]{2,1,0:T(8,128)S(1)} all-to-all(f32[2,1024,256]{2,1,0:T(8,128)S(1)} %shard_map.25), channel_id=1, replica_groups={{0,4},{8,12},{1,5},{9,13},{2,6},{10,14},{3,7},{11,15},{16,20},{24,28},{..., dimensions={0} | all-to-all | bytes 4194304 | tf_op jit(solution)/shard_map/all_to_all | solution.py:305
  273.2 8.3 %collective-permute-done.11.refs_2_ = f32[1024,256]{1,0:T(8,128)S(1)} collective-permute-done((f32[1024,256]{1,0:T(8,128)S(1)}, f32[1024,256]{1,0:T(8,128)S(1)}, u32[]{:S(2)}, u32[]{:S(2)}) %collective-permute-start.11) | collective-permute-done | bytes 1048608 | tf_op jit(solution)/shard_map/far_block/ppermute | solution.py:295
  282.8 6.6 %shard_map.26 = f32[2,1024,256]{2,1,0:T(8,128)S(1)} custom-call(s32[1]{0:T(128)} %bitcast.7.core_ref, bf16[1024,1024]{1,0:T(8,128)(2,1)} %copy-done, bf16[1024,1024]{1,0:T(8,128)(2,1)} %copy-done.2, bf16[1024,1024]{1,0:T(8,128)(2,1)} %copy-done.5, bf16[1024,1024]{1,0:T(8,128)(2,1)} %copy-done.6, f32[1024,256]{1,0:T(8,128)S(1)} %collective-permute-done.11.refs_2_, ...), custom_call_target="tpu_custom_call" | custom-call | flops 1 | bytes 1 | tf_op jit(solution)/shard_map/pallas_call | solution.py:170
  289.5 5.5 %all_to_all.23 = f32[2,1024,256]{2,1,0:T(8,128)S(1)} all-to-all(f32[2,1024,256]{2,1,0:T(8,128)S(1)} %shard_map.26), channel_id=1, replica_groups={{0,4},{8,12},{1,5},{9,13},{2,6},{10,14},{3,7},{11,15},{16,20},{24,28},{..., dimensions={0} | all-to-all | bytes 4194304 | tf_op jit(solution)/shard_map/all_to_all | solution.py:305
  299.4 5.1 %convolution_multiply_fusion.refs_12_ = f32[1024,1024]{1,0:T(8,128)} fusion(f32[8,1024]{1,0:T(8,128)S(1)} %add_add_fusion.refs_3_.refs_0_, f32[4,1024]{1,0:T(4,128)S(1)} %get-tuple-element.30, f32[1024]{0:T(1024)S(1)} %bitcast.22, f32[1024]{0:T(1024)S(1)} %get-tuple-element.27), kind=kOutput, calls=%fused_computation.2 | convolution fusion | flops 51388416 | bytes 4235264 | tf_op jit(solution)/shard_map/dot_general | solution.py:352
  304.5 6.4 %shard_map.27.refs_13_ = f32[1024,1024]{1,0:T(8,128)} custom-call(s32[2]{0:T(128)S(1)} %pad_add_fusion.flags, f32[1024,1024]{1,0:T(8,128)} %add.66.refs_0_, f32[1024,1024]{1,0:T(8,128)} %collective-permute-done.1.refs_2_.refs_1_, f32[1024,1024]{1,0:T(8,128)} %add.73.refs_2_, f32[1024,1024]{1,0:T(8,128)} %collective-permute-done.8.refs_4_.refs_3_, ...), custom_call_target="tpu_custom_call" | custom-call | flops 1 | bytes 1 | tf_op jit(solution)/shard_map/pallas_call | solution.py:237
  310.9 5.2 %shard_map.28.refs_13_ = f32[1024,1024]{1,0:T(8,128)} custom-call(s32[2]{0:T(128)S(1)} %pad_add_fusion.flags, f32[1024,1024]{1,0:T(8,128)} %add.66.refs_0_, f32[1024,1024]{1,0:T(8,128)} %collective-permute-done.1.refs_2_.refs_1_, f32[1024,1024]{1,0:T(8,128)} %add.73.refs_2_, ...), custom_call_target="tpu_custom_call", output_to_operand_aliasing={{}: (14, {})} | custom-call | flops 1 | bytes 1 | tf_op jit(solution)/shard_map/pallas_call | solution.py:237
  316.1 5.2 %shard_map.29 = f32[1024,1024]{1,0:T(8,128)} custom-call(s32[2]{0:T(128)S(1)} %pad_add_fusion.flags, f32[1024,1024]{1,0:T(8,128)} %add.66.refs_0_, f32[1024,1024]{1,0:T(8,128)} %collective-permute-done.1.refs_2_.refs_1_, f32[1024,1024]{1,0:T(8,128)} %add.73.refs_2_, ...), custom_call_target="tpu_custom_call", output_to_operand_aliasing={{}: (14, {})} | custom-call | flops 1 | bytes 1 | tf_op jit(solution)/shard_map/pallas_call | solution.py:237
  (77 shorter events, 49.1 us)
Async XLA Ops:
  17.2 9.6 %collective-permute-start = (f32[1024,1024]{1,0:T(8,128)}, f32[1024,1024]{1,0:T(8,128)S(1)}, u32[]{:S(2)}, u32[]{:S(2)}) collective-permute-start(f32[1024,1024]{1,0:T(8,128)} %get-tuple-element.16.refs_0_), channel_id=1, source_target_pairs={{4,0},{1,5},{6,2},{3,7},{12,8},{9,13},{14,10},{11,15},{20,16},{17,... | collective-permute-start | bytes 12582920 | tf_op jit(solution)/shard_map/own_core/ppermute | solution.py:291
  20.0 97.1 %collective-permute-start.2 = (f32[1024,1024]{1,0:T(8,128)}, f32[1024,1024]{1,0:T(8,128)}, u32[]{:S(2)}, u32[]{:S(2)}) collective-permute-start(f32[1024,1024]{1,0:T(8,128)} %get-tuple-element.15.turned_ref), channel_id=1, source_target_pairs={{0,1},{1,0},{2,3},{3,2},{4,5},{5,4},{6,7},{7,6},{8,9},{9,8},{10,11... | collective-permute-start | bytes 12582920 | tf_op jit(solution)/shard_map/pair_block/ppermute | solution.py:295
  20.1 97.0 %collective-permute-start.3 = (f32[1024,1024]{1,0:T(8,128)}, f32[1024,1024]{1,0:T(8,128)}, u32[]{:S(2)}, u32[]{:S(2)}) collective-permute-start(f32[1024,1024]{1,0:T(8,128)} %get-tuple-element.19.from_ref), channel_id=1, source_target_pairs={{1,2},{2,1},{5,6},{6,5},{9,10},{10,9},{13,14},{14,13},{17,18},{18,... | collective-permute-start | bytes 12582920 | tf_op jit(solution)/shard_map/mid_block/ppermute | solution.py:295
  31.8 85.3 %collective-permute-start.1 = (f32[1024,1024]{1,0:T(8,128)}, f32[1024,1024]{1,0:T(8,128)}, u32[]{:S(2)}, u32[]{:S(2)}) collective-permute-start(f32[1024,1024]{1,0:T(8,128)} %add.66.refs_0_), channel_id=1, source_target_pairs={{8,0},{13,5},{2,10},{7,15},{24,16},{29,21},{18,26},{23,31}} | collective-permute-start | bytes 12582920 | tf_op jit(solution)/shard_map/own_lane/ppermute | solution.py:291
  40.7 1.3 collective-permute-start.6
  41.4 2.0 collective-permute-start.5
  42.1 75.0 %collective-permute-start.4 = (f32[8,1024]{1,0:T(8,128)S(1)}, f32[8,1024]{1,0:T(8,128)S(1)}, u32[]{:S(2)}, u32[]{:S(2)}) collective-permute-start(f32[8,1024]{1,0:T(8,128)S(1)} %maximum_maximum_fusion), channel_id=1, source_target_pairs={{0,1},{5,6},{10,11},{15,12},{16,17},{21,22},{26,27},{31,28}} | collective-permute-start | bytes 98312 | tf_op jit(solution)/shard_map/moments/ppermute | solution.py:291
  117.2 22.4 %copy-start.1 = (bf16[1024,1024]{1,0:T(8,128)(2,1)S(1)}, bf16[1024,1024]{1,0:T(8,128)(2,1)}, u32[]{:S(2)}) copy-start(bf16[1024,1024]{1,0:T(8,128)(2,1)} %copy-done) | copy-start | bytes 6291460
  117.2 22.4 %copy-start.3 = (bf16[1024,1024]{1,0:T(8,128)(2,1)S(1)}, bf16[1024,1024]{1,0:T(8,128)(2,1)}, u32[]{:S(2)}) copy-start(bf16[1024,1024]{1,0:T(8,128)(2,1)} %copy-done.2) | copy-start | bytes 6291460
  150.3 32.7 %collective-permute-start.7 = (f32[1024,1024]{1,0:T(8,128)}, f32[1024,1024]{1,0:T(8,128)}, u32[]{:S(2)}, u32[]{:S(2)}) collective-permute-start(f32[1024,1024]{1,0:T(8,128)} %shard_map.20.refs_0_.refs_4_), channel_id=1, source_target_pairs={{0,4},{5,1},{2,6},{7,3},{8,12},{13,9},{10,14},{15,11},{16,20},{21,... | collective-permute-start | bytes 12582920 | tf_op jit(solution)/shard_map/pair_core/ppermute | solution.py:291
  168.2 14.8 %copy-start.10 = (f32[1024,1024]{1,0:T(8,128)S(1)}, f32[1024,1024]{1,0:T(8,128)}, u32[]{:S(2)}) copy-start(f32[1024,1024]{1,0:T(8,128)} %shard_map.20.refs_0_.refs_4_) | copy-start | bytes 12582916
  168.2 90.8 %collective-permute-start.9 = (f32[1024,1024]{1,0:T(8,128)}, f32[1024,1024]{1,0:T(8,128)}, u32[]{:S(2)}, u32[]{:S(2)}) collective-permute-start(f32[1024,1024]{1,0:T(8,128)} %fusion.refs_3_.refs_4_), channel_id=1, source_target_pairs={{1,9},{14,6},{5,8},{10,7},{17,25},{30,22},{21,24},{26,23}} | collective-permute-start | bytes 12582920 | tf_op jit(solution)/shard_map/mid_sum_first/ppermute | solution.py:291
  171.1 89.2 %collective-permute-start.10 = (f32[1024,1024]{1,0:T(8,128)}, f32[1024,1024]{1,0:T(8,128)}, u32[]{:S(2)}, u32[]{:S(2)}) collective-permute-start(f32[1024,1024]{1,0:T(8,128)} %fusion.refs_3_.refs_4_), channel_id=1, source_target_pairs={{13,8},{2,7},{29,24},{18,23}} | collective-permute-start | bytes 12582920 | tf_op jit(solution)/shard_map/mid_sum_second/ppermute | solution.py:291
  177.5 49.9 %collective-permute-start.13 = (f32[1024,512]{1,0:T(8,128)}, f32[1024,512]{1,0:T(8,128)}, u32[]{:S(2)}, u32[]{:S(2)}) collective-permute-start(f32[1024,512]{1,0:T(8,128)} %shard_map.23), channel_id=1, source_target_pairs={{0,2},{3,1},{4,6},{7,5},{8,10},{11,9},{12,14},{15,13},{16,18},{19,... | collective-permute-start | bytes 6291464 | tf_op jit(solution)/shard_map/far_block/ppermute | solution.py:295
  188.6 94.2 %collective-permute-start.8 = (f32[1024,1024]{1,0:T(8,128)}, f32[1024,1024]{1,0:T(8,128)}, u32[]{:S(2)}, u32[]{:S(2)}) collective-permute-start(f32[1024,1024]{1,0:T(8,128)} %add.73.refs_2_), channel_id=1, source_target_pairs={{12,4},{9,1},{6,14},{3,11},{28,20},{25,17},{22,30},{19,27}} | collective-permute-start | bytes 12582920 | tf_op jit(solution)/shard_map/pair_lane/ppermute | solution.py:291
  191.9 35.5 %copy-start.4 = (bf16[1024,1024]{1,0:T(8,128)(2,1)S(1)}, bf16[1024,1024]{1,0:T(8,128)(2,1)}, u32[]{:S(2)}) copy-start(bf16[1024,1024]{1,0:T(8,128)(2,1)} %copy-done.2) | copy-start | bytes 6291460
  194.1 57.7 %collective-permute-start.12 = (f32[1024,256]{1,0:T(8,128)S(1)}, f32[1024,256]{1,0:T(8,128)S(1)}, u32[]{:S(2)}, u32[]{:S(2)}) collective-permute-start(f32[1024,256]{1,0:T(8,128)S(1)} %shard_map.22), channel_id=1, source_target_pairs={{0,2},{3,1},{4,6},{7,5},{8,10},{11,9},{12,14},{15,13},{16,18},{19,... | collective-permute-start | bytes 3145736 | tf_op jit(solution)/shard_map/far_block/ppermute | solution.py:295
  248.4 47.9 %collective-permute-start.18 = (f32[1024,512]{1,0:T(8,128)}, f32[1024,512]{1,0:T(8,128)S(1)}, u32[]{:S(2)}, u32[]{:S(2)}) collective-permute-start(f32[1024,512]{1,0:T(8,128)} %fusion.1.refs_3_.refs_7_), channel_id=1, source_target_pairs={{5,13},{10,2},{1,12},{14,3},{21,29},{26,18},{17,28},{30,19}} | collective-permute-start | bytes 6291464 | tf_op jit(solution)/shard_map/far_sum_first/ppermute | solution.py:291
  251.8 29.7 %collective-permute-start.11 = (f32[1024,256]{1,0:T(8,128)S(1)}, f32[1024,256]{1,0:T(8,128)S(1)}, u32[]{:S(2)}, u32[]{:S(2)}) collective-permute-start(f32[1024,256]{1,0:T(8,128)S(1)} %shard_map.21), channel_id=1, source_target_pairs={{0,2},{3,1},{4,6},{7,5},{8,10},{11,9},{12,14},{15,13},{16,18},{19,... | collective-permute-start | bytes 3145736 | tf_op jit(solution)/shard_map/far_block/ppermute | solution.py:295
  259.0 45.5 %collective-permute-start.19 = (f32[1024,512]{1,0:T(8,128)}, f32[1024,512]{1,0:T(8,128)}, u32[]{:S(2)}, u32[]{:S(2)}) collective-permute-start(f32[1024,512]{1,0:T(8,128)} %fusion.1.refs_3_.refs_7_), channel_id=1, source_target_pairs={{9,12},{6,3},{25,28},{22,19}} | collective-permute-start | bytes 6291464 | tf_op jit(solution)/shard_map/far_sum_second/ppermute | solution.py:291
  271.9 39.0 %collective-permute-start.16 = (f32[1024,256]{1,0:T(8,128)S(1)}, f32[1024,256]{1,0:T(8,128)}, u32[]{:S(2)}, u32[]{:S(2)}) collective-permute-start(f32[1024,256]{1,0:T(8,128)S(1)} %fusion.3.refs_3_.refs_7_), channel_id=1, source_target_pairs={{5,13},{10,2},{1,12},{14,3},{21,29},{26,18},{17,28},{30,19}} | collective-permute-start | bytes 3145736 | tf_op jit(solution)/shard_map/far_sum_first/ppermute | solution.py:291
  281.5 29.4 %collective-permute-start.17 = (f32[1024,256]{1,0:T(8,128)S(1)}, f32[1024,256]{1,0:T(8,128)}, u32[]{:S(2)}, u32[]{:S(2)}) collective-permute-start(f32[1024,256]{1,0:T(8,128)S(1)} %fusion.3.refs_3_.refs_7_), channel_id=1, source_target_pairs={{9,12},{6,3},{25,28},{22,19}} | collective-permute-start | bytes 3145736 | tf_op jit(solution)/shard_map/far_sum_second/ppermute | solution.py:291
  295.1 21.0 %collective-permute-start.14 = (f32[1024,256]{1,0:T(8,128)S(1)}, f32[1024,256]{1,0:T(8,128)}, u32[]{:S(2)}, u32[]{:S(2)}) collective-permute-start(f32[1024,256]{1,0:T(8,128)S(1)} %fusion.2.refs_7_), channel_id=1, source_target_pairs={{5,13},{10,2},{1,12},{14,3},{21,29},{26,18},{17,28},{30,19}} | collective-permute-start | bytes 3145736 | tf_op jit(solution)/shard_map/far_sum_first/ppermute | solution.py:291
  297.7 18.4 %collective-permute-start.15 = (f32[1024,256]{1,0:T(8,128)S(1)}, f32[1024,256]{1,0:T(8,128)}, u32[]{:S(2)}, u32[]{:S(2)}) collective-permute-start(f32[1024,256]{1,0:T(8,128)S(1)} %fusion.2.refs_7_), channel_id=1, source_target_pairs={{9,12},{6,3},{25,28},{22,19}} | collective-permute-start | bytes 3145736 | tf_op jit(solution)/shard_map/far_sum_second/ppermute | solution.py:291
  (8 other events, 52.2 us)

commit v2 on v0

v2 whole, which is shorter than its diff:
```python
import functools

import jax
import jax.numpy as jnp
from jax import lax
from jax.experimental import pallas as pl
from jax.experimental.pallas import tpu as pltpu
from jax.sharding import PartitionSpec as P

BOTH = ("cells", "blocks")
TILE = 256
FAR_WIDTHS = (1, 1)
PAD = 16
f32, bf16 = jnp.float32, jnp.bfloat16
ANYWHERE = pl.BlockSpec(memory_space=pl.ANY)


def call(kernel, *, grid, in_specs, out_specs, out_shape, scratch=(), scalars=0, aliases=None, flops=1):
    return pl.pallas_call(
        kernel,
        grid_spec=pltpu.PrefetchScalarGridSpec(
            num_scalar_prefetch=scalars,
            grid=grid,
            in_specs=in_specs,
            out_specs=out_specs,
            scratch_shapes=scratch,
        ),
        out_shape=out_shape,
        input_output_aliases=aliases or {},
        cost_estimate=pl.CostEstimate(flops=flops, bytes_accessed=1, transcendentals=0),
        compiler_params=pltpu.CompilerParams(vmem_limit_bytes=48 << 20),
    )


def shape(*dims):
    return jax.ShapeDtypeStruct(dims, f32)


def split(value):
    high = value.astype(bf16)
    return high, (value - high.astype(f32)).astype(bf16)


def centre_kernel(x_ref, centred_ref, turned_ref, mean_ref, spread_ref):
    value = x_ref[...].astype(f32)
    mean = jnp.sum(value, axis=0, keepdims=True) / value.shape[0]
    value = value - mean
    centred_ref[...] = value
    turned_ref[...] = value.T
    mean_ref[...] = mean
    spread_ref[...] = jnp.sum(value * value, axis=0, keepdims=True)


def centre(expression):
    rows, width = expression.shape
    column = pl.BlockSpec((rows, TILE), lambda g: (0, g))
    line = pl.BlockSpec((1, TILE), lambda g: (0, g))
    return call(
        centre_kernel,
        grid=(width // TILE,),
        in_specs=[column],
        out_specs=[column, pl.BlockSpec((TILE, rows), lambda g: (g, 0)), line, line],
        out_shape=[shape(rows, width), shape(width, rows), shape(1, width), shape(1, width)],
    )(expression)


def copy_kernel(from_ref, *refs):
    refs[-1][...] = from_ref[...]


def columns(source, start, size, *earlier):
    rows = source.shape[0]
    tile = (rows + PAD) // 2
    return call(
        copy_kernel,
        grid=(2,),
        in_specs=[pl.BlockSpec((tile, size), lambda i: (i, start // size))]
        + [ANYWHERE] * len(earlier),
        out_specs=pl.BlockSpec((tile, size), lambda i: (i, 0)),
        out_shape=shape(rows + PAD, size),
    )(source, *earlier)


def gram_kernel(roles, turned, role_ref, *refs):
    lefts, rights = refs[: 2 * roles], refs[2 * roles : 2 * roles + 2]
    out_ref, left_high, left_low, right_high, right_low = refs[-5:]
    cells = lefts[0].shape[1]

    @pl.when(pl.program_id(0) == 0)
    def _():
        for core, ref in enumerate(rights):
            span = slice(core * cells, (core + 1) * cells)
            at = (slice(None), span) if turned else span
            right_high[at], right_low[at] = split(ref[...])

    for role in range(roles):

        @pl.when(role_ref[0] == role if roles > 1 else True)
        def _():
            for core in range(2):
                at = (slice(None), slice(core * cells, (core + 1) * cells))
                left_high[at], left_low[at] = split(lefts[2 * role + core][...])

    contract = (((1,), (1 if turned else 0,)), ((), ()))

    def dot(left, right):
        return lax.dot_general(left, right, contract, preferred_element_type=f32)

    width = out_ref.shape[1]
    for start in range(0, width, 512):
        span = slice(start, min(start + 512, width))
        at = span if turned else (slice(None), span)
        high, low = right_high[at], right_low[at]
        out_ref[:, span] = dot(left_high[...], high) + (
            dot(left_high[...], low) + dot(left_low[...], high)
        )


def gram(role, lefts, rights, turned, earlier, columns=None):
    width, cells = lefts[0].shape
    roles = len(lefts) // 2
    start, size = (0, width) if turned else columns or (0, rights[0].shape[1])

    def left_spec(of_role):
        def index(i, role_ref):
            return (jnp.where(role_ref[0] == of_role, i, 0) if roles > 1 else i), 0

        return pl.BlockSpec((TILE, cells), index)

    right_block = (width, cells) if turned else (cells, size)
    right_shape = (width, 2 * cells) if turned else (2 * cells, size)
    return call(
        functools.partial(gram_kernel, roles, turned),
        scalars=1,
        grid=(width // TILE,),
        in_specs=[left_spec(n // 2) for n in range(len(lefts))]
        + [pl.BlockSpec(right_block, lambda i, role_ref: (0, start // size))] * 2
        + [ANYWHERE] * len(earlier),
        out_specs=pl.BlockSpec((TILE, size), lambda i, role_ref: (i, 0)),
        out_shape=shape(width, size),
        scratch=[pltpu.VMEM((TILE, 2 * cells), bf16)] * 2 + [pltpu.VMEM(right_shape, bf16)] * 2,
    )(role, *lefts, *rights, *earlier)


def together(work, *given):
    like = jax.eval_shape(work, *given)
    zeros = lambda *_: jax.tree.map(lambda leaf: jnp.zeros(leaf.shape, leaf.dtype), like)
    return lax.cond(lax.axis_index("cells") >= 0, work, zeros, *given)


def power_six(ratio):
    half = (1.0 + ratio) * 0.5
    square = half * half
    return square * square * square


def add_kernel(*refs):
    refs[-1][...] = refs[0][...] + refs[1][...]


def add(left, right, *earlier):
    block = pl.BlockSpec((TILE, left.shape[1]), lambda i: (i, 0))
    return call(
        add_kernel,
        grid=(left.shape[0] // TILE,),
        in_specs=[block] * 2 + [ANYWHERE] * len(earlier),
        out_specs=block,
        out_shape=shape(*left.shape),
    )(left, right, *earlier)


def base_kernel(kinds, flags, *refs):
    sums, (rs, cs, offset), out_ref = refs[: len(kinds)], refs[len(kinds) : len(kinds) + 3], refs[-1]
    for kind in sorted(set(kind for used, _ in kinds for kind in used)):

        @pl.when(flags[0] == kind)
        def _():
            tiles = {}
            for ref, (used, start) in zip(sums, kinds):
                if kind in used:
                    tiles.setdefault(start, []).append(ref)
            for start, (left, *rights) in tiles.items():
                at = (slice(None), slice(start, start + left.shape[1]))
                right = rights[0][...]
                if len(rights) > 1:
                    right = jnp.where(2 * pl.program_id(0) < pl.num_programs(0), right, rights[1][...])
                ratio = (left[...] + right) * rs[...] * cs[at] + offset[at]
                out_ref[at] = power_six(ratio)


def base(flags, sums, scales, *earlier):
    width = scales[2].shape[0]
    arrays, kinds = [array for array, _, _ in sums], [(used, start) for _, used, start in sums]

    def spec(array, used):
        steps = array.shape[0] // TILE

        def index(i, flags):
            mine = functools.reduce(jnp.logical_or, [flags[0] == kind for kind in used])
            return jnp.where(mine, i % steps, 0), 0

        return pl.BlockSpec((TILE, array.shape[1]), index)

    here = pl.BlockSpec((TILE, width), lambda i, flags: (i, 0))
    return call(
        functools.partial(base_kernel, kinds),
        scalars=1,
        grid=(width // TILE,),
        in_specs=[spec(array, used) for array, used, _ in sums]
        + [
            pl.BlockSpec((TILE, 1), lambda i, flags: (i, 0)),
            pl.BlockSpec((1, width), lambda i, flags: (0, 0)),
            here,
        ]
        + [ANYWHERE] * len(earlier),
        out_specs=here,
        out_shape=shape(width, width),
    )(flags, *arrays, *scales, *earlier)


def finish_kernel(flags, merged, first, second, rs, cs, offset, before, out_ref):
    @pl.when(flags[1] == 0)
    def _():
        out_ref[...] = before[...]

    for outer, left in enumerate((merged, second)):

        @pl.when(flags[1] == 1 + outer)
        def _():
            tile = left[...] + first[...]
            out_ref[...] = power_six(tile * rs[...] * cs[...] + offset[...])


def finish(flags, far, scales, before, start):
    (row_scale, column_scale, offset), (width, size) = scales, far[0].shape
    column = start // size
    whole = pl.BlockSpec((TILE, size), lambda i, flags: (i, 0))
    here = pl.BlockSpec((TILE, size), lambda i, flags: (i, column))
    operands = [flags, *far, row_scale, column_scale, offset, before]
    return call(
        finish_kernel,
        scalars=1,
        grid=(width // TILE,),
        in_specs=[whole] * 3
        + [
            pl.BlockSpec((TILE, 1), lambda i, flags: (i, 0)),
            pl.BlockSpec((1, size), lambda i, flags: (0, column)),
            here,
            here,
        ],
        out_specs=here,
        out_shape=shape(width, width),
        aliases={len(operands) - 1: 0},
    )(*operands)


def cross_gram(left, right):
    return lax.dot_general(
        left,
        right,
        (((0,), (0,)), ((), ())),
        preferred_element_type=f32,
        precision=lax.Precision.HIGH,
    )


def pieces(width, shares):
    unit = width // sum(shares)
    starts = [unit * sum(shares[:i]) for i in range(len(shares))]
    return [(start, unit * share) for start, share in zip(starts, shares)]


def local_statistics(values):
    mean = jnp.sum(values, axis=0) / values.shape[0]
    shifted = values - mean[None, :]
    return shifted, mean, jnp.sum(shifted * shifted, axis=0)


def statistics(rows, mean, spread):
    shards = lax.all_gather(jnp.stack([mean, spread]), "cells")
    away = shards[:, 0] - jnp.mean(shards[:, 0], axis=0)[None, :]
    variance = jnp.sum(shards[:, 1], axis=0) + rows * jnp.sum(away * away, axis=0)
    return away, variance


def on_a_line(expression):
    rows, width = expression.shape
    z = lax.axis_index("blocks")
    k = lax.axis_index("cells")
    mid_of, far_of = (2, 2, 1, 1), (3, 3, 0, 0)
    own_owner, pair_owner = (0, 1, 2, 3), (1, 0, 3, 2)
    far_id = jnp.where(z < 2, 3, 0)
    outer = ((z == 0) | (z == 3)).astype(jnp.int32)
    kind = jnp.where(k == far_id, 4, 2) + outer
    kind = jnp.where(k == z, 0, jnp.where(k == (z ^ 1), 1, kind))
    flags = jnp.stack([kind, jnp.where(k == far_id, 1 + outer, 0)]).astype(jnp.int32)
    far_role = (k % 2 != far_id % 2).astype(jnp.int32)[None]
    mid_role = 1 - far_role

    def between(part, pairs, name):
        with jax.named_scope(name):
            return lax.ppermute(part, BOTH, [(a * 4 + b, c * 4 + d) for (a, b), (c, d) in pairs])

    def along(part, pairs, name):
        with jax.named_scope(name):
            return lax.ppermute(part, "blocks", pairs)

    def other(part, name):
        return between(part, [((i, b), (i ^ 1, b)) for i in range(4) for b in range(4)], name)

    def to_lane(part, owner, name):
        return between(part, [((owner[b] ^ 2, b), (owner[b], b)) for b in range(4)], name)

    def in_halves(part, owner, name):
        half = width // 2
        return [to_lane(part[:half], owner, name), to_lane(part[half:], owner, name)]

    def onward(part, owner, name):
        pairs = [((owner[b] ^ 2, b), (owner[b], b)) for b in (1, 2)]
        pairs += [((owner[b] ^ 3, b), (owner[b], b ^ 1)) for b in (1, 2)]
        pairs += [((owner[b] ^ 1, b), (owner[b] ^ 1, b ^ 1)) for b in (1, 2)]
        return between(part, pairs, name)

    def folded(part, owner, name):
        return between(part, [((owner[b] ^ 1, b), (owner[b], b)) for b in (0, 3)], name)

    centred, turned, mean, spread = centre(expression)
    mid_got = along(centred, [(1, 2), (2, 1)], "mid_block")
    pair_got = along(turned, [(0, 1), (1, 0), (2, 3), (3, 2)], "pair_block")
    far = pieces(width, FAR_WIDTHS)
    away, variance = statistics(rows, mean[0], spread[0])
    mine = jnp.concatenate([away, variance[None, :], jnp.zeros((11, width), f32)])

    def own_work(turned, mine):
        own = turned, other(turned, "own_other")
        return gram(mid_role, own, own, True, (mine,)), own[1]

    def mid_work(own, pair_got, mid_got, earlier):
        pair = pair_got, other(pair_got, "pair_other")
        right = mid_got, other(mid_got, "mid_other")
        return gram(mid_role, own + pair, right, False, earlier), pair[1]

    def far_work(own, pair, got, earlier):
        right = got, other(got, "far_other")
        return gram(far_role, own + pair, right, False, earlier)

    own_sum, own_other = together(own_work, turned, mine)
    own = turned, own_other
    pairs = [((a, b), (b, a)) for a in range(4) for b in range(4) if a != b]
    column = between(mine, pairs, "moments")
    far_got = []
    for start, size in far:
        part = columns(centred, start, size, pair_got, mid_got, column)
        far_got.append(along(part, [(0, 2), (3, 1)], "far_block"))
    own_far = to_lane(own_sum, own_owner, "own_lane")
    mid_sum, pair_other = together(mid_work, own, pair_got, mid_got, (own_sum,))
    pair = pair_got, pair_other
    mid_far = onward(mid_sum, mid_of, "mid_sum")
    pair_sum = gram(mid_role, own, pair, True, (mid_sum,))
    pair_far = in_halves(pair_sum, pair_owner, "pair_lane")
    waits = [(own_far,), ()]
    far_sums, last = [], pair_sum
    for part, wait in enumerate(waits):
        last = together(far_work, own, pair, far_got[part], (last, *wait))
        sent = jnp.pad(last, ((0, PAD), (0, 0))) if part == 0 else last
        far_sums.append((last, onward(sent, far_of, "far_sum")))

    column = jnp.where(k == z, mine, column)
    row_scale = 1.0 / jnp.sqrt(variance)
    column_scale = 1.0 / jnp.sqrt(column[4])
    offset = rows * lax.dot_general(
        away * row_scale[None, :],
        column[:4] * column_scale[None, :],
        (((0,), (0,)), ((), ())),
        precision=lax.Precision.HIGHEST,
    )
    scales = (row_scale[:, None], column_scale[None, :], offset)

    def base_work(near, mid, fars, scales):
        sums = [(array, (n // 2 if n < 4 else 1,), 0) for n, array in enumerate(near)]
        sums += [(mid[0], (2,), 0), (mid[1], (2, 3), 0), (folded(mid[1], mid_of, "mid_fold"), (3,), 0)]
        for (total, got), (start, _) in zip(fars, far):
            fold = folded(got, far_of, "far_fold")
            sums += [(total, (4,), start), (got, (4, 5), start), (fold, (5,), start)]
        return base(flags, sums, scales)

    def last_base_work(tile, scales, result):
        tile = (*tile, folded(tile[1], far_of, "far_fold"))
        return finish(flags, tile, scales, result, far[-1][0])

    near = own_sum, own_far, pair_sum, *pair_far
    result = together(base_work, near, (mid_sum, mid_far), far_sums[:-1], scales)
    return together(last_base_work, far_sums[-1], scales, result)


def on_a_ring(expression):
    rows, width = expression.shape
    block_count = lax.axis_size("blocks")
    shifted, mean, spread = local_statistics(expression.astype(jnp.float32))
    away, variance = statistics(rows, mean, spread)
    centred = shifted + lax.dynamic_index_in_dim(away, lax.axis_index("cells"), 0)
    every_variance = lax.all_gather(variance, "blocks", axis=0, tiled=True)
    mine = lax.axis_index("blocks")
    partial_value = jnp.zeros((width, width * block_count), jnp.float32)
    current = centred
    for step in range(block_count):
        if step > 0:
            ring = [(i, (i + 1) % block_count) for i in range(block_count)]
            current = lax.ppermute(current, "blocks", ring)
        source = (mine - step) % block_count
        partial_value = lax.dynamic_update_slice_in_dim(
            partial_value, cross_gram(centred, current), source * width, 1
        )
    tile = lax.psum_scatter(partial_value, "cells", scatter_dimension=1, tiled=True)
    column_start = lax.axis_index("cells") * tile.shape[1]
    column_variance = lax.dynamic_slice_in_dim(every_variance, column_start, tile.shape[1])
    row_scale, column_scale = 1.0 / jnp.sqrt(variance), 1.0 / jnp.sqrt(column_variance)
    return power_six(tile * row_scale[:, None] * column_scale[None, :])


def solution(mesh):
    line = mesh.shape["cells"] == 4 and mesh.shape["blocks"] == 4
    return jax.shard_map(
        on_a_line if line else on_a_ring,
        mesh=mesh,
        in_specs=(P(("groups", "cells"), "blocks"),),
        out_specs=P(("groups", "blocks"), "cells"),
        check_vma=False,
    )
```

time: 454 us -> 280 us (0.62)
  waiting for transfers between devices: 329 us -> 107 us
  Pallas kernels: 0 us -> 112 us
  matrix products: 62.8 us -> 5.13 us
  starting transfers between devices: 1.35 us -> 41.4 us
  blocking collectives: 24.4 us -> 5.96 us
  between operations: 13.4 us -> 0.14 us
  other arithmetic: 9.74 us -> 0.31 us
    ppermute x3 -> x19, waiting for transfers between devices: 222 us -> 107 us  [the longest x15 107 us: between(): lax.ppermute(part, BOTH, [(a * 4 + b, c * 4 + d) for (a, b), (c, d) in pa...]
    pallas_call x0 -> x10, Pallas kernels: none -> 112 us  [the longest x5 88.2 us: gram(): call(functools.partial(gram_kernel, roles, turned), scalars=1, grid=(widt...]
    reduce_scatter x1 -> x0, waiting for transfers between devices: 107 us -> none  [local(): lax.psum_scatter(partial_value, 'cells', scatter_dimension=1, tiled=True)]
    dot_general x4 -> x1, matrix products: 62.8 us -> 5.13 us  [on_a_line(): lax.dot_general(away * row_scale[None, :], column[:4] * column_scale[None...]
    ppermute x3 -> x19, starting transfers between devices: 1.35 us -> 41.4 us  [the longest x15 29.3 us: between(): lax.ppermute(part, BOTH, [(a * 4 + b, c * 4 + d) for (a, b), (c, d) in pa...]
    psum x2 -> x0, blocking collectives: 14.1 us -> none  [the longest x1 8.4 us: local(): row_variance = lax.psum(jnp.sum(centred * centred, axis=0), 'cells')]
    broadcast_in_dim x1, local copies, waits for them, and re-layouts: 7.82 us -> 0.01 us  [on_a_line(): jnp.zeros((11, width), f32)]
    mul x1 -> x0, other arithmetic: 5.43 us -> none  [local(): return ((1.0 + ratio) / 2.0) ** 6]
  transfers between devices with their start and end apart: 4 -> 19, of which waited for: 4 -> 8; matrix products, arithmetic and copies ran while one was open for 12% -> 4% of each run, Pallas kernels for 0% -> 36%
where the time goes in v2:
time: 280 us; the launch traced here: 279 us
  Pallas kernels  112 us (40%)
  waiting for transfers between devices  107 us (38%)
  starting transfers between devices  41.4 us (15%)
  local copies, waits for them, and re-layouts  7.65 us (3%)
  blocking collectives  5.96 us (2%)
  matrix products  5.13 us (2%)
    ppermute x15, waiting for transfers between devices, between(): lax.ppermute(part, BOTH, [(a * 4 + b, c * 4 + d) for (a, b), (c, d) in pa...  107 us
    pallas_call x5, Pallas kernels, gram(): call(functools.partial(gram_kernel, roles, turned), scalars=1, grid=(widt...  88.2 us
    ppermute x15, starting transfers between devices, between(): lax.ppermute(part, BOTH, [(a * 4 + b, c * 4 + d) for (a, b), (c, d) in pa...  29.3 us
    ppermute x4, starting transfers between devices, along(): return lax.ppermute(part, 'blocks', pairs)  12.1 us
    pallas_call x1, Pallas kernels, base(): call(functools.partial(base_kernel, kinds), scalars=1, grid=(width // TIL...  8.73 us
    all_gather x1, blocking collectives, statistics(): shards = lax.all_gather(jnp.stack([mean, spread]), 'cells')  5.96 us
    pallas_call x1, Pallas kernels, finish(): call(finish_kernel, scalars=1, grid=(width // TILE,), in_specs=[whole] *...  5.95 us
  transfers between devices with their start and end apart: 19, of which 8 were waited for; matrix products, arithmetic and copies ran while one was open for 4% of the time, Pallas kernels for 36%

profile of v2, /device:TPU:5, one launch (start us, length us, event | category | flops | bytes accessed | tf_op | source)
XLA Modules:
  0.0 279.2 jit_solution(5957041921721098374)
XLA Ops:
  10.0 6.0 %all-gather.1 = f32[4,2,1024]{2,1,0:T(2,128)S(1)} all-gather(f32[1,2,1024]{2,1,0:T(2,128)S(1)} %maximum_bitcast_fusion), channel_id=2, replica_groups=mesh['groups'=2,'cells'=4,'blocks'=4] {'cells'}, dimensions={0}, use_global_device_ids=true | all-gather | bytes 40960 | tf_op jit(solution)/shard_map/all_gather | solution.py:280
  16.1 28.4 %conditional.6 = (f32[1024,1024]{1,0:T(8,128)}, f32[1024,1024]{1,0:T(8,128)}) conditional(s32[]{:T(128)} %convert_element_type.5, () %tuple.47, (f32[1024,1024]{1,0:T(8,128)}, s32[1]{0:T(128)}, f32[16,1024]{1,0:T(8,128)S(1)}) %tuple.48), branch_computations={%region_3.4_spmd, %region_4.5_spmd} | conditional | flops 1 | bytes 16777272 | solution.py:148
  16.3 7.3 %collective-permute-done.refs_1_.refs_3_ = f32[1024,1024]{1,0:T(8,128)} collective-permute-done((f32[1024,1024]{1,0:T(8,128)}, f32[1024,1024]{1,0:T(8,128)}, u32[]{:S(2)}, u32[]{:S(2)}) %collective-permute-start) | collective-permute-done | bytes 4194336 | tf_op jit(solution)/shard_map/cond/branch_1_fun/own_other/ppermute | solution.py:302
  23.6 20.9 %branch_1_fun.6 = f32[1024,1024]{1,0:T(8,128)} custom-call(s32[1]{0:T(128)} %get-tuple-element.95.role_ref, f32[1024,1024]{1,0:T(8,128)} %get-tuple-element.104.refs_0_.refs_2_, f32[1024,1024]{1,0:T(8,128)} %collective-permute-done.refs_1_.refs_3_, f32[1024,1024]{1,0:T(8,128)} %get-tuple-element.104.refs_0_.refs_2_, ...), custom_call_target="tpu_custom_call" | custom-call | flops 1 | bytes 1 | tf_op jit(solution)/shard_map/cond/branch_1_fun/pallas_call | solution.py:132
  51.2 50.7 %collective-permute-done.10.refs_2_ = f32[16,1024]{1,0:T(8,128)S(1)} collective-permute-done((f32[16,1024]{1,0:T(8,128)S(1)}, f32[16,1024]{1,0:T(8,128)S(1)}, u32[]{:S(2)}, u32[]{:S(2)}) %collective-permute-start.10) | collective-permute-done | bytes 65568 | tf_op jit(solution)/shard_map/moments/ppermute | solution.py:302
  104.6 5.6 %collective-permute-start.12 = (f32[1040,512]{1,0:T(8,128)}, f32[1040,512]{1,0:T(8,128)}, u32[]{:S(2)}, u32[]{:S(2)}) collective-permute-start(f32[1040,512]{1,0:T(8,128)} %shard_map.21), channel_id=1, source_target_pairs={{0,2},{3,1},{4,6},{7,5},{8,10},{11,9},{12,14},{15,13},{16,18},{19,... | collective-permute-start | bytes 6389768 | tf_op jit(solution)/shard_map/far_block/ppermute | solution.py:306
  114.5 36.8 %conditional.7 = (f32[1024,1024]{1,0:T(8,128)}, f32[1024,1024]{1,0:T(8,128)}) conditional(s32[]{:T(128)} %convert_element_type.5, () %tuple.49, (f32[1024,1024]{1,0:T(8,128)}, f32[1024,1024]{1,0:T(8,128)}, s32[1]{0:T(128)}, f32[1024,1024]{1,0:T(8,128)}, f32[1024,1024]{1,0:T(8,128)}, /*index=5*/f32[1024,1024]{1,0:T(8,128)}) %tuple.50), branch_computations={%region_5.6_spmd, %region_6.7_spmd} | conditional | flops 1 | bytes 33554528 | solution.py:148
  117.3 13.1 %collective-permute-done.1.refs_3_ = f32[1024,1024]{1,0:T(8,128)} collective-permute-done((f32[1024,1024]{1,0:T(8,128)}, f32[1024,1024]{1,0:T(8,128)}, u32[]{:S(2)}, u32[]{:S(2)}) %collective-permute-start.1) | collective-permute-done | bytes 4194336 | tf_op jit(solution)/shard_map/cond/branch_1_fun/pair_other/ppermute | solution.py:302
  130.4 20.8 %branch_1_fun.7 = f32[1024,1024]{1,0:T(8,128)} custom-call(s32[1]{0:T(128)} %get-tuple-element.108.role_ref, f32[1024,1024]{1,0:T(8,128)} %get-tuple-element.109.refs_0_, f32[1024,1024]{1,0:T(8,128)} %get-tuple-element.110.refs_1_, f32[1024,1024]{1,0:T(8,128)} %get-tuple-element.111.refs_2_, f32[1024,1024]{1,0:T(8,128)} %collective-permute-done.1.refs_3_, ...), custom_call_target="tpu_custom_call" | custom-call | flops 1 | bytes 1 | tf_op jit(solution)/shard_map/cond/branch_1_fun/pallas_call | solution.py:132
  152.7 20.4 %shard_map.22 = f32[1024,1024]{1,0:T(8,128)} custom-call(s32[1]{0:T(128)} %sub.13.role_ref, f32[1024,1024]{1,0:T(8,128)} %get-tuple-element.158.refs_0_, f32[1024,1024]{1,0:T(8,128)} %get-tuple-element.161.refs_1_, f32[1024,1024]{1,0:T(8,128)} %collective-permute-done.8.refs_0_.refs_2_, f32[1024,1024]{1,0:T(8,128)} %get-tuple-element.163.refs_3_, ...), custom_call_target="tpu_custom_call" | custom-call | flops 1 | bytes 1 | tf_op jit(solution)/shard_map/pallas_call | solution.py:132
  173.1 17.9 %conditional.8 = (f32[1024,512]{1,0:T(8,128)}) conditional(s32[]{:T(128)} %convert_element_type.5, () %tuple.51, (f32[1040,512]{1,0:T(8,128)}, s32[1]{0:T(128)}, f32[1024,1024]{1,0:T(8,128)}, f32[1024,1024]{1,0:T(8,128)}, f32[1024,1024]{1,0:T(8,128)}, /*index=5*/f32[1024,1024]{1,0:T(8,128)}, f32[1024,1024]{1,0:T(8,128)}, f32[1024,1024]{1,0:T(8,128)}) %tuple.52), branch_computations={%region_7.8_spmd, %region_8.9_spmd} | conditional | flops 1 | bytes 8519729 | solution.py:148
  177.9 13.1 %branch_1_fun.8 = f32[1024,512]{1,0:T(8,128)} custom-call(s32[1]{0:T(128)} %get-tuple-element.114.role_ref, f32[1024,1024]{1,0:T(8,128)} %get-tuple-element.115.refs_0_, f32[1024,1024]{1,0:T(8,128)} %get-tuple-element.116.refs_1_, f32[1024,1024]{1,0:T(8,128)} %get-tuple-element.117.refs_2_, f32[1024,1024]{1,0:T(8,128)} %get-tuple-element.118.refs_3_, ...), custom_call_target="tpu_custom_call" | custom-call | flops 1 | bytes 1 | tf_op jit(solution)/shard_map/cond/branch_1_fun/pallas_call | solution.py:132
  197.8 6.1 %collective-permute-start.17 = (f32[512,1024]{1,0:T(8,128)}, f32[512,1024]{1,0:T(8,128)}, u32[]{:S(2)}, u32[]{:S(2)}) collective-permute-start(f32[512,1024]{1,0:T(8,128)} %get-tuple-element.213), channel_id=1, source_target_pairs={{12,4},{9,1},{6,14},{3,11},{28,20},{25,17},{22,30},{19,27}} | collective-permute-start | bytes 6291464 | tf_op jit(solution)/shard_map/pair_lane/ppermute | solution.py:302
  206.5 17.5 %conditional.9 = (f32[1024,512]{1,0:T(8,128)}) conditional(s32[]{:T(128)} %convert_element_type.5, () %tuple.46, (f32[1040,512]{1,0:T(8,128)}, s32[1]{0:T(128)}, f32[1024,1024]{1,0:T(8,128)}, f32[1024,1024]{1,0:T(8,128)}, f32[1024,1024]{1,0:T(8,128)}, /*index=5*/f32[1024,1024]{1,0:T(8,128)}, f32[1024,512]{1,0:T(8,128)}) %tuple.53), branch_computations={%region_9.10_spmd, %region_10.11_spmd} | conditional | flops 1 | bytes 8519729 | solution.py:148
  206.5 4.4 %collective-permute-done.4.refs_5_ = f32[1040,512]{1,0:T(8,128)S(1)} collective-permute-done((f32[1040,512]{1,0:T(8,128)}, f32[1040,512]{1,0:T(8,128)S(1)}, u32[]{:S(2)}, u32[]{:S(2)}) %collective-permute-start.4) | collective-permute-done | bytes 2129952 | tf_op jit(solution)/shard_map/cond/branch_1_fun/far_other/ppermute | solution.py:302
  210.9 13.1 %branch_1_fun.9 = f32[1024,512]{1,0:T(8,128)} custom-call(s32[1]{0:T(128)} %get-tuple-element.122.role_ref, f32[1024,1024]{1,0:T(8,128)} %get-tuple-element.123.refs_0_, f32[1024,1024]{1,0:T(8,128)} %get-tuple-element.124.refs_1_, f32[1024,1024]{1,0:T(8,128)} %get-tuple-element.125.refs_2_, f32[1024,1024]{1,0:T(8,128)} %get-tuple-element.126.refs_3_, ...), custom_call_target="tpu_custom_call" | custom-call | flops 1 | bytes 1 | tf_op jit(solution)/shard_map/cond/branch_1_fun/pallas_call | solution.py:132
  225.5 5.1 %convolution_multiply_fusion = f32[1024,1024]{1,0:T(8,128)} fusion(f32[16,1024]{1,0:T(8,128)S(1)} %broadcast_select_fusion, f32[4,1024]{1,0:T(4,128)S(1)} %get-tuple-element.211, f32[1024]{0:T(1024)S(1)} %bitcast.13, f32[1024]{0:T(1024)S(1)} %get-tuple-element.208), kind=kOutput, calls=%fused_computation | convolution fusion | flops 51388416 | bytes 4235264 | tf_op jit(solution)/shard_map/dot_general | solution.py:371
  230.6 17.6 %collective-permute-done.18 = f32[512,1024]{1,0:T(8,128)} collective-permute-done((f32[512,1024]{1,0:T(8,128)}, f32[512,1024]{1,0:T(8,128)}, u32[]{:S(2)}, u32[]{:S(2)}) %collective-permute-start.18) | collective-permute-done | bytes 2097184 | tf_op jit(solution)/shard_map/pair_lane/ppermute | solution.py:302
  248.3 18.3 %conditional.10 = (f32[1024,1024]{1,0:T(8,128)}) conditional(s32[]{:T(128)} %convert_element_type.5, () %tuple.54, (f32[1024,1024]{1,0:T(8,128)}, f32[1040,512]{1,0:T(8,128)}, s32[2]{0:T(128)S(1)}, f32[1024,1024]{1,0:T(8,128)}, f32[1024,1024]{1,0:T(8,128)}, /*index=5*/f32[1024,1024]{1,0:T(8,128)}, f32[512,1024]{1,0:T(8,128)}, ...), branch_computations={%region_11.12_spmd, %region_12.13_spmd} | conditional | flops 1 | bytes 25305176 | solution.py:148
  253.3 4.6 %collective-permute-done.6.refs_10_ = f32[1040,512]{1,0:T(8,128)S(1)} collective-permute-done((f32[1040,512]{1,0:T(8,128)}, f32[1040,512]{1,0:T(8,128)S(1)}, u32[]{:S(2)}, u32[]{:S(2)}) %collective-permute-start.6) | collective-permute-done | bytes 2129952 | tf_op jit(solution)/shard_map/cond/branch_1_fun/far_fold/ppermute | solution.py:302
  257.8 8.7 %branch_1_fun.10 = f32[1024,1024]{1,0:T(8,128)} custom-call(s32[2]{0:T(128)S(1)} %get-tuple-element.129.flags, f32[1024,1024]{1,0:T(8,128)} %get-tuple-element.130.refs_0_, f32[1024,1024]{1,0:T(8,128)} %get-tuple-element.131.refs_1_, f32[1024,1024]{1,0:T(8,128)} %get-tuple-element.132.refs_2_, f32[512,1024]{1,0:T(8,128)} %get-tuple-element.133.refs_3_, ...), custom_call_target="tpu_custom_call" | custom-call | flops 1 | bytes 1 | tf_op jit(solution)/shard_map/cond/branch_1_fun/pallas_call | solution.py:205
  266.6 12.6 %conditional.11 = (f32[1024,1024]{1,0:T(8,128)}) conditional(s32[]{:T(128)} %convert_element_type.5, () %tuple.45, (f32[1024,512]{1,0:T(8,128)}, s32[2]{0:T(128)S(1)}, f32[1024,512]{1,0:T(8,128)}, f32[1024,1]{0,1:T(1,128)S(1)}, f32[1,1024]{1,0:T(1,128)S(1)}, /*index=5*/f32[1024,1024]{1,0:T(8,128)}, f32[1024,1024]{1,0:T(8,128)}) %tuple.81), branch_computations={%region_13.14_spmd, %region_14.15_spmd} | conditional | flops 1 | bytes 8396849 | solution.py:148
  268.1 5.1 %collective-permute-done.7.second = f32[1024,512]{1,0:T(8,128)S(1)} collective-permute-done((f32[1024,512]{1,0:T(8,128)}, f32[1024,512]{1,0:T(8,128)S(1)}, u32[]{:S(2)}, u32[]{:S(2)}) %collective-permute-start.7) | collective-permute-done | bytes 2097184 | tf_op jit(solution)/shard_map/cond/branch_1_fun/far_fold/ppermute | solution.py:302
  273.2 5.9 %branch_1_fun.11 = f32[1024,1024]{1,0:T(8,128)} custom-call(s32[2]{0:T(128)S(1)} %get-tuple-element.142.flags, f32[1024,512]{1,0:T(8,128)} %get-tuple-element.143.merged, f32[1024,512]{1,0:T(8,128)} %get-tuple-element.144.first, f32[1024,512]{1,0:T(8,128)S(1)} %collective-permute-done.7.second, ...), custom_call_target="tpu_custom_call", output_to_operand_aliasing={{}: (7, {})} | custom-call | flops 1 | bytes 1 | tf_op jit(solution)/shard_map/cond/branch_1_fun/pallas_call | solution.py:240
  (51 shorter events, 50.4 us)
Async XLA Ops:
  0.0 1.6 copy-start
  6.0 96.0 %collective-permute-start.8 = (f32[1024,1024]{1,0:T(8,128)}, f32[1024,1024]{1,0:T(8,128)}, u32[]{:S(2)}, u32[]{:S(2)}) collective-permute-start(f32[1024,1024]{1,0:T(8,128)} %get-tuple-element.158.refs_0_), channel_id=1, source_target_pairs={{0,1},{1,0},{2,3},{3,2},{4,5},{5,4},{6,7},{7,6},{8,9},{9,8},{10,11... | collective-permute-start | bytes 12582920 | tf_op jit(solution)/shard_map/pair_block/ppermute | solution.py:306
  7.3 94.7 %collective-permute-start.9 = (f32[1024,1024]{1,0:T(8,128)}, f32[1024,1024]{1,0:T(8,128)}, u32[]{:S(2)}, u32[]{:S(2)}) collective-permute-start(f32[1024,1024]{1,0:T(8,128)} %get-tuple-element.157.from_ref), channel_id=1, source_target_pairs={{1,2},{2,1},{5,6},{6,5},{9,10},{10,9},{13,14},{14,13},{17,18},{18,... | collective-permute-start | bytes 12582920 | tf_op jit(solution)/shard_map/mid_block/ppermute | solution.py:306
  16.1 7.5 %collective-permute-start = (f32[1024,1024]{1,0:T(8,128)}, f32[1024,1024]{1,0:T(8,128)}, u32[]{:S(2)}, u32[]{:S(2)}) collective-permute-start(f32[1024,1024]{1,0:T(8,128)} %get-tuple-element.104.refs_0_.refs_2_), channel_id=1, source_target_pairs={{0,4},{1,5},{2,6},{3,7},{4,0},{5,1},{6,2},{7,3},{8,12},{9,13},{10,... | collective-permute-start | bytes 12582920 | tf_op jit(solution)/shard_map/cond/branch_1_fun/own_other/ppermute | solution.py:302
  44.5 128.6 %collective-permute-start.13 = (f32[1024,1024]{1,0:T(8,128)}, f32[1024,1024]{1,0:T(8,128)}, u32[]{:S(2)}, u32[]{:S(2)}) collective-permute-start(f32[1024,1024]{1,0:T(8,128)} %get-tuple-element.162), channel_id=1, source_target_pairs={{8,0},{13,5},{2,10},{7,15},{24,16},{29,21},{18,26},{23,31}} | collective-permute-start | bytes 12582920 | tf_op jit(solution)/shard_map/own_lane/ppermute | solution.py:302
  47.1 54.9 %collective-permute-start.10 = (f32[16,1024]{1,0:T(8,128)S(1)}, f32[16,1024]{1,0:T(8,128)S(1)}, u32[]{:S(2)}, u32[]{:S(2)}) collective-permute-start(f32[16,1024]{1,0:T(8,128)S(1)} %maximum_maximum_fusion), channel_id=1, source_target_pairs={{1,4},{2,8},{3,12},{4,1},{6,9},{7,13},{8,2},{9,6},{11,14},{12,3},{... | collective-permute-start | bytes 196616 | tf_op jit(solution)/shard_map/moments/ppermute | solution.py:302
  104.6 68.4 %collective-permute-start.12 = (f32[1040,512]{1,0:T(8,128)}, f32[1040,512]{1,0:T(8,128)}, u32[]{:S(2)}, u32[]{:S(2)}) collective-permute-start(f32[1040,512]{1,0:T(8,128)} %shard_map.21), channel_id=1, source_target_pairs={{0,2},{3,1},{4,6},{7,5},{8,10},{11,9},{12,14},{15,13},{16,18},{19,... | collective-permute-start | bytes 6389768 | tf_op jit(solution)/shard_map/far_block/ppermute | solution.py:306
  111.9 94.6 %collective-permute-start.11 = (f32[1040,512]{1,0:T(8,128)S(1)}, f32[1040,512]{1,0:T(8,128)}, u32[]{:S(2)}, u32[]{:S(2)}) collective-permute-start(f32[1040,512]{1,0:T(8,128)S(1)} %shard_map.20), channel_id=1, source_target_pairs={{0,2},{3,1},{4,6},{7,5},{8,10},{11,9},{12,14},{15,13},{16,18},{19,... | collective-permute-start | bytes 6389768 | tf_op jit(solution)/shard_map/far_block/ppermute | solution.py:306
  114.5 15.9 %collective-permute-start.1 = (f32[1024,1024]{1,0:T(8,128)}, f32[1024,1024]{1,0:T(8,128)}, u32[]{:S(2)}, u32[]{:S(2)}) collective-permute-start(f32[1024,1024]{1,0:T(8,128)} %get-tuple-element.111.refs_2_), channel_id=1, source_target_pairs={{0,4},{1,5},{2,6},{3,7},{4,0},{5,1},{6,2},{7,3},{8,12},{9,13},{10,... | collective-permute-start | bytes 12582920 | tf_op jit(solution)/shard_map/cond/branch_1_fun/pair_other/ppermute | solution.py:302
  117.3 13.1 %collective-permute-start.2 = (f32[1024,1024]{1,0:T(8,128)}, f32[1024,1024]{1,0:T(8,128)S(1)}, u32[]{:S(2)}, u32[]{:S(2)}) collective-permute-start(f32[1024,1024]{1,0:T(8,128)} %get-tuple-element.112.refs_4_), channel_id=1, source_target_pairs={{0,4},{1,5},{2,6},{3,7},{4,0},{5,1},{6,2},{7,3},{8,12},{9,13},{10,... | collective-permute-start | bytes 12582920 | tf_op jit(solution)/shard_map/cond/branch_1_fun/mid_other/ppermute | solution.py:302
  151.2 97.0 %collective-permute-start.15 = (f32[1024,1024]{1,0:T(8,128)}, f32[1024,1024]{1,0:T(8,128)}, u32[]{:S(2)}, u32[]{:S(2)}) collective-permute-start(f32[1024,1024]{1,0:T(8,128)} %get-tuple-element.164.refs_4_), channel_id=1, source_target_pairs={{1,9},{14,6},{5,8},{10,7},{13,12},{2,3},{17,25},{30,22},{21,24},{2... | collective-permute-start | bytes 12582920 | tf_op jit(solution)/shard_map/mid_sum/ppermute | solution.py:302
  173.1 4.8 %collective-permute-start.3 = (f32[1040,512]{1,0:T(8,128)}, f32[1040,512]{1,0:T(8,128)S(1)}, u32[]{:S(2)}, u32[]{:S(2)}) collective-permute-start(f32[1040,512]{1,0:T(8,128)} %get-tuple-element.119.refs_4_), channel_id=1, source_target_pairs={{0,4},{1,5},{2,6},{3,7},{4,0},{5,1},{6,2},{7,3},{8,12},{9,13},{10,... | collective-permute-start | bytes 6389768 | tf_op jit(solution)/shard_map/cond/branch_1_fun/far_other/ppermute | solution.py:302
  191.0 4.5 %copy-start.1 = (f32[1024,1024]{1,0:T(8,128)S(1)}, f32[1024,1024]{1,0:T(8,128)}, u32[]{:S(2)}) copy-start(f32[1024,1024]{1,0:T(8,128)} %shard_map.22) | copy-start | bytes 12582916
  194.2 54.0 %collective-permute-start.16 = (f32[1040,512]{1,0:T(8,128)}, f32[1040,512]{1,0:T(8,128)}, u32[]{:S(2)}, u32[]{:S(2)}) collective-permute-start(f32[1040,512]{1,0:T(8,128)} %pad.4), channel_id=1, source_target_pairs={{5,13},{10,2},{1,12},{14,3},{9,8},{6,7},{21,29},{26,18},{17,28},{3... | collective-permute-start | bytes 6389768 | tf_op jit(solution)/shard_map/far_sum/ppermute | solution.py:302
  197.8 32.8 %collective-permute-start.17 = (f32[512,1024]{1,0:T(8,128)}, f32[512,1024]{1,0:T(8,128)}, u32[]{:S(2)}, u32[]{:S(2)}) collective-permute-start(f32[512,1024]{1,0:T(8,128)} %get-tuple-element.213), channel_id=1, source_target_pairs={{12,4},{9,1},{6,14},{3,11},{28,20},{25,17},{22,30},{19,27}} | collective-permute-start | bytes 6291464 | tf_op jit(solution)/shard_map/pair_lane/ppermute | solution.py:302
  203.9 44.4 %collective-permute-start.18 = (f32[512,1024]{1,0:T(8,128)}, f32[512,1024]{1,0:T(8,128)}, u32[]{:S(2)}, u32[]{:S(2)}) collective-permute-start(f32[512,1024]{1,0:T(8,128)} %get-tuple-element.212), channel_id=1, source_target_pairs={{12,4},{9,1},{6,14},{3,11},{28,20},{25,17},{22,30},{19,27}} | collective-permute-start | bytes 6291464 | tf_op jit(solution)/shard_map/pair_lane/ppermute | solution.py:302
  206.5 4.4 %collective-permute-start.4 = (f32[1040,512]{1,0:T(8,128)}, f32[1040,512]{1,0:T(8,128)S(1)}, u32[]{:S(2)}, u32[]{:S(2)}) collective-permute-start(f32[1040,512]{1,0:T(8,128)} %get-tuple-element.127.refs_4_), channel_id=1, source_target_pairs={{0,4},{1,5},{2,6},{3,7},{4,0},{5,1},{6,2},{7,3},{8,12},{9,13},{10,... | collective-permute-start | bytes 6389768 | tf_op jit(solution)/shard_map/cond/branch_1_fun/far_other/ppermute | solution.py:302
  224.0 42.6 %collective-permute-start.14 = (f32[1024,512]{1,0:T(8,128)}, f32[1024,512]{1,0:T(8,128)}, u32[]{:S(2)}, u32[]{:S(2)}) collective-permute-start(f32[1024,512]{1,0:T(8,128)} %get-tuple-element.226), channel_id=1, source_target_pairs={{5,13},{10,2},{1,12},{14,3},{9,8},{6,7},{21,29},{26,18},{17,28},{3... | collective-permute-start | bytes 6291464 | tf_op jit(solution)/shard_map/far_sum/ppermute | solution.py:302
  248.3 9.6 %collective-permute-start.5 = (f32[1024,1024]{1,0:T(8,128)}, f32[1024,1024]{1,0:T(8,128)}, u32[]{:S(2)}, u32[]{:S(2)}) collective-permute-start(f32[1024,1024]{1,0:T(8,128)} %get-tuple-element.136.refs_6_), channel_id=1, source_target_pairs={{12,8},{3,7},{28,24},{19,23}} | collective-permute-start | bytes 12582920 | tf_op jit(solution)/shard_map/cond/branch_1_fun/mid_fold/ppermute | solution.py:302
  251.5 6.3 %collective-permute-start.6 = (f32[1040,512]{1,0:T(8,128)}, f32[1040,512]{1,0:T(8,128)S(1)}, u32[]{:S(2)}, u32[]{:S(2)}) collective-permute-start(f32[1040,512]{1,0:T(8,128)} %get-tuple-element.138.refs_9_), channel_id=1, source_target_pairs={{8,12},{7,3},{24,28},{23,19}} | collective-permute-start | bytes 6389768 | tf_op jit(solution)/shard_map/cond/branch_1_fun/far_fold/ppermute | solution.py:302
  266.6 6.6 %collective-permute-start.7 = (f32[1024,512]{1,0:T(8,128)}, f32[1024,512]{1,0:T(8,128)S(1)}, u32[]{:S(2)}, u32[]{:S(2)}) collective-permute-start(f32[1024,512]{1,0:T(8,128)} %get-tuple-element.144.first), channel_id=1, source_target_pairs={{8,12},{7,3},{24,28},{23,19}} | collective-permute-start | bytes 6291464 | tf_op jit(solution)/shard_map/cond/branch_1_fun/far_fold/ppermute | solution.py:302

commit v3 on v2

--- a/solution.py
+++ b/solution.py
@@ -116,28 +116,29 @@
         )
 
 
-def gram(role, lefts, rights, turned, earlier, columns=None):
+def gram(role, lefts, rights, turned, earlier, rows=None, pad=0):
     width, cells = lefts[0].shape
-    roles = len(lefts) // 2
-    start, size = (0, width) if turned else columns or (0, rights[0].shape[1])
+    roles, rows = len(lefts) // 2, rows or width
+    size = rights[0].shape[0 if turned else 1]
 
     def left_spec(of_role):
         def index(i, role_ref):
-            return (jnp.where(role_ref[0] == of_role, i, 0) if roles > 1 else i), 0
+            at = i + role_ref[1]
+            return (jnp.where(role_ref[0] == of_role, at, 0) if roles > 1 else at), 0
 
         return pl.BlockSpec((TILE, cells), index)
 
-    right_block = (width, cells) if turned else (cells, size)
-    right_shape = (width, 2 * cells) if turned else (2 * cells, size)
+    right_block = (size, cells) if turned else (cells, size)
+    right_shape = (size, 2 * cells) if turned else (2 * cells, size)
     return call(
         functools.partial(gram_kernel, roles, turned),
         scalars=1,
-        grid=(width // TILE,),
+        grid=(rows // TILE,),
         in_specs=[left_spec(n // 2) for n in range(len(lefts))]
-        + [pl.BlockSpec(right_block, lambda i, role_ref: (0, start // size))] * 2
+        + [pl.BlockSpec(right_block, lambda i, role_ref: (0, 0))] * 2
         + [ANYWHERE] * len(earlier),
         out_specs=pl.BlockSpec((TILE, size), lambda i, role_ref: (i, 0)),
-        out_shape=shape(width, size),
+        out_shape=shape(rows + pad, size),
         scratch=[pltpu.VMEM((TILE, 2 * cells), bf16)] * 2 + [pltpu.VMEM(right_shape, bf16)] * 2,
     )(role, *lefts, *rights, *earlier)
 
@@ -179,13 +180,13 @@
             for ref, (used, start) in zip(sums, kinds):
                 if kind in used:
                     tiles.setdefault(start, []).append(ref)
-            for start, (left, *rights) in tiles.items():
+            for start, (left, right) in tiles.items():
                 at = (slice(None), slice(start, start + left.shape[1]))
-                right = rights[0][...]
-                if len(rights) > 1:
-                    right = jnp.where(2 * pl.program_id(0) < pl.num_programs(0), right, rights[1][...])
-                ratio = (left[...] + right) * rs[...] * cs[at] + offset[at]
-                out_ref[at] = power_six(ratio)
+                tile = left[...] + right[...]
+                if kind == 1:
+                    half = 2 * pl.program_id(0) // pl.num_programs(0)
+                    tile = jnp.where(flags[2] == half, left[...], right[...])
+                out_ref[at] = power_six(tile * rs[...] * cs[at] + offset[at])
 
 
 def base(flags, sums, scales, *earlier):
@@ -293,9 +294,10 @@
     outer = ((z == 0) | (z == 3)).astype(jnp.int32)
     kind = jnp.where(k == far_id, 4, 2) + outer
     kind = jnp.where(k == z, 0, jnp.where(k == (z ^ 1), 1, kind))
-    flags = jnp.stack([kind, jnp.where(k == far_id, 1 + outer, 0)]).astype(jnp.int32)
-    far_role = (k % 2 != far_id % 2).astype(jnp.int32)[None]
-    mid_role = 1 - far_role
+    flags = jnp.stack([kind, jnp.where(k == far_id, 1 + outer, 0), k % 2]).astype(jnp.int32)
+    far_role = jnp.stack([(k % 2 != far_id % 2).astype(jnp.int32), 0])
+    mid_role = jnp.stack([1 - far_role[0], 0])
+    pair_half = jnp.stack([0, (k % 2) * (width // 2 // TILE)]).astype(jnp.int32)
 
     def between(part, pairs, name):
         with jax.named_scope(name):
@@ -308,12 +310,9 @@
     def other(part, name):
         return between(part, [((i, b), (i ^ 1, b)) for i in range(4) for b in range(4)], name)
 
-    def to_lane(part, owner, name):
-        return between(part, [((owner[b] ^ 2, b), (owner[b], b)) for b in range(4)], name)
-
-    def in_halves(part, owner, name):
-        half = width // 2
-        return [to_lane(part[:half], owner, name), to_lane(part[half:], owner, name)]
+    def to_lane(part, owner, name, cores=(0,)):
+        pairs = [((owner[b] ^ 2 ^ c, b), (owner[b] ^ c, b)) for b in range(4) for c in cores]
+        return between(part, pairs, name)
 
     def onward(part, owner, name):
         pairs = [((owner[b] ^ 2, b), (owner[b], b)) for b in (1, 2)]
@@ -340,9 +339,9 @@
         right = mid_got, other(mid_got, "mid_other")
         return gram(mid_role, own + pair, right, False, earlier), pair[1]
 
-    def far_work(own, pair, got, earlier):
+    def far_work(own, pair, got, earlier, pad):
         right = got, other(got, "far_other")
-        return gram(far_role, own + pair, right, False, earlier)
+        return gram(far_role, own + pair, right, False, earlier, pad=pad)
 
     own_sum, own_other = together(own_work, turned, mine)
     own = turned, own_other
@@ -356,14 +355,14 @@
     mid_sum, pair_other = together(mid_work, own, pair_got, mid_got, (own_sum,))
     pair = pair_got, pair_other
     mid_far = onward(mid_sum, mid_of, "mid_sum")
-    pair_sum = gram(mid_role, own, pair, True, (mid_sum,))
-    pair_far = in_halves(pair_sum, pair_owner, "pair_lane")
+    pair_sum = gram(pair_half, own, pair, True, (mid_sum,), rows=width // 2, pad=PAD)
+    pair_far = to_lane(pair_sum, pair_owner, "pair_lane", cores=(0, 1))
     waits = [(own_far,), ()]
     far_sums, last = [], pair_sum
     for part, wait in enumerate(waits):
-        last = together(far_work, own, pair, far_got[part], (last, *wait))
-        sent = jnp.pad(last, ((0, PAD), (0, 0))) if part == 0 else last
-        far_sums.append((last, onward(sent, far_of, "far_sum")))
+        work = functools.partial(far_work, pad=PAD if part == 0 else 0)
+        last = together(work, own, pair, far_got[part], (last, *wait))
+        far_sums.append((last, onward(last, far_of, "far_sum")))
 
     column = jnp.where(k == z, mine, column)
     row_scale = 1.0 / jnp.sqrt(variance)
@@ -377,7 +376,10 @@
     scales = (row_scale[:, None], column_scale[None, :], offset)
 
     def base_work(near, mid, fars, scales):
-        sums = [(array, (n // 2 if n < 4 else 1,), 0) for n, array in enumerate(near)]
+        own_sum, own_far, pair_sum, pair_far = near
+        pair_sum += pair_far
+        sums = [(own_sum, (0,), 0), (own_far, (0,), 0)]
+        sums += [(pair_sum, (1,), 0), (other(pair_sum, "pair_fold"), (1,), 0)]
         sums += [(mid[0], (2,), 0), (mid[1], (2, 3), 0), (folded(mid[1], mid_of, "mid_fold"), (3,), 0)]
         for (total, got), (start, _) in zip(fars, far):
             fold = folded(got, far_of, "far_fold")
@@ -388,7 +390,7 @@
         tile = (*tile, folded(tile[1], far_of, "far_fold"))
         return finish(flags, tile, scales, result, far[-1][0])
 
-    near = own_sum, own_far, pair_sum, *pair_far
+    near = own_sum, own_far, pair_sum, pair_far
     result = together(base_work, near, (mid_sum, mid_far), far_sums[:-1], scales)
     return together(last_base_work, far_sums[-1], scales, result)
 

time: 280 us -> 261 us (0.932)
  waiting for transfers between devices: 107 us -> 94.7 us
  local copies, waits for them, and re-layouts: 7.65 us -> 2.12 us
  Pallas kernels: 112 us -> 107 us
  other arithmetic: 0.31 us -> 3.21 us
    ppermute x15, waiting for transfers between devices: 107 us -> 89.5 us  [between(): lax.ppermute(part, BOTH, [(a * 4 + b, c * 4 + d) for (a, b), (c, d) in pa...]
    ppermute x4, waiting for transfers between devices: 0.01 us -> 5.14 us  [along(): return lax.ppermute(part, 'blocks', pairs)]
    pallas_call x5, Pallas kernels: 88.2 us -> 83.6 us  [gram(): call(functools.partial(gram_kernel, roles, turned), scalars=1, grid=(rows...]
    pad x1 -> x0, local copies, waits for them, and re-layouts: 3.25 us -> none  [on_a_line(): sent = jnp.pad(last, ((0, PAD), (0, 0))) if part == 0 else last]
  transfers between devices with their start and end apart: 19 -> 19, of which waited for: 8 -> 8; matrix products, arithmetic and copies ran while one was open for 4% -> 3% of each run, Pallas kernels for 36% -> 37%
where the time goes in v3:
time: 261 us
  Pallas kernels  107 us (41%)
  waiting for transfers between devices  94.7 us (36%)
  starting transfers between devices  42.7 us (16%)
  blocking collectives  5.96 us (2%)
  matrix products  5.15 us (2%)
  other arithmetic  3.21 us (1%)
    ppermute x15, waiting for transfers between devices, between(): lax.ppermute(part, BOTH, [(a * 4 + b, c * 4 + d) for (a, b), (c, d) in pa...  89.5 us
    pallas_call x5, Pallas kernels, gram(): call(functools.partial(gram_kernel, roles, turned), scalars=1, grid=(rows...  83.6 us
    ppermute x15, starting transfers between devices, between(): lax.ppermute(part, BOTH, [(a * 4 + b, c * 4 + d) for (a, b), (c, d) in pa...  30.5 us
    ppermute x4, starting transfers between devices, along(): return lax.ppermute(part, 'blocks', pairs)  12.1 us
    pallas_call x1, Pallas kernels, base(): call(functools.partial(base_kernel, kinds), scalars=1, grid=(width // TIL...  8.63 us
    pallas_call x1, Pallas kernels, finish(): call(finish_kernel, scalars=1, grid=(width // TILE,), in_specs=[whole] *...  5.96 us
    all_gather x1, blocking collectives, statistics(): shards = lax.all_gather(jnp.stack([mean, spread]), 'cells')  5.96 us
  transfers between devices with their start and end apart: 19, of which 8 were waited for; matrix products, arithmetic and copies ran while one was open for 3% of the time, Pallas kernels for 37%

profile of v3, /device:TPU:5, one launch (start us, length us, event | category | flops | bytes accessed | tf_op | source)
XLA Modules:
  0.0 260.7 jit_solution(4984776266140277629)
XLA Ops:
  1.6 4.2 %shard_map.19 = (f32[1024,1024]{1,0:T(8,128)}, f32[1024,1024]{1,0:T(8,128)}, f32[1,1024]{1,0:T(1,128)S(1)}, f32[1,1024]{1,0:T(1,128)S(1)}) custom-call(bf16[1024,1024]{1,0:T(8,128)(2,1)S(1)} %copy-done), custom_call_target="tpu_custom_call" | custom-call | flops 1 | bytes 1 | tf_op jit(solution)/shard_map/pallas_call | solution.py:58
  9.8 6.0 %all-gather.1 = f32[4,2,1024]{2,1,0:T(2,128)S(1)} all-gather(f32[1,2,1024]{2,1,0:T(2,128)S(1)} %maximum_bitcast_fusion), channel_id=2, replica_groups=mesh['groups'=2,'cells'=4,'blocks'=4] {'cells'}, dimensions={0}, use_global_device_ids=true | all-gather | bytes 40960 | tf_op jit(solution)/shard_map/all_gather | solution.py:281
  16.1 28.7 %conditional.6 = (f32[1024,1024]{1,0:T(8,128)}, f32[1024,1024]{1,0:T(8,128)}) conditional(s32[]{:T(128)} %convert_element_type.6, () %tuple.47, (f32[1024,1024]{1,0:T(8,128)}, s32[2]{0:T(128)S(1)}, f32[16,1024]{1,0:T(8,128)S(1)}) %tuple.48), branch_computations={%region_3.4_spmd, %region_4.5_spmd} | conditional | flops 1 | bytes 16777272 | solution.py:149
  16.3 7.3 %collective-permute-done.refs_1_.refs_3_ = f32[1024,1024]{1,0:T(8,128)} collective-permute-done((f32[1024,1024]{1,0:T(8,128)}, f32[1024,1024]{1,0:T(8,128)}, u32[]{:S(2)}, u32[]{:S(2)}) %collective-permute-start) | collective-permute-done | bytes 4194336 | tf_op jit(solution)/shard_map/cond/branch_1_fun/own_other/ppermute | solution.py:304
  23.6 21.2 %branch_1_fun.6 = f32[1024,1024]{1,0:T(8,128)} custom-call(s32[2]{0:T(128)S(1)} %get-tuple-element.93.role_ref, f32[1024,1024]{1,0:T(8,128)} %get-tuple-element.102.refs_0_.refs_2_, f32[1024,1024]{1,0:T(8,128)} %collective-permute-done.refs_1_.refs_3_, f32[1024,1024]{1,0:T(8,128)} %get-tuple-element.102.refs_0_.refs_2_, ...), custom_call_target="tpu_custom_call" | custom-call | flops 1 | bytes 1 | tf_op jit(solution)/shard_map/cond/branch_1_fun/pallas_call | solution.py:133
  51.5 50.3 %collective-permute-done.11.refs_2_ = f32[16,1024]{1,0:T(8,128)S(1)} collective-permute-done((f32[16,1024]{1,0:T(8,128)S(1)}, f32[16,1024]{1,0:T(8,128)S(1)}, u32[]{:S(2)}, u32[]{:S(2)}) %collective-permute-start.11) | collective-permute-done | bytes 65568 | tf_op jit(solution)/shard_map/moments/ppermute | solution.py:304
  104.5 5.6 %collective-permute-start.13 = (f32[1040,512]{1,0:T(8,128)}, f32[1040,512]{1,0:T(8,128)}, u32[]{:S(2)}, u32[]{:S(2)}) collective-permute-start(f32[1040,512]{1,0:T(8,128)} %shard_map.21), channel_id=1, source_target_pairs={{0,2},{3,1},{4,6},{7,5},{8,10},{11,9},{12,14},{15,13},{16,18},{19,... | collective-permute-start | bytes 6389768 | tf_op jit(solution)/shard_map/far_block/ppermute | solution.py:308
  114.4 37.3 %conditional.7 = (f32[1024,1024]{1,0:T(8,128)}, f32[1024,1024]{1,0:T(8,128)}) conditional(s32[]{:T(128)} %convert_element_type.6, () %tuple.49, (f32[1024,1024]{1,0:T(8,128)}, f32[1024,1024]{1,0:T(8,128)}, s32[2]{0:T(128)S(1)}, f32[1024,1024]{1,0:T(8,128)}, f32[1024,1024]{1,0:T(8,128)}, /*index=5*/f32[1024,1024]{1,0:T(8,128)}) %tuple.50), branch_computations={%region_5.6_spmd, %region_6.7_spmd} | conditional | flops 1 | bytes 33554528 | solution.py:149
  117.2 13.1 %collective-permute-done.1.refs_3_ = f32[1024,1024]{1,0:T(8,128)} collective-permute-done((f32[1024,1024]{1,0:T(8,128)}, f32[1024,1024]{1,0:T(8,128)}, u32[]{:S(2)}, u32[]{:S(2)}) %collective-permute-start.1) | collective-permute-done | bytes 4194336 | tf_op jit(solution)/shard_map/cond/branch_1_fun/pair_other/ppermute | solution.py:304
  130.3 21.3 %branch_1_fun.7 = f32[1024,1024]{1,0:T(8,128)} custom-call(s32[2]{0:T(128)S(1)} %get-tuple-element.106.role_ref, f32[1024,1024]{1,0:T(8,128)} %get-tuple-element.107.refs_0_, f32[1024,1024]{1,0:T(8,128)} %get-tuple-element.108.refs_1_, f32[1024,1024]{1,0:T(8,128)} %get-tuple-element.109.refs_2_, f32[1024,1024]{1,0:T(8,128)} %collective-permute-done.1.refs_3_, ...), custom_call_target="tpu_custom_call" | custom-call | flops 1 | bytes 1 | tf_op jit(solution)/shard_map/cond/branch_1_fun/pallas_call | solution.py:133
  153.2 13.8 %shard_map.22 = f32[528,1024]{1,0:T(8,128)} custom-call(s32[2]{0:T(128)S(1)} %pad_add_fusion.2.role_ref, f32[1024,1024]{1,0:T(8,128)} %get-tuple-element.155.refs_0_, f32[1024,1024]{1,0:T(8,128)} %get-tuple-element.158.refs_1_, f32[1024,1024]{1,0:T(8,128)} %collective-permute-done.9.refs_0_.refs_2_, f32[1024,1024]{1,0:T(8,128)} %get-tuple-element.160.refs_3_, ...), custom_call_target="tpu_custom_call" | custom-call | flops 1 | bytes 1 | tf_op jit(solution)/shard_map/pallas_call | solution.py:133
  167.0 5.6 %collective-permute-start.16 = (f32[528,1024]{1,0:T(8,128)}, f32[528,1024]{1,0:T(8,128)}, u32[]{:S(2)}, u32[]{:S(2)}) collective-permute-start(f32[528,1024]{1,0:T(8,128)} %shard_map.22), channel_id=1, source_target_pairs={{12,4},{8,0},{9,1},{13,5},{6,14},{2,10},{3,11},{7,15},{28,20},{24,... | collective-permute-start | bytes 6488072 | tf_op jit(solution)/shard_map/pair_lane/ppermute | solution.py:304
  172.7 18.5 %conditional.8 = (f32[1040,512]{1,0:T(8,128)}) conditional(s32[]{:T(128)} %convert_element_type.6, () %tuple.51, (f32[1040,512]{1,0:T(8,128)}, s32[2]{0:T(128)S(1)}, f32[1024,1024]{1,0:T(8,128)}, f32[1024,1024]{1,0:T(8,128)}, f32[1024,1024]{1,0:T(8,128)}, /*index=5*/f32[1024,1024]{1,0:T(8,128)}, f32[528,1024]{1,0:T(8,128)}, ...), branch_computations={%region_7.8_spmd, %region_8.9_spmd} | conditional | flops 1 | bytes 8519729 | solution.py:149
  177.6 13.7 %branch_1_fun.8 = f32[1040,512]{1,0:T(8,128)} custom-call(s32[2]{0:T(128)S(1)} %get-tuple-element.112.role_ref, f32[1024,1024]{1,0:T(8,128)} %get-tuple-element.113.refs_0_, f32[1024,1024]{1,0:T(8,128)} %get-tuple-element.114.refs_1_, f32[1024,1024]{1,0:T(8,128)} %get-tuple-element.115.refs_2_, f32[1024,1024]{1,0:T(8,128)} %get-tuple-element.116.refs_3_, ...), custom_call_target="tpu_custom_call" | custom-call | flops 1 | bytes 1 | tf_op jit(solution)/shard_map/cond/branch_1_fun/pallas_call | solution.py:133
  192.5 5.1 %collective-permute-done.12 = f32[1040,512]{1,0:T(8,128)} collective-permute-done((f32[1040,512]{1,0:T(8,128)S(1)}, f32[1040,512]{1,0:T(8,128)}, u32[]{:S(2)}, u32[]{:S(2)}) %collective-permute-start.12) | collective-permute-done | bytes 2129952 | tf_op jit(solution)/shard_map/far_block/ppermute | solution.py:308
  197.6 21.2 %conditional.9 = (f32[1024,512]{1,0:T(8,128)}) conditional(s32[]{:T(128)} %convert_element_type.6, () %tuple.46, (f32[1040,512]{1,0:T(8,128)}, s32[2]{0:T(128)S(1)}, f32[1024,1024]{1,0:T(8,128)}, f32[1024,1024]{1,0:T(8,128)}, f32[1024,1024]{1,0:T(8,128)}, /*index=5*/f32[1024,1024]{1,0:T(8,128)}, f32[1040,512]{1,0:T(8,128)}) %tuple.53), branch_computations={%region_9.10_spmd, %region_10.11_spmd} | conditional | flops 1 | bytes 8519729 | solution.py:149
  205.2 13.7 %branch_1_fun.9 = f32[1024,512]{1,0:T(8,128)} custom-call(s32[2]{0:T(128)S(1)} %get-tuple-element.120.role_ref, f32[1024,1024]{1,0:T(8,128)} %get-tuple-element.121.refs_0_, f32[1024,1024]{1,0:T(8,128)} %get-tuple-element.122.refs_1_, f32[1024,1024]{1,0:T(8,128)} %get-tuple-element.123.refs_2_, f32[1024,1024]{1,0:T(8,128)} %get-tuple-element.124.refs_3_, ...), custom_call_target="tpu_custom_call" | custom-call | flops 1 | bytes 1 | tf_op jit(solution)/shard_map/cond/branch_1_fun/pallas_call | solution.py:133
  220.3 5.1 %convolution_multiply_fusion = f32[1024,1024]{1,0:T(8,128)} fusion(f32[16,1024]{1,0:T(8,128)S(1)} %broadcast_select_fusion, f32[4,1024]{1,0:T(4,128)S(1)} %get-tuple-element.206, f32[1024]{0:T(1024)S(1)} %bitcast.16, f32[1024]{0:T(1024)S(1)} %get-tuple-element.203), kind=kOutput, calls=%fused_computation | convolution fusion | flops 51388416 | bytes 4235264 | tf_op jit(solution)/shard_map/dot_general | solution.py:370
  225.5 23.0 %conditional.10 = (f32[1024,1024]{1,0:T(8,128)}) conditional(s32[]{:T(128)} %convert_element_type.6, () %tuple.54, (f32[528,1024]{1,0:T(8,128)}, f32[528,1024]{1,0:T(8,128)}, f32[1024,1024]{1,0:T(8,128)}, f32[1040,512]{1,0:T(8,128)}, s32[3]{0:T(128)S(1)}, /*index=5*/f32[1024,1024]{1,0:T(8,128)}, f32[1024,1024]{1,0:T(8,128)}, ...), branch_computations={%region_11.12_spmd, %region_12.13_spmd} | conditional | flops 540673 | bytes 40444032 | solution.py:149
  234.0 5.9 %collective-permute-done.7.refs_9_ = f32[1040,512]{1,0:T(8,128)} collective-permute-done((f32[1040,512]{1,0:T(8,128)}, f32[1040,512]{1,0:T(8,128)}, u32[]{:S(2)}, u32[]{:S(2)}) %collective-permute-start.7) | collective-permute-done | bytes 2129952 | tf_op jit(solution)/shard_map/cond/branch_1_fun/far_fold/ppermute | solution.py:304
  239.9 8.6 %branch_1_fun.10 = f32[1024,1024]{1,0:T(8,128)} custom-call(s32[3]{0:T(128)S(1)} %get-tuple-element.127.flags, f32[1024,1024]{1,0:T(8,128)} %get-tuple-element.128.refs_0_, f32[1024,1024]{1,0:T(8,128)} %get-tuple-element.129.refs_1_, f32[528,1024]{1,0:T(8,128)S(1)} %add.36.refs_2_, f32[528,1024]{1,0:T(8,128)} %collective-permute-done.5.refs_3_, ...), custom_call_target="tpu_custom_call" | custom-call | flops 1 | bytes 1 | tf_op jit(solution)/shard_map/cond/branch_1_fun/pallas_call | solution.py:206
  248.5 12.2 %conditional.11 = (f32[1024,1024]{1,0:T(8,128)}) conditional(s32[]{:T(128)} %convert_element_type.6, () %tuple.45, (f32[1024,512]{1,0:T(8,128)}, s32[3]{0:T(128)S(1)}, f32[1024,512]{1,0:T(8,128)}, f32[1024,1]{0,1:T(1,128)S(1)}, f32[1,1024]{1,0:T(1,128)S(1)}, /*index=5*/f32[1024,1024]{1,0:T(8,128)}, f32[1024,1024]{1,0:T(8,128)}) %tuple.80), branch_computations={%region_13.14_spmd, %region_14.15_spmd} | conditional | flops 1 | bytes 8396849 | solution.py:149
  250.0 4.7 %collective-permute-done.8.second = f32[1024,512]{1,0:T(8,128)S(1)} collective-permute-done((f32[1024,512]{1,0:T(8,128)}, f32[1024,512]{1,0:T(8,128)S(1)}, u32[]{:S(2)}, u32[]{:S(2)}) %collective-permute-start.8) | collective-permute-done | bytes 2097184 | tf_op jit(solution)/shard_map/cond/branch_1_fun/far_fold/ppermute | solution.py:304
  254.8 6.0 %branch_1_fun.11 = f32[1024,1024]{1,0:T(8,128)} custom-call(s32[3]{0:T(128)S(1)} %get-tuple-element.139.flags, f32[1024,512]{1,0:T(8,128)} %get-tuple-element.140.merged, f32[1024,512]{1,0:T(8,128)} %get-tuple-element.141.first, f32[1024,512]{1,0:T(8,128)S(1)} %collective-permute-done.8.second, ...), custom_call_target="tpu_custom_call", output_to_operand_aliasing={{}: (7, {})} | custom-call | flops 1 | bytes 1 | tf_op jit(solution)/shard_map/cond/branch_1_fun/pallas_call | solution.py:241
  (51 shorter events, 49.2 us)
Async XLA Ops:
  0.0 1.6 copy-start
  5.8 96.0 %collective-permute-start.9 = (f32[1024,1024]{1,0:T(8,128)}, f32[1024,1024]{1,0:T(8,128)}, u32[]{:S(2)}, u32[]{:S(2)}) collective-permute-start(f32[1024,1024]{1,0:T(8,128)} %get-tuple-element.155.refs_0_), channel_id=1, source_target_pairs={{0,1},{1,0},{2,3},{3,2},{4,5},{5,4},{6,7},{7,6},{8,9},{9,8},{10,11... | collective-permute-start | bytes 12582920 | tf_op jit(solution)/shard_map/pair_block/ppermute | solution.py:308
  7.1 94.7 %collective-permute-start.10 = (f32[1024,1024]{1,0:T(8,128)}, f32[1024,1024]{1,0:T(8,128)}, u32[]{:S(2)}, u32[]{:S(2)}) collective-permute-start(f32[1024,1024]{1,0:T(8,128)} %get-tuple-element.154.from_ref), channel_id=1, source_target_pairs={{1,2},{2,1},{5,6},{6,5},{9,10},{10,9},{13,14},{14,13},{17,18},{18,... | collective-permute-start | bytes 12582920 | tf_op jit(solution)/shard_map/mid_block/ppermute | solution.py:308
  16.1 7.5 %collective-permute-start = (f32[1024,1024]{1,0:T(8,128)}, f32[1024,1024]{1,0:T(8,128)}, u32[]{:S(2)}, u32[]{:S(2)}) collective-permute-start(f32[1024,1024]{1,0:T(8,128)} %get-tuple-element.102.refs_0_.refs_2_), channel_id=1, source_target_pairs={{0,4},{1,5},{2,6},{3,7},{4,0},{5,1},{6,2},{7,3},{8,12},{9,13},{10,... | collective-permute-start | bytes 12582920 | tf_op jit(solution)/shard_map/cond/branch_1_fun/own_other/ppermute | solution.py:304
  44.7 128.0 %collective-permute-start.14 = (f32[1024,1024]{1,0:T(8,128)}, f32[1024,1024]{1,0:T(8,128)}, u32[]{:S(2)}, u32[]{:S(2)}) collective-permute-start(f32[1024,1024]{1,0:T(8,128)} %get-tuple-element.159), channel_id=1, source_target_pairs={{8,0},{13,5},{2,10},{7,15},{24,16},{29,21},{18,26},{23,31}} | collective-permute-start | bytes 12582920 | tf_op jit(solution)/shard_map/own_lane/ppermute | solution.py:304
  47.4 54.5 %collective-permute-start.11 = (f32[16,1024]{1,0:T(8,128)S(1)}, f32[16,1024]{1,0:T(8,128)S(1)}, u32[]{:S(2)}, u32[]{:S(2)}) collective-permute-start(f32[16,1024]{1,0:T(8,128)S(1)} %maximum_maximum_fusion), channel_id=1, source_target_pairs={{1,4},{2,8},{3,12},{4,1},{6,9},{7,13},{8,2},{9,6},{11,14},{12,3},{... | collective-permute-start | bytes 196616 | tf_op jit(solution)/shard_map/moments/ppermute | solution.py:304
  104.5 68.2 %collective-permute-start.13 = (f32[1040,512]{1,0:T(8,128)}, f32[1040,512]{1,0:T(8,128)}, u32[]{:S(2)}, u32[]{:S(2)}) collective-permute-start(f32[1040,512]{1,0:T(8,128)} %shard_map.21), channel_id=1, source_target_pairs={{0,2},{3,1},{4,6},{7,5},{8,10},{11,9},{12,14},{15,13},{16,18},{19,... | collective-permute-start | bytes 6389768 | tf_op jit(solution)/shard_map/far_block/ppermute | solution.py:308
  111.8 85.9 %collective-permute-start.12 = (f32[1040,512]{1,0:T(8,128)S(1)}, f32[1040,512]{1,0:T(8,128)}, u32[]{:S(2)}, u32[]{:S(2)}) collective-permute-start(f32[1040,512]{1,0:T(8,128)S(1)} %shard_map.20), channel_id=1, source_target_pairs={{0,2},{3,1},{4,6},{7,5},{8,10},{11,9},{12,14},{15,13},{16,18},{19,... | collective-permute-start | bytes 6389768 | tf_op jit(solution)/shard_map/far_block/ppermute | solution.py:308
  114.4 15.9 %collective-permute-start.1 = (f32[1024,1024]{1,0:T(8,128)}, f32[1024,1024]{1,0:T(8,128)}, u32[]{:S(2)}, u32[]{:S(2)}) collective-permute-start(f32[1024,1024]{1,0:T(8,128)} %get-tuple-element.109.refs_2_), channel_id=1, source_target_pairs={{0,4},{1,5},{2,6},{3,7},{4,0},{5,1},{6,2},{7,3},{8,12},{9,13},{10,... | collective-permute-start | bytes 12582920 | tf_op jit(solution)/shard_map/cond/branch_1_fun/pair_other/ppermute | solution.py:304
  117.2 13.1 %collective-permute-start.2 = (f32[1024,1024]{1,0:T(8,128)}, f32[1024,1024]{1,0:T(8,128)S(1)}, u32[]{:S(2)}, u32[]{:S(2)}) collective-permute-start(f32[1024,1024]{1,0:T(8,128)} %get-tuple-element.110.refs_4_), channel_id=1, source_target_pairs={{0,4},{1,5},{2,6},{3,7},{4,0},{5,1},{6,2},{7,3},{8,12},{9,13},{10,... | collective-permute-start | bytes 12582920 | tf_op jit(solution)/shard_map/cond/branch_1_fun/mid_other/ppermute | solution.py:304
  151.7 73.8 %collective-permute-start.17 = (f32[1024,1024]{1,0:T(8,128)}, f32[1024,1024]{1,0:T(8,128)}, u32[]{:S(2)}, u32[]{:S(2)}) collective-permute-start(f32[1024,1024]{1,0:T(8,128)} %get-tuple-element.161.refs_4_), channel_id=1, source_target_pairs={{1,9},{14,6},{5,8},{10,7},{13,12},{2,3},{17,25},{30,22},{21,24},{2... | collective-permute-start | bytes 12582920 | tf_op jit(solution)/shard_map/mid_sum/ppermute | solution.py:304
  167.0 58.4 %collective-permute-start.16 = (f32[528,1024]{1,0:T(8,128)}, f32[528,1024]{1,0:T(8,128)}, u32[]{:S(2)}, u32[]{:S(2)}) collective-permute-start(f32[528,1024]{1,0:T(8,128)} %shard_map.22), channel_id=1, source_target_pairs={{12,4},{8,0},{9,1},{13,5},{6,14},{2,10},{3,11},{7,15},{28,20},{24,... | collective-permute-start | bytes 6488072 | tf_op jit(solution)/shard_map/pair_lane/ppermute | solution.py:304
  172.7 4.8 %collective-permute-start.3 = (f32[1040,512]{1,0:T(8,128)}, f32[1040,512]{1,0:T(8,128)S(1)}, u32[]{:S(2)}, u32[]{:S(2)}) collective-permute-start(f32[1040,512]{1,0:T(8,128)} %get-tuple-element.117.refs_4_), channel_id=1, source_target_pairs={{0,4},{1,5},{2,6},{3,7},{4,0},{5,1},{6,2},{7,3},{8,12},{9,13},{10,... | collective-permute-start | bytes 6389768 | tf_op jit(solution)/shard_map/cond/branch_1_fun/far_other/ppermute | solution.py:304
  191.2 34.3 %collective-permute-start.18 = (f32[1040,512]{1,0:T(8,128)}, f32[1040,512]{1,0:T(8,128)}, u32[]{:S(2)}, u32[]{:S(2)}) collective-permute-start(f32[1040,512]{1,0:T(8,128)} %get-tuple-element.218), channel_id=1, source_target_pairs={{5,13},{10,2},{1,12},{14,3},{9,8},{6,7},{21,29},{26,18},{17,28},{3... | collective-permute-start | bytes 6389768 | tf_op jit(solution)/shard_map/far_sum/ppermute | solution.py:304
  197.6 7.5 %collective-permute-start.4 = (f32[1040,512]{1,0:T(8,128)}, f32[1040,512]{1,0:T(8,128)S(1)}, u32[]{:S(2)}, u32[]{:S(2)}) collective-permute-start(f32[1040,512]{1,0:T(8,128)} %get-tuple-element.125.refs_4_), channel_id=1, source_target_pairs={{0,4},{1,5},{2,6},{3,7},{4,0},{5,1},{6,2},{7,3},{8,12},{9,13},{10,... | collective-permute-start | bytes 6389768 | tf_op jit(solution)/shard_map/cond/branch_1_fun/far_other/ppermute | solution.py:304
  218.8 29.7 %collective-permute-start.15 = (f32[1024,512]{1,0:T(8,128)}, f32[1024,512]{1,0:T(8,128)}, u32[]{:S(2)}, u32[]{:S(2)}) collective-permute-start(f32[1024,512]{1,0:T(8,128)} %get-tuple-element.219), channel_id=1, source_target_pairs={{5,13},{10,2},{1,12},{14,3},{9,8},{6,7},{21,29},{26,18},{17,28},{3... | collective-permute-start | bytes 6291464 | tf_op jit(solution)/shard_map/far_sum/ppermute | solution.py:304
  225.5 14.3 %collective-permute-start.6 = (f32[1024,1024]{1,0:T(8,128)}, f32[1024,1024]{1,0:T(8,128)}, u32[]{:S(2)}, u32[]{:S(2)}) collective-permute-start(f32[1024,1024]{1,0:T(8,128)} %get-tuple-element.133.refs_5_), channel_id=1, source_target_pairs={{12,8},{3,7},{28,24},{19,23}} | collective-permute-start | bytes 12582920 | tf_op jit(solution)/shard_map/cond/branch_1_fun/mid_fold/ppermute | solution.py:304
  232.1 7.7 %collective-permute-start.5 = (f32[528,1024]{1,0:T(8,128)S(1)}, f32[528,1024]{1,0:T(8,128)}, u32[]{:S(2)}, u32[]{:S(2)}) collective-permute-start(f32[528,1024]{1,0:T(8,128)S(1)} %add.36.refs_2_), channel_id=1, source_target_pairs={{0,4},{1,5},{2,6},{3,7},{4,0},{5,1},{6,2},{7,3},{8,12},{9,13},{10,... | collective-permute-start | bytes 6488072 | tf_op jit(solution)/shard_map/cond/branch_1_fun/pair_fold/ppermute | solution.py:304
  232.2 7.6 %collective-permute-start.7 = (f32[1040,512]{1,0:T(8,128)}, f32[1040,512]{1,0:T(8,128)}, u32[]{:S(2)}, u32[]{:S(2)}) collective-permute-start(f32[1040,512]{1,0:T(8,128)} %get-tuple-element.135.refs_8_), channel_id=1, source_target_pairs={{8,12},{7,3},{24,28},{23,19}} | collective-permute-start | bytes 6389768 | tf_op jit(solution)/shard_map/cond/branch_1_fun/far_fold/ppermute | solution.py:304
  248.5 6.3 %collective-permute-start.8 = (f32[1024,512]{1,0:T(8,128)}, f32[1024,512]{1,0:T(8,128)S(1)}, u32[]{:S(2)}, u32[]{:S(2)}) collective-permute-start(f32[1024,512]{1,0:T(8,128)} %get-tuple-element.141.first), channel_id=1, source_target_pairs={{8,12},{7,3},{24,28},{23,19}} | collective-permute-start | bytes 6291464 | tf_op jit(solution)/shard_map/cond/branch_1_fun/far_fold/ppermute | solution.py:304

commit v4 on v3

--- a/solution.py
+++ b/solution.py
@@ -64,21 +64,31 @@
     )(expression)
 
 
-def copy_kernel(from_ref, *refs):
-    refs[-1][...] = from_ref[...]
-
-
-def columns(source, start, size, *earlier):
+def copy_kernel(from_ref, to_ref):
+    to_ref[...] = from_ref[...]
+
+
+def columns(source, start, size):
     rows = source.shape[0]
     tile = (rows + PAD) // 2
     return call(
         copy_kernel,
         grid=(2,),
-        in_specs=[pl.BlockSpec((tile, size), lambda i: (i, start // size))]
-        + [ANYWHERE] * len(earlier),
+        in_specs=[pl.BlockSpec((tile, size), lambda i: (i, start // size))],
         out_specs=pl.BlockSpec((tile, size), lambda i: (i, 0)),
         out_shape=shape(rows + PAD, size),
-    )(source, *earlier)
+    )(source)
+
+
+def pass_on(value, *earlier):
+    return call(
+        lambda *refs: None,
+        grid=(1,),
+        in_specs=[ANYWHERE] * (1 + len(earlier)),
+        out_specs=ANYWHERE,
+        out_shape=shape(*value.shape),
+        aliases={0: 0},
+    )(value, *earlier)
 
 
 def gram_kernel(roles, turned, role_ref, *refs):
@@ -170,56 +180,51 @@
     )(left, right, *earlier)
 
 
-def base_kernel(kinds, flags, *refs):
-    sums, (rs, cs, offset), out_ref = refs[: len(kinds)], refs[len(kinds) : len(kinds) + 3], refs[-1]
-    for kind in sorted(set(kind for used, _ in kinds for kind in used)):
-
-        @pl.when(flags[0] == kind)
-        def _():
-            tiles = {}
-            for ref, (used, start) in zip(sums, kinds):
-                if kind in used:
-                    tiles.setdefault(start, []).append(ref)
-            for start, (left, right) in tiles.items():
-                at = (slice(None), slice(start, start + left.shape[1]))
-                tile = left[...] + right[...]
-                if kind == 1:
-                    half = 2 * pl.program_id(0) // pl.num_programs(0)
-                    tile = jnp.where(flags[2] == half, left[...], right[...])
-                out_ref[at] = power_six(tile * rs[...] * cs[at] + offset[at])
-
-
-def base(flags, sums, scales, *earlier):
-    width = scales[2].shape[0]
-    arrays, kinds = [array for array, _, _ in sums], [(used, start) for _, used, start in sums]
-
-    def spec(array, used):
+def adjacency(left, right, rs, cs, row_moments, column_moments):
+    between_shards = sum(row_moments[:, n : n + 1] * column_moments[n : n + 1] for n in range(4))
+    return power_six((left + right) * rs * cs + between_shards)
+
+
+def scale_specs(size, column):
+    return [
+        pl.BlockSpec((TILE, 1), lambda i, flags: (i, 0)),
+        pl.BlockSpec((1, size), lambda i, flags: (0, column)),
+        pl.BlockSpec((TILE, 8), lambda i, flags: (i, 0)),
+        pl.BlockSpec((8, size), lambda i, flags: (0, column)),
+    ]
+
+
+def base_kernel(pieces, flags, *refs):
+    (rs, cs, rm, cm, out_ref), refs = refs[-5:], iter(refs)
+    in_first = 2 * pl.program_id(0) < pl.num_programs(0)
+    for start, halves in pieces:
+        left, right = next(refs)[...], next(refs)[...]
+        if halves:
+            left = jnp.where(in_first, left, next(refs)[...])
+            right = jnp.where(in_first, right, next(refs)[...])
+        at = (slice(None), slice(start, start + left.shape[1]))
+        out_ref[at] = adjacency(left, right, rs[...], cs[at], rm[...], cm[at])
+
+
+def base(flags, pieces, scales):
+    width = scales[0].shape[0]
+    arrays = [array for _, *parts in pieces for array in parts]
+
+    def spec(array):
         steps = array.shape[0] // TILE
-
-        def index(i, flags):
-            mine = functools.reduce(jnp.logical_or, [flags[0] == kind for kind in used])
-            return jnp.where(mine, i % steps, 0), 0
-
-        return pl.BlockSpec((TILE, array.shape[1]), index)
-
-    here = pl.BlockSpec((TILE, width), lambda i, flags: (i, 0))
-    return call(
-        functools.partial(base_kernel, kinds),
+        return pl.BlockSpec((TILE, array.shape[1]), lambda i, flags: (i % steps, 0))
+
+    return call(
+        functools.partial(base_kernel, [(start, len(parts) == 4) for start, *parts in pieces]),
         scalars=1,
         grid=(width // TILE,),
-        in_specs=[spec(array, used) for array, used, _ in sums]
-        + [
-            pl.BlockSpec((TILE, 1), lambda i, flags: (i, 0)),
-            pl.BlockSpec((1, width), lambda i, flags: (0, 0)),
-            here,
-        ]
-        + [ANYWHERE] * len(earlier),
-        out_specs=here,
+        in_specs=[spec(array) for array in arrays] + scale_specs(width, 0),
+        out_specs=pl.BlockSpec((TILE, width), lambda i, flags: (i, 0)),
         out_shape=shape(width, width),
-    )(flags, *arrays, *scales, *earlier)
-
-
-def finish_kernel(flags, merged, first, second, rs, cs, offset, before, out_ref):
+    )(flags, *arrays, *scales)
+
+
+def finish_kernel(flags, merged, first, second, rs, cs, rm, cm, before, out_ref):
     @pl.when(flags[1] == 0)
     def _():
         out_ref[...] = before[...]
@@ -228,27 +233,28 @@
 
         @pl.when(flags[1] == 1 + outer)
         def _():
-            tile = left[...] + first[...]
-            out_ref[...] = power_six(tile * rs[...] * cs[...] + offset[...])
+            out_ref[...] = adjacency(left[...], first[...], rs[...], cs[...], rm[...], cm[...])
 
 
 def finish(flags, far, scales, before, start):
-    (row_scale, column_scale, offset), (width, size) = scales, far[0].shape
-    column = start // size
-    whole = pl.BlockSpec((TILE, size), lambda i, flags: (i, 0))
-    here = pl.BlockSpec((TILE, size), lambda i, flags: (i, column))
-    operands = [flags, *far, row_scale, column_scale, offset, before]
+    width, size = before.shape[0], far[0].shape[1]
+    here = pl.BlockSpec((TILE, size), lambda i, flags: (i, start // size))
+
+    def spec(*kinds, column=0):
+        def index(i, flags):
+            used = functools.reduce(jnp.logical_or, [flags[1] == kind for kind in kinds])
+            return jnp.where(used, i, 0), column
+
+        return pl.BlockSpec((TILE, size), index)
+
+    operands = [flags, *far, *scales, before]
     return call(
         finish_kernel,
         scalars=1,
         grid=(width // TILE,),
-        in_specs=[whole] * 3
-        + [
-            pl.BlockSpec((TILE, 1), lambda i, flags: (i, 0)),
-            pl.BlockSpec((1, size), lambda i, flags: (0, column)),
-            here,
-            here,
-        ],
+        in_specs=[spec(1), spec(1, 2), spec(2)]
+        + scale_specs(size, start // size)
+        + [spec(0, column=start // size)],
         out_specs=here,
         out_shape=shape(width, width),
         aliases={len(operands) - 1: 0},
@@ -292,9 +298,9 @@
     own_owner, pair_owner = (0, 1, 2, 3), (1, 0, 3, 2)
     far_id = jnp.where(z < 2, 3, 0)
     outer = ((z == 0) | (z == 3)).astype(jnp.int32)
-    kind = jnp.where(k == far_id, 4, 2) + outer
-    kind = jnp.where(k == z, 0, jnp.where(k == (z ^ 1), 1, kind))
-    flags = jnp.stack([kind, jnp.where(k == far_id, 1 + outer, 0), k % 2]).astype(jnp.int32)
+    kind = jnp.where(k == far_id, 5, 3) + outer
+    kind = jnp.where(k == z, 0, jnp.where(k == (z ^ 1), 1 + k % 2, kind))
+    flags = jnp.stack([kind, jnp.where(k == far_id, 1 + outer, 0)]).astype(jnp.int32)
     far_role = jnp.stack([(k % 2 != far_id % 2).astype(jnp.int32), 0])
     mid_role = jnp.stack([1 - far_role[0], 0])
     pair_half = jnp.stack([0, (k % 2) * (width // 2 // TILE)]).astype(jnp.int32)
@@ -320,6 +326,12 @@
         pairs += [((owner[b] ^ 1, b), (owner[b] ^ 1, b ^ 1)) for b in (1, 2)]
         return between(part, pairs, name)
 
+    def directly(part, owner, name):
+        first = [((owner[b] ^ 2, b), (owner[b], b)) for b in (1, 2)]
+        first += [((owner[b] ^ 3, b), (owner[b], b ^ 1)) for b in (1, 2)]
+        second = [((owner[b] ^ 1, b), (owner[b], b ^ 1)) for b in (1, 2)]
+        return between(part, first, name + "_first"), between(part, second, name + "_second")
+
     def folded(part, owner, name):
         return between(part, [((owner[b] ^ 1, b), (owner[b], b)) for b in (0, 3)], name)
 
@@ -327,29 +339,35 @@
     mid_got = along(centred, [(1, 2), (2, 1)], "mid_block")
     pair_got = along(turned, [(0, 1), (1, 0), (2, 3), (3, 2)], "pair_block")
     far = pieces(width, FAR_WIDTHS)
+    far_parts = [columns(centred, *piece) for piece in far]
     away, variance = statistics(rows, mean[0], spread[0])
     mine = jnp.concatenate([away, variance[None, :], jnp.zeros((11, width), f32)])
 
-    def own_work(turned, mine):
+    def own_work(turned, earlier):
         own = turned, other(turned, "own_other")
-        return gram(mid_role, own, own, True, (mine,)), own[1]
+        return gram(mid_role, own, own, True, earlier), own[1]
 
     def mid_work(own, pair_got, mid_got, earlier):
         pair = pair_got, other(pair_got, "pair_other")
         right = mid_got, other(mid_got, "mid_other")
         return gram(mid_role, own + pair, right, False, earlier), pair[1]
 
-    def far_work(own, pair, got, earlier, pad):
+    def first_far_work(own, pair, got, pair_sum, earlier):
         right = got, other(got, "far_other")
-        return gram(far_role, own + pair, right, False, earlier, pad=pad)
-
-    own_sum, own_other = together(own_work, turned, mine)
+        total = gram(far_role, own + pair, right, False, earlier, pad=PAD)
+        return total, other(pass_on(pair_sum, right[1]), "pair_fold")
+
+    def last_far_work(own, pair, got, earlier):
+        right = got, other(got, "far_other")
+        return gram(far_role, own + pair, right, False, earlier)
+
+    own_sum, own_other = together(own_work, turned, (mine, *far_parts))
     own = turned, own_other
     pairs = [((a, b), (b, a)) for a in range(4) for b in range(4) if a != b]
     column = between(mine, pairs, "moments")
     far_got = []
-    for start, size in far:
-        part = columns(centred, start, size, pair_got, mid_got, column)
+    for part in far_parts:
+        part = pass_on(part, pair_got, mid_got, column)
         far_got.append(along(part, [(0, 2), (3, 1)], "far_block"))
     own_far = to_lane(own_sum, own_owner, "own_lane")
     mid_sum, pair_other = together(mid_work, own, pair_got, mid_got, (own_sum,))
@@ -357,42 +375,37 @@
     mid_far = onward(mid_sum, mid_of, "mid_sum")
     pair_sum = gram(pair_half, own, pair, True, (mid_sum,), rows=width // 2, pad=PAD)
     pair_far = to_lane(pair_sum, pair_owner, "pair_lane", cores=(0, 1))
-    waits = [(own_far,), ()]
-    far_sums, last = [], pair_sum
-    for part, wait in enumerate(waits):
-        work = functools.partial(far_work, pad=PAD if part == 0 else 0)
-        last = together(work, own, pair, far_got[part], (last, *wait))
-        far_sums.append((last, onward(last, far_of, "far_sum")))
+    first_sum, pair_fold = together(
+        first_far_work, own, pair, far_got[0], pair_sum, (pair_sum, own_far)
+    )
+    first_far = onward(first_sum, far_of, "far_sum")
+    last_sum = together(last_far_work, own, pair, far_got[1], (first_sum,))
+    last_far = directly(last_sum, far_of, "far_sum")
 
     column = jnp.where(k == z, mine, column)
     row_scale = 1.0 / jnp.sqrt(variance)
     column_scale = 1.0 / jnp.sqrt(column[4])
-    offset = rows * lax.dot_general(
-        away * row_scale[None, :],
-        column[:4] * column_scale[None, :],
-        (((0,), (0,)), ((), ())),
-        precision=lax.Precision.HIGHEST,
-    )
-    scales = (row_scale[:, None], column_scale[None, :], offset)
-
-    def base_work(near, mid, fars, scales):
-        own_sum, own_far, pair_sum, pair_far = near
-        pair_sum += pair_far
-        sums = [(own_sum, (0,), 0), (own_far, (0,), 0)]
-        sums += [(pair_sum, (1,), 0), (other(pair_sum, "pair_fold"), (1,), 0)]
-        sums += [(mid[0], (2,), 0), (mid[1], (2, 3), 0), (folded(mid[1], mid_of, "mid_fold"), (3,), 0)]
-        for (total, got), (start, _) in zip(fars, far):
-            fold = folded(got, far_of, "far_fold")
-            sums += [(total, (4,), start), (got, (4, 5), start), (fold, (5,), start)]
-        return base(flags, sums, scales)
-
-    def last_base_work(tile, scales, result):
-        tile = (*tile, folded(tile[1], far_of, "far_fold"))
-        return finish(flags, tile, scales, result, far[-1][0])
-
-    near = own_sum, own_far, pair_sum, pair_far
-    result = together(base_work, near, (mid_sum, mid_far), far_sums[:-1], scales)
-    return together(last_base_work, far_sums[-1], scales, result)
+    row_moments = rows * jnp.pad(away * row_scale[None, :], ((0, 4), (0, 0))).T
+    column_moments = jnp.pad(column[:4] * column_scale[None, :], ((0, 4), (0, 0)))
+    scales = row_scale[:, None], column_scale[None, :], row_moments, column_moments
+
+    def base_work(near, mid, far, scales):
+        own_sum, own_far, pair_sum, pair_far, pair_fold = near
+        pair_far_fold = other(pair_far, "pair_fold")
+        cases = [
+            [(0, own_sum, own_far)],
+            [(0, pair_sum, pair_far, pair_fold, pair_far_fold)],
+            [(0, pair_fold, pair_far_fold, pair_sum, pair_far)],
+            [(0, *mid)],
+            [(0, folded(mid[1], mid_of, "mid_fold"), mid[1])],
+            [(0, *far)],
+            [(0, folded(far[1], far_of, "far_fold"), far[1])],
+        ]
+        return lax.switch(flags[0], [lambda case=case: base(flags, case, scales) for case in cases])
+
+    near = own_sum, own_far, pair_sum, pair_far, pair_fold
+    result = together(base_work, near, (mid_sum, mid_far), (first_sum, first_far), scales)
+    return finish(flags, (last_sum, *last_far), scales, result, far[1][0])
 
 
 def on_a_ring(expression):

time: 261 us -> 255 us (0.977)
  local copies, waits for them, and re-layouts: 2.12 us -> 9.29 us
  Pallas kernels: 107 us -> 101 us
  matrix products: 5.15 us -> 0 us
  starting transfers between devices: 42.7 us -> 38.1 us
  other arithmetic: 3.21 us -> 0.56 us
    dot_general x1 -> x0, matrix products: 5.15 us -> none  [on_a_line(): lax.dot_general(away * row_scale[None, :], column[:4] * column_scale[None...]
    unnamed x2 -> x6, local copies, waits for them, and re-layouts: 1.59 us -> 5.14 us
    ppermute x4, waiting for transfers between devices: 5.14 us -> 8.63 us  [along(): return lax.ppermute(part, 'blocks', pairs)]
    pallas_call x2 -> x5, Pallas kernels: 14.6 us -> 11.4 us  [the longest x1 6.05 us: base(): call(functools.partial(base_kernel, [(start, len(parts) == 4) for start,...]
    ppermute x15 -> x16, starting transfers between devices: 30.5 us -> 27.4 us  [between(): lax.ppermute(part, BOTH, [(a * 4 + b, c * 4 + d) for (a, b), (c, d) in pa...]
    add x1 -> x0, other arithmetic: 2.67 us -> none  [base_work(): pair_sum += pair_far]
    ppermute x15 -> x16, waiting for transfers between devices: 89.5 us -> 87.9 us  [between(): lax.ppermute(part, BOTH, [(a * 4 + b, c * 4 + d) for (a, b), (c, d) in pa...]
  transfers between devices with their start and end apart: 19 -> 20, of which waited for: 8 -> 10; matrix products, arithmetic and copies ran while one was open for 3% -> 2% of each run, Pallas kernels for 37% -> 36%
where the time goes in v4:
time: 255 us; the launch traced here: 252 us
  Pallas kernels  101 us (40%)
  waiting for transfers between devices  96.6 us (38%)
  starting transfers between devices  38.1 us (15%)
  local copies, waits for them, and re-layouts  9.29 us (4%)
  blocking collectives  6.24 us (2%)
    ppermute x16, waiting for transfers between devices, between(): lax.ppermute(part, BOTH, [(a * 4 + b, c * 4 + d) for (a, b), (c, d) in pa...  87.9 us
    pallas_call x5, Pallas kernels, gram(): call(functools.partial(gram_kernel, roles, turned), scalars=1, grid=(rows...  83.3 us
    ppermute x16, starting transfers between devices, between(): lax.ppermute(part, BOTH, [(a * 4 + b, c * 4 + d) for (a, b), (c, d) in pa...  27.4 us
    ppermute x4, starting transfers between devices, along(): return lax.ppermute(part, 'blocks', pairs)  10.6 us
    ppermute x4, waiting for transfers between devices, along(): return lax.ppermute(part, 'blocks', pairs)  8.63 us
    all_gather x1, blocking collectives, statistics(): shards = lax.all_gather(jnp.stack([mean, spread]), 'cells')  6.24 us
    pallas_call x1, Pallas kernels, base(): call(functools.partial(base_kernel, [(start, len(parts) == 4) for start,...  6.05 us
    pallas_call x1, Pallas kernels, finish(): call(finish_kernel, scalars=1, grid=(width // TILE,), in_specs=[spec(1),...  5.37 us
  transfers between devices with their start and end apart: 20, of which 10 were waited for; matrix products, arithmetic and copies ran while one was open for 2% of the time, Pallas kernels for 36%

profile of v4, /device:TPU:5, one launch (start us, length us, event | category | flops | bytes accessed | tf_op | source)
XLA Modules:
  0.0 252.2 jit_solution(886859701177780571)
XLA Ops:
  1.6 4.4 %shard_map.17 = (f32[1024,1024]{1,0:T(8,128)}, f32[1024,1024]{1,0:T(8,128)}, f32[1,1024]{1,0:T(1,128)S(1)}, f32[1,1024]{1,0:T(1,128)S(1)}) custom-call(bf16[1024,1024]{1,0:T(8,128)(2,1)S(1)} %copy-done.1), custom_call_target="tpu_custom_call" | custom-call | flops 1 | bytes 1 | tf_op jit(solution)/shard_map/pallas_call | solution.py:58
  15.0 6.2 %all-gather.1 = f32[4,2,1024]{2,1,0:T(2,128)S(1)} all-gather(f32[1,2,1024]{2,1,0:T(2,128)S(1)} %maximum_bitcast_fusion), channel_id=2, replica_groups=mesh['groups'=2,'cells'=4,'blocks'=4] {'cells'}, dimensions={0}, use_global_device_ids=true | all-gather | bytes 40960 | tf_op jit(solution)/shard_map/all_gather | solution.py:287
  21.5 29.1 %conditional.6 = (f32[1024,1024]{1,0:T(8,128)}, f32[1024,1024]{1,0:T(8,128)}) conditional(s32[]{:T(128)} %convert_element_type.17, () %tuple.63, (f32[1024,1024]{1,0:T(8,128)}, s32[2]{0:T(128)S(1)}, f32[16,1024]{1,0:T(8,128)S(1)}, f32[1040,512]{1,0:T(8,128)}, f32[1040,512]{1,0:T(8,128)S(1)}) %tuple.64), branch_computations={%region_3.4_spmd, %region_4.5_spmd} | conditional | flops 1 | bytes 16777272 | solution.py:159
  21.7 7.3 %collective-permute-done.refs_1_.refs_3_ = f32[1024,1024]{1,0:T(8,128)} collective-permute-done((f32[1024,1024]{1,0:T(8,128)}, f32[1024,1024]{1,0:T(8,128)}, u32[]{:S(2)}, u32[]{:S(2)}) %collective-permute-start) | collective-permute-done | bytes 4194336 | tf_op jit(solution)/shard_map/cond/branch_1_fun/own_other/ppermute | solution.py:310
  29.0 21.6 %branch_1_fun.6 = f32[1024,1024]{1,0:T(8,128)} custom-call(s32[2]{0:T(128)S(1)} %get-tuple-element.162.role_ref, f32[1024,1024]{1,0:T(8,128)} %get-tuple-element.163.refs_0_.refs_2_, f32[1024,1024]{1,0:T(8,128)} %collective-permute-done.refs_1_.refs_3_, f32[1024,1024]{1,0:T(8,128)} %get-tuple-element.163.refs_0_.refs_2_, ...), custom_call_target="tpu_custom_call" | custom-call | flops 1 | bytes 1 | tf_op jit(solution)/shard_map/cond/branch_1_fun/pallas_call | solution.py:143
  56.2 48.1 %collective-permute-done.11.refs_3_ = f32[16,1024]{1,0:T(8,128)S(1)} collective-permute-done((f32[16,1024]{1,0:T(8,128)S(1)}, f32[16,1024]{1,0:T(8,128)S(1)}, u32[]{:S(2)}, u32[]{:S(2)}) %collective-permute-start.11) | collective-permute-done | bytes 65568 | tf_op jit(solution)/shard_map/moments/ppermute | solution.py:310
  110.4 35.7 %conditional.7 = (f32[1024,1024]{1,0:T(8,128)}, f32[1024,1024]{1,0:T(8,128)}) conditional(s32[]{:T(128)} %convert_element_type.17, () %tuple.65, (f32[1024,1024]{1,0:T(8,128)}, f32[1024,1024]{1,0:T(8,128)}, s32[2]{0:T(128)S(1)}, f32[1024,1024]{1,0:T(8,128)}, f32[1024,1024]{1,0:T(8,128)}, /*index=5*/f32[1024,1024]{1,0:T(8,128)}) %tuple.66), branch_computations={%region_5.6_spmd, %region_6.7_spmd} | conditional | flops 1 | bytes 33554528 | solution.py:159
  111.6 13.1 %collective-permute-done.1.refs_3_ = f32[1024,1024]{1,0:T(8,128)} collective-permute-done((f32[1024,1024]{1,0:T(8,128)}, f32[1024,1024]{1,0:T(8,128)}, u32[]{:S(2)}, u32[]{:S(2)}) %collective-permute-start.1) | collective-permute-done | bytes 4194336 | tf_op jit(solution)/shard_map/cond/branch_1_fun/pair_other/ppermute | solution.py:310
  124.7 21.4 %branch_1_fun.7 = f32[1024,1024]{1,0:T(8,128)} custom-call(s32[2]{0:T(128)S(1)} %get-tuple-element.210.role_ref, f32[1024,1024]{1,0:T(8,128)} %get-tuple-element.212.refs_0_, f32[1024,1024]{1,0:T(8,128)} %get-tuple-element.214.refs_1_, f32[1024,1024]{1,0:T(8,128)} %get-tuple-element.215.refs_2_, f32[1024,1024]{1,0:T(8,128)} %collective-permute-done.1.refs_3_, ...), custom_call_target="tpu_custom_call" | custom-call | flops 1 | bytes 1 | tf_op jit(solution)/shard_map/cond/branch_1_fun/pallas_call | solution.py:143
  147.6 13.8 %shard_map.22 = f32[528,1024]{1,0:T(8,128)} custom-call(s32[2]{0:T(128)S(1)} %pad_add_fusion.3.role_ref, f32[1024,1024]{1,0:T(8,128)} %get-tuple-element.312.refs_0_, f32[1024,1024]{1,0:T(8,128)} %get-tuple-element.315.refs_1_, f32[1024,1024]{1,0:T(8,128)} %collective-permute-done.9.refs_1_.refs_2_, f32[1024,1024]{1,0:T(8,128)} %get-tuple-element.317.refs_3_, ...), custom_call_target="tpu_custom_call" | custom-call | flops 1 | bytes 1 | tf_op jit(solution)/shard_map/pallas_call | solution.py:143
  161.4 6.3 %collective-permute-start.17 = (f32[528,1024]{1,0:T(8,128)}, f32[528,1024]{1,0:T(8,128)}, u32[]{:S(2)}, u32[]{:S(2)}) collective-permute-start(f32[528,1024]{1,0:T(8,128)} %shard_map.22), channel_id=1, source_target_pairs={{12,4},{8,0},{9,1},{13,5},{6,14},{2,10},{3,11},{7,15},{28,20},{24,... | collective-permute-start | bytes 6488072 | tf_op jit(solution)/shard_map/pair_lane/ppermute | solution.py:310
  167.9 19.1 %conditional.8 = (f32[1040,512]{1,0:T(8,128)}, f32[528,1024]{1,0:T(8,128)}) conditional(s32[]{:T(128)} %convert_element_type.17, () %tuple.67, (f32[1040,512]{1,0:T(8,128)}, s32[2]{0:T(128)S(1)}, f32[1024,1024]{1,0:T(8,128)}, f32[1024,1024]{1,0:T(8,128)}, f32[1024,1024]{1,0:T(8,128)}, /*index=5*/f32[1024,1024]{1,0:T(8,128)}, f32[528,1024]{1,0:T(8,128)}, ...), branch_computations={%region_7.8_spmd, %region_8.9_spmd} | conditional | flops 2 | bytes 21495906 | solution.py:159
  173.3 13.7 %branch_1_fun.8 = f32[1040,512]{1,0:T(8,128)} custom-call(s32[2]{0:T(128)S(1)} %get-tuple-element.218.role_ref, f32[1024,1024]{1,0:T(8,128)} %get-tuple-element.219.refs_0_, f32[1024,1024]{1,0:T(8,128)} %get-tuple-element.220.refs_1_, f32[1024,1024]{1,0:T(8,128)} %get-tuple-element.221.refs_2_, f32[1024,1024]{1,0:T(8,128)} %get-tuple-element.222.refs_3_, ...), custom_call_target="tpu_custom_call" | custom-call | flops 1 | bytes 1 | tf_op jit(solution)/shard_map/cond/branch_1_fun/pallas_call | solution.py:143
  188.2 8.6 %collective-permute-done.12 = f32[1040,512]{1,0:T(8,128)} collective-permute-done((f32[1040,512]{1,0:T(8,128)S(1)}, f32[1040,512]{1,0:T(8,128)}, u32[]{:S(2)}, u32[]{:S(2)}) %collective-permute-start.12) | collective-permute-done | bytes 2129952 | tf_op jit(solution)/shard_map/far_block/ppermute | solution.py:314
  196.9 18.7 %conditional.9 = (f32[1024,512]{1,0:T(8,128)S(1)}) conditional(s32[]{:T(128)} %convert_element_type.17, () %tuple.62, (f32[1040,512]{1,0:T(8,128)}, s32[2]{0:T(128)S(1)}, f32[1024,1024]{1,0:T(8,128)}, f32[1024,1024]{1,0:T(8,128)}, f32[1024,1024]{1,0:T(8,128)}, /*index=5*/f32[1024,1024]{1,0:T(8,128)}, f32[1040,512]{1,0:T(8,128)}) %tuple.69), branch_computations={%region_9.10_spmd, %region_10.11_spmd} | conditional | flops 1 | bytes 8519729 | solution.py:159
  198.7 4.0 %collective-permute-done.5.refs_5_ = f32[1040,512]{1,0:T(8,128)S(1)} collective-permute-done((f32[1040,512]{1,0:T(8,128)}, f32[1040,512]{1,0:T(8,128)S(1)}, u32[]{:S(2)}, u32[]{:S(2)}) %collective-permute-start.5) | collective-permute-done | bytes 2129952 | tf_op jit(solution)/shard_map/cond/branch_1_fun/far_other/ppermute | solution.py:310
  202.8 12.8 %branch_1_fun.10 = f32[1024,512]{1,0:T(8,128)S(1)} custom-call(s32[2]{0:T(128)S(1)} %get-tuple-element.226.role_ref, f32[1024,1024]{1,0:T(8,128)} %get-tuple-element.227.refs_0_, f32[1024,1024]{1,0:T(8,128)} %get-tuple-element.228.refs_1_, f32[1024,1024]{1,0:T(8,128)} %get-tuple-element.229.refs_2_, f32[1024,1024]{1,0:T(8,128)} %get-tuple-element.230.refs_3_, ...), custom_call_target="tpu_custom_call" | custom-call | flops 1 | bytes 1 | tf_op jit(solution)/shard_map/cond/branch_1_fun/pallas_call | solution.py:143
  220.3 18.5 %conditional.10 = (f32[1024,1024]{1,0:T(8,128)}) conditional(s32[]{:T(128)} %convert_element_type.17, () %tuple.70, (s32[]{:T(128)}, f32[528,1024]{1,0:T(8,128)}, f32[1024,1024]{1,0:T(8,128)}, f32[1040,512]{1,0:T(8,128)}, s32[2]{0:T(128)S(1)}, /*index=5*/f32[1024,1024]{1,0:T(8,128)}, f32[1024,1024]{1,0:T(8,128)}, f32[1024,1]{0,1:T(1,128)S(1)}, ...), branch_computations={%region_11.12_spmd, %region_12.20_spmd} | conditional | flops 2 | bytes 34021944 | solution.py:159
  220.3 4.2 %collective-permute-start.7 = (f32[1024,1024]{1,0:T(8,128)}, f32[1024,1024]{1,0:T(8,128)}, u32[]{:S(2)}, u32[]{:S(2)}) collective-permute-start(f32[1024,1024]{1,0:T(8,128)} %get-tuple-element.298), channel_id=1, source_target_pairs={{12,8},{3,7},{28,24},{19,23}} | collective-permute-start | bytes 12582920 | tf_op jit(solution)/shard_map/cond/branch_1_fun/mid_fold/ppermute | solution.py:310
  227.8 4.3 %collective-permute-done.8 = f32[1040,512]{1,0:T(8,128)} collective-permute-done((f32[1040,512]{1,0:T(8,128)}, f32[1040,512]{1,0:T(8,128)}, u32[]{:S(2)}, u32[]{:S(2)}) %collective-permute-start.8) | collective-permute-done | bytes 2129952 | tf_op jit(solution)/shard_map/cond/branch_1_fun/far_fold/ppermute | solution.py:310
  232.7 6.1 %conditional = (f32[1024,1024]{1,0:T(8,128)}) conditional(s32[]{:T(128)} %clamp.2, (s32[2]{0:T(128)S(1)}, f32[1024,1024]{1,0:T(8,128)}, f32[1024,1024]{1,0:T(8,128)}, f32[1024,1]{1,0:T(8,128)}, f32[1,1024]{1,0:T(1,128)S(1)}, /*index=5*/f32[1024,8]{1,0:T(8,128)}, f32[8,1024]{1,0:T(8,128)S(1)}) %tuple.45, ...), branch_computations={%region_13.13_spmd, %region_14.14_spmd, %region_15.15_spmd, %regio... | conditional | flops 1 | bytes 9 | solution.py:404
  232.7 6.1 %branch_6_fun.1 = f32[1024,1024]{1,0:T(8,128)} custom-call(s32[2]{0:T(128)S(1)} %get-tuple-element.279.flags, f32[1040,512]{1,0:T(8,128)} %get-tuple-element.280.refs_0_, f32[1040,512]{1,0:T(8,128)} %get-tuple-element.281.refs_1_, f32[1024,1]{1,0:T(8,128)} %get-tuple-element.282.refs_2_, f32[1,1024]{1,0:T(1,128)S(1)} %get-tuple-element.283.refs_3_, ...), custom_call_target="tpu_custom_call" | custom-call | flops 1 | bytes 1 | tf_op jit(solution)/shard_map/cond/branch_1_fun/cond/branch_6_fun/pallas_call | solution.py:217
  238.8 5.8 %collective-permute-done.16.second = f32[1024,512]{1,0:T(8,128)S(1)} collective-permute-done((f32[1024,512]{1,0:T(8,128)}, f32[1024,512]{1,0:T(8,128)S(1)}, u32[]{:S(2)}, u32[]{:S(2)}) %collective-permute-start.16) | collective-permute-done | bytes 2097184 | tf_op jit(solution)/shard_map/far_sum_second/ppermute | solution.py:310
  246.8 5.4 %shard_map.23 = f32[1024,1024]{1,0:T(8,128)} custom-call(s32[2]{0:T(128)S(1)} %pad_add_fusion.2.flags, f32[1024,512]{1,0:T(8,128)} %copy-done.2, f32[1024,512]{1,0:T(8,128)} %collective-permute-done.15.first, f32[1024,512]{1,0:T(8,128)S(1)} %collective-permute-done.16.second, f32[1024,1]{1,0:T(8,128)S(1)} %copy.15.rs, ...), custom_call_target="tpu_custom_call", output_to_operand_aliasing={{}: (8, {})} | custom-call | flops 1 | bytes 1 | tf_op jit(solution)/shard_map/pallas_call | solution.py:251
  (65 shorter events, 44.8 us)
Async XLA Ops:
  0.0 1.6 copy-start.1
  6.0 98.3 %collective-permute-start.10 = (f32[1024,1024]{1,0:T(8,128)}, f32[1024,1024]{1,0:T(8,128)}, u32[]{:S(2)}, u32[]{:S(2)}) collective-permute-start(f32[1024,1024]{1,0:T(8,128)} %get-tuple-element.311.from_ref), channel_id=1, source_target_pairs={{1,2},{2,1},{5,6},{6,5},{9,10},{10,9},{13,14},{14,13},{17,18},{18,... | collective-permute-start | bytes 12582920 | tf_op jit(solution)/shard_map/mid_block/ppermute | solution.py:314
  8.6 95.7 %collective-permute-start.9 = (f32[1024,1024]{1,0:T(8,128)}, f32[1024,1024]{1,0:T(8,128)}, u32[]{:S(2)}, u32[]{:S(2)}) collective-permute-start(f32[1024,1024]{1,0:T(8,128)} %get-tuple-element.312.refs_0_), channel_id=1, source_target_pairs={{0,1},{1,0},{2,3},{3,2},{4,5},{5,4},{6,7},{7,6},{8,9},{9,8},{10,11... | collective-permute-start | bytes 12582920 | tf_op jit(solution)/shard_map/pair_block/ppermute | solution.py:314
  10.5 2.2 copy-start
  21.5 7.5 %collective-permute-start = (f32[1024,1024]{1,0:T(8,128)}, f32[1024,1024]{1,0:T(8,128)}, u32[]{:S(2)}, u32[]{:S(2)}) collective-permute-start(f32[1024,1024]{1,0:T(8,128)} %get-tuple-element.163.refs_0_.refs_2_), channel_id=1, source_target_pairs={{0,4},{1,5},{2,6},{3,7},{4,0},{5,1},{6,2},{7,3},{8,12},{9,13},{10,... | collective-permute-start | bytes 12582920 | tf_op jit(solution)/shard_map/cond/branch_1_fun/own_other/ppermute | solution.py:310
  50.6 117.3 %collective-permute-start.14 = (f32[1024,1024]{1,0:T(8,128)}, f32[1024,1024]{1,0:T(8,128)}, u32[]{:S(2)}, u32[]{:S(2)}) collective-permute-start(f32[1024,1024]{1,0:T(8,128)} %get-tuple-element.316), channel_id=1, source_target_pairs={{8,0},{13,5},{2,10},{7,15},{24,16},{29,21},{18,26},{23,31}} | collective-permute-start | bytes 12582920 | tf_op jit(solution)/shard_map/own_lane/ppermute | solution.py:310
  53.2 51.1 %collective-permute-start.11 = (f32[16,1024]{1,0:T(8,128)S(1)}, f32[16,1024]{1,0:T(8,128)S(1)}, u32[]{:S(2)}, u32[]{:S(2)}) collective-permute-start(f32[16,1024]{1,0:T(8,128)S(1)} %maximum_maximum_fusion), channel_id=1, source_target_pairs={{1,4},{2,8},{3,12},{4,1},{6,9},{7,13},{8,2},{9,6},{11,14},{12,3},{... | collective-permute-start | bytes 196616 | tf_op jit(solution)/shard_map/moments/ppermute | solution.py:310
  104.3 63.6 %collective-permute-start.13 = (f32[1040,512]{1,0:T(8,128)}, f32[1040,512]{1,0:T(8,128)}, u32[]{:S(2)}, u32[]{:S(2)}) collective-permute-start(f32[1040,512]{1,0:T(8,128)} %shard_map.21), channel_id=1, source_target_pairs={{0,2},{3,1},{4,6},{7,5},{8,10},{11,9},{12,14},{15,13},{16,18},{19,... | collective-permute-start | bytes 6389768 | tf_op jit(solution)/shard_map/far_block/ppermute | solution.py:314
  107.7 89.2 %collective-permute-start.12 = (f32[1040,512]{1,0:T(8,128)S(1)}, f32[1040,512]{1,0:T(8,128)}, u32[]{:S(2)}, u32[]{:S(2)}) collective-permute-start(f32[1040,512]{1,0:T(8,128)S(1)} %shard_map.19), channel_id=1, source_target_pairs={{0,2},{3,1},{4,6},{7,5},{8,10},{11,9},{12,14},{15,13},{16,18},{19,... | collective-permute-start | bytes 6389768 | tf_op jit(solution)/shard_map/far_block/ppermute | solution.py:314
  110.4 14.3 %collective-permute-start.1 = (f32[1024,1024]{1,0:T(8,128)}, f32[1024,1024]{1,0:T(8,128)}, u32[]{:S(2)}, u32[]{:S(2)}) collective-permute-start(f32[1024,1024]{1,0:T(8,128)} %get-tuple-element.215.refs_2_), channel_id=1, source_target_pairs={{0,4},{1,5},{2,6},{3,7},{4,0},{5,1},{6,2},{7,3},{8,12},{9,13},{10,... | collective-permute-start | bytes 12582920 | tf_op jit(solution)/shard_map/cond/branch_1_fun/pair_other/ppermute | solution.py:310
  111.6 13.1 %collective-permute-start.2 = (f32[1024,1024]{1,0:T(8,128)}, f32[1024,1024]{1,0:T(8,128)S(1)}, u32[]{:S(2)}, u32[]{:S(2)}) collective-permute-start(f32[1024,1024]{1,0:T(8,128)} %get-tuple-element.216.refs_4_), channel_id=1, source_target_pairs={{0,4},{1,5},{2,6},{3,7},{4,0},{5,1},{6,2},{7,3},{8,12},{9,13},{10,... | collective-permute-start | bytes 12582920 | tf_op jit(solution)/shard_map/cond/branch_1_fun/mid_other/ppermute | solution.py:310
  146.1 74.2 %collective-permute-start.18 = (f32[1024,1024]{1,0:T(8,128)}, f32[1024,1024]{1,0:T(8,128)}, u32[]{:S(2)}, u32[]{:S(2)}) collective-permute-start(f32[1024,1024]{1,0:T(8,128)} %get-tuple-element.318.refs_4_), channel_id=1, source_target_pairs={{1,9},{14,6},{5,8},{10,7},{13,12},{2,3},{17,25},{30,22},{21,24},{2... | collective-permute-start | bytes 12582920 | tf_op jit(solution)/shard_map/mid_sum/ppermute | solution.py:310
  161.4 58.8 %collective-permute-start.17 = (f32[528,1024]{1,0:T(8,128)}, f32[528,1024]{1,0:T(8,128)}, u32[]{:S(2)}, u32[]{:S(2)}) collective-permute-start(f32[528,1024]{1,0:T(8,128)} %shard_map.22), channel_id=1, source_target_pairs={{12,4},{8,0},{9,1},{13,5},{6,14},{2,10},{3,11},{7,15},{28,20},{24,... | collective-permute-start | bytes 6488072 | tf_op jit(solution)/shard_map/pair_lane/ppermute | solution.py:310
  167.9 5.0 %collective-permute-start.3 = (f32[1040,512]{1,0:T(8,128)}, f32[1040,512]{1,0:T(8,128)S(1)}, u32[]{:S(2)}, u32[]{:S(2)}) collective-permute-start(f32[1040,512]{1,0:T(8,128)} %get-tuple-element.223.refs_4_), channel_id=1, source_target_pairs={{0,4},{1,5},{2,6},{3,7},{4,0},{5,1},{6,2},{7,3},{8,12},{9,13},{10,... | collective-permute-start | bytes 6389768 | tf_op jit(solution)/shard_map/cond/branch_1_fun/far_other/ppermute | solution.py:310
  172.9 14.0 %collective-permute-start.4 = (f32[528,1024]{1,0:T(8,128)S(1)}, f32[528,1024]{1,0:T(8,128)}, u32[]{:S(2)}, u32[]{:S(2)}) collective-permute-start(f32[528,1024]{1,0:T(8,128)S(1)} %branch_1_fun.9), channel_id=1, source_target_pairs={{0,4},{1,5},{2,6},{3,7},{4,0},{5,1},{6,2},{7,3},{8,12},{9,13},{10,... | collective-permute-start | bytes 6488072 | tf_op jit(solution)/shard_map/cond/branch_1_fun/pair_fold/ppermute | solution.py:310
  186.9 33.3 %collective-permute-start.19 = (f32[1040,512]{1,0:T(8,128)}, f32[1040,512]{1,0:T(8,128)}, u32[]{:S(2)}, u32[]{:S(2)}) collective-permute-start(f32[1040,512]{1,0:T(8,128)} %get-tuple-element.319), channel_id=1, source_target_pairs={{5,13},{10,2},{1,12},{14,3},{9,8},{6,7},{21,29},{26,18},{17,28},{3... | collective-permute-start | bytes 6389768 | tf_op jit(solution)/shard_map/far_sum/ppermute | solution.py:310
  196.9 5.9 %collective-permute-start.5 = (f32[1040,512]{1,0:T(8,128)}, f32[1040,512]{1,0:T(8,128)S(1)}, u32[]{:S(2)}, u32[]{:S(2)}) collective-permute-start(f32[1040,512]{1,0:T(8,128)} %get-tuple-element.231.refs_4_), channel_id=1, source_target_pairs={{0,4},{1,5},{2,6},{3,7},{4,0},{5,1},{6,2},{7,3},{8,12},{9,13},{10,... | collective-permute-start | bytes 6389768 | tf_op jit(solution)/shard_map/cond/branch_1_fun/far_other/ppermute | solution.py:310
  215.6 1.4 copy-start.2
  217.0 27.6 %collective-permute-start.16 = (f32[1024,512]{1,0:T(8,128)}, f32[1024,512]{1,0:T(8,128)S(1)}, u32[]{:S(2)}, u32[]{:S(2)}) collective-permute-start(f32[1024,512]{1,0:T(8,128)} %copy-done.2), channel_id=1, source_target_pairs={{9,12},{6,3},{25,28},{22,19}} | collective-permute-start | bytes 6291464 | tf_op jit(solution)/shard_map/far_sum_second/ppermute | solution.py:310
  218.3 28.6 %collective-permute-start.15 = (f32[1024,512]{1,0:T(8,128)}, f32[1024,512]{1,0:T(8,128)}, u32[]{:S(2)}, u32[]{:S(2)}) collective-permute-start(f32[1024,512]{1,0:T(8,128)} %copy-done.2), channel_id=1, source_target_pairs={{5,13},{10,2},{1,12},{14,3},{21,29},{26,18},{17,28},{30,19}} | collective-permute-start | bytes 6291464 | tf_op jit(solution)/shard_map/far_sum_first/ppermute | solution.py:310
  220.3 12.4 %collective-permute-start.7 = (f32[1024,1024]{1,0:T(8,128)}, f32[1024,1024]{1,0:T(8,128)}, u32[]{:S(2)}, u32[]{:S(2)}) collective-permute-start(f32[1024,1024]{1,0:T(8,128)} %get-tuple-element.298), channel_id=1, source_target_pairs={{12,8},{3,7},{28,24},{19,23}} | collective-permute-start | bytes 12582920 | tf_op jit(solution)/shard_map/cond/branch_1_fun/mid_fold/ppermute | solution.py:310
  224.5 8.2 %collective-permute-start.6 = (f32[528,1024]{1,0:T(8,128)}, f32[528,1024]{1,0:T(8,128)}, u32[]{:S(2)}, u32[]{:S(2)}) collective-permute-start(f32[528,1024]{1,0:T(8,128)} %get-tuple-element.295), channel_id=1, source_target_pairs={{0,4},{1,5},{2,6},{3,7},{4,0},{5,1},{6,2},{7,3},{8,12},{9,13},{10,... | collective-permute-start | bytes 6488072 | tf_op jit(solution)/shard_map/cond/branch_1_fun/pair_fold/ppermute | solution.py:310
  224.5 7.6 %collective-permute-start.8 = (f32[1040,512]{1,0:T(8,128)}, f32[1040,512]{1,0:T(8,128)}, u32[]{:S(2)}, u32[]{:S(2)}) collective-permute-start(f32[1040,512]{1,0:T(8,128)} %get-tuple-element.300), channel_id=1, source_target_pairs={{8,12},{7,3},{24,28},{23,19}} | collective-permute-start | bytes 6389768 | tf_op jit(solution)/shard_map/cond/branch_1_fun/far_fold/ppermute | solution.py:310

commit v5 on v4

--- a/solution.py
+++ b/solution.py
@@ -9,7 +9,7 @@
 
 BOTH = ("cells", "blocks")
 TILE = 256
-FAR_WIDTHS = (1, 1)
+FAR_WIDTHS = (2, 1, 1)
 PAD = 16
 f32, bf16 = jnp.float32, jnp.bfloat16
 ANYWHERE = pl.BlockSpec(memory_space=pl.ANY)
@@ -68,15 +68,15 @@
     to_ref[...] = from_ref[...]
 
 
-def columns(source, start, size):
+def columns(source, start, size, pad):
     rows = source.shape[0]
-    tile = (rows + PAD) // 2
+    tile = (rows + pad) // 2
     return call(
         copy_kernel,
         grid=(2,),
         in_specs=[pl.BlockSpec((tile, size), lambda i: (i, start // size))],
         out_specs=pl.BlockSpec((tile, size), lambda i: (i, 0)),
-        out_shape=shape(rows + PAD, size),
+        out_shape=shape(rows + pad, size),
     )(source)
 
 
@@ -91,8 +91,9 @@
     )(value, *earlier)
 
 
-def gram_kernel(roles, turned, role_ref, *refs):
-    lefts, rights = refs[: 2 * roles], refs[2 * roles : 2 * roles + 2]
+def gram_kernel(roles, cores, turned, adds, role_ref, *refs):
+    lefts, rights = refs[: cores * roles], refs[cores * roles : cores * (roles + 1)]
+    before_ref = refs[cores * (roles + 1)]
     out_ref, left_high, left_low, right_high, right_low = refs[-5:]
     cells = lefts[0].shape[1]
 
@@ -107,9 +108,9 @@
 
         @pl.when(role_ref[0] == role if roles > 1 else True)
         def _():
-            for core in range(2):
+            for core in range(cores):
                 at = (slice(None), slice(core * cells, (core + 1) * cells))
-                left_high[at], left_low[at] = split(lefts[2 * role + core][...])
+                left_high[at], left_low[at] = split(lefts[cores * role + core][...])
 
     contract = (((1,), (1 if turned else 0,)), ((), ()))
 
@@ -121,14 +122,16 @@
         span = slice(start, min(start + 512, width))
         at = span if turned else (slice(None), span)
         high, low = right_high[at], right_low[at]
-        out_ref[:, span] = dot(left_high[...], high) + (
+        total = dot(left_high[...], high) + (
             dot(left_high[...], low) + dot(left_low[...], high)
         )
-
-
-def gram(role, lefts, rights, turned, earlier, rows=None, pad=0):
+        out_ref[:, span] = before_ref[:, span] + total if adds else total
+
+
+def gram(role, lefts, rights, turned, earlier, rows=None, pad=0, before=None):
     width, cells = lefts[0].shape
-    roles, rows = len(lefts) // 2, rows or width
+    cores, adds = len(rights), before is not None
+    roles, rows = len(lefts) // cores, rows or width
     size = rights[0].shape[0 if turned else 1]
 
     def left_spec(of_role):
@@ -139,18 +142,20 @@
         return pl.BlockSpec((TILE, cells), index)
 
     right_block = (size, cells) if turned else (cells, size)
-    right_shape = (size, 2 * cells) if turned else (2 * cells, size)
-    return call(
-        functools.partial(gram_kernel, roles, turned),
+    right_shape = (size, cores * cells) if turned else (cores * cells, size)
+    out = pl.BlockSpec((TILE, size), lambda i, role_ref: (i, 0))
+    return call(
+        functools.partial(gram_kernel, roles, cores, turned, adds),
         scalars=1,
         grid=(rows // TILE,),
-        in_specs=[left_spec(n // 2) for n in range(len(lefts))]
-        + [pl.BlockSpec(right_block, lambda i, role_ref: (0, 0))] * 2
+        in_specs=[left_spec(n // cores) for n in range(len(lefts))]
+        + [pl.BlockSpec(right_block, lambda i, role_ref: (0, 0))] * cores
+        + [out] * adds
         + [ANYWHERE] * len(earlier),
-        out_specs=pl.BlockSpec((TILE, size), lambda i, role_ref: (i, 0)),
+        out_specs=out,
         out_shape=shape(rows + pad, size),
-        scratch=[pltpu.VMEM((TILE, 2 * cells), bf16)] * 2 + [pltpu.VMEM(right_shape, bf16)] * 2,
-    )(role, *lefts, *rights, *earlier)
+        scratch=[pltpu.VMEM((TILE, cores * cells), bf16)] * 2 + [pltpu.VMEM(right_shape, bf16)] * 2,
+    )(role, *lefts, *rights, *([before] if adds else []), *earlier)
 
 
 def together(work, *given):
@@ -224,37 +229,45 @@
     )(flags, *arrays, *scales)
 
 
-def finish_kernel(flags, merged, first, second, rs, cs, rm, cm, before, out_ref):
+def finish_kernel(flags, *refs):
+    (rs, cs, rm, cm, before, out_ref), tiles = refs[-6:], refs[:-6]
+
     @pl.when(flags[1] == 0)
     def _():
         out_ref[...] = before[...]
 
-    for outer, left in enumerate((merged, second)):
+    for outer in range(2):
 
         @pl.when(flags[1] == 1 + outer)
         def _():
-            out_ref[...] = adjacency(left[...], first[...], rs[...], cs[...], rm[...], cm[...])
-
-
-def finish(flags, far, scales, before, start):
-    width, size = before.shape[0], far[0].shape[1]
+            for n in range(len(tiles) // 3):
+                merged, first, second = tiles[3 * n : 3 * n + 3]
+                size = first.shape[1]
+                at = (slice(None), slice(n * size, (n + 1) * size))
+                left = (second if outer else merged)[...]
+                out_ref[at] = adjacency(left, first[...], rs[...], cs[at], rm[...], cm[at])
+
+
+def finish(flags, tiles, scales, before, start):
+    width, size = before.shape[0], sum(tile[0].shape[1] for tile in tiles)
     here = pl.BlockSpec((TILE, size), lambda i, flags: (i, start // size))
 
-    def spec(*kinds, column=0):
+    def spec(size, *kinds, column=0):
         def index(i, flags):
             used = functools.reduce(jnp.logical_or, [flags[1] == kind for kind in kinds])
             return jnp.where(used, i, 0), column
 
         return pl.BlockSpec((TILE, size), index)
 
-    operands = [flags, *far, *scales, before]
+    operands = [flags, *(array for tile in tiles for array in tile), *scales, before]
+    in_specs = []
+    for tile in tiles:
+        in_specs += [spec(tile[0].shape[1], *kinds) for kinds in ((1,), (1, 2), (2,))]
     return call(
         finish_kernel,
         scalars=1,
         grid=(width // TILE,),
-        in_specs=[spec(1), spec(1, 2), spec(2)]
-        + scale_specs(size, start // size)
-        + [spec(0, column=start // size)],
+        in_specs=in_specs + scale_specs(size, start // size) + [spec(size, 0, column=start // size)],
         out_specs=here,
         out_shape=shape(width, width),
         aliases={len(operands) - 1: 0},
@@ -326,12 +339,6 @@
         pairs += [((owner[b] ^ 1, b), (owner[b] ^ 1, b ^ 1)) for b in (1, 2)]
         return between(part, pairs, name)
 
-    def directly(part, owner, name):
-        first = [((owner[b] ^ 2, b), (owner[b], b)) for b in (1, 2)]
-        first += [((owner[b] ^ 3, b), (owner[b], b ^ 1)) for b in (1, 2)]
-        second = [((owner[b] ^ 1, b), (owner[b], b ^ 1)) for b in (1, 2)]
-        return between(part, first, name + "_first"), between(part, second, name + "_second")
-
     def folded(part, owner, name):
         return between(part, [((owner[b] ^ 1, b), (owner[b], b)) for b in (0, 3)], name)
 
@@ -339,7 +346,7 @@
     mid_got = along(centred, [(1, 2), (2, 1)], "mid_block")
     pair_got = along(turned, [(0, 1), (1, 0), (2, 3), (3, 2)], "pair_block")
     far = pieces(width, FAR_WIDTHS)
-    far_parts = [columns(centred, *piece) for piece in far]
+    far_parts = [columns(centred, *piece, pad) for piece, pad in zip(far, (PAD, PAD, 4 * PAD))]
     away, variance = statistics(rows, mean[0], spread[0])
     mine = jnp.concatenate([away, variance[None, :], jnp.zeros((11, width), f32)])
 
@@ -347,19 +354,23 @@
         own = turned, other(turned, "own_other")
         return gram(mid_role, own, own, True, earlier), own[1]
 
+    def in_turn(role, own, pair, got, got_other, earlier, pad=0):
+        mine = gram(role, (own[0], pair[0]), (got,), False, earlier)
+        return gram(role, (own[1], pair[1]), (got_other,), False, (), pad=pad, before=mine)
+
     def mid_work(own, pair_got, mid_got, earlier):
         pair = pair_got, other(pair_got, "pair_other")
-        right = mid_got, other(mid_got, "mid_other")
-        return gram(mid_role, own + pair, right, False, earlier), pair[1]
+        mid_other = other(mid_got, "mid_other")
+        return in_turn(mid_role, own, pair, mid_got, mid_other, earlier), pair[1]
 
     def first_far_work(own, pair, got, pair_sum, earlier):
         right = got, other(got, "far_other")
         total = gram(far_role, own + pair, right, False, earlier, pad=PAD)
         return total, other(pass_on(pair_sum, right[1]), "pair_fold")
 
-    def last_far_work(own, pair, got, earlier):
+    def far_work(own, pair, got, earlier):
         right = got, other(got, "far_other")
-        return gram(far_role, own + pair, right, False, earlier)
+        return gram(far_role, own + pair, right, False, earlier, pad=PAD)
 
     own_sum, own_other = together(own_work, turned, (mine, *far_parts))
     own = turned, own_other
@@ -373,14 +384,16 @@
     mid_sum, pair_other = together(mid_work, own, pair_got, mid_got, (own_sum,))
     pair = pair_got, pair_other
     mid_far = onward(mid_sum, mid_of, "mid_sum")
-    pair_sum = gram(pair_half, own, pair, True, (mid_sum,), rows=width // 2, pad=PAD)
+    pair_sum = gram(pair_half, own, pair, True, (mid_sum, own_far), rows=width // 2, pad=PAD)
     pair_far = to_lane(pair_sum, pair_owner, "pair_lane", cores=(0, 1))
     first_sum, pair_fold = together(
-        first_far_work, own, pair, far_got[0], pair_sum, (pair_sum, own_far)
+        first_far_work, own, pair, far_got[0], pair_sum, (pair_sum,)
     )
     first_far = onward(first_sum, far_of, "far_sum")
-    last_sum = together(last_far_work, own, pair, far_got[1], (first_sum,))
-    last_far = directly(last_sum, far_of, "far_sum")
+    second_sum = together(far_work, own, pair, far_got[1], (first_sum,))
+    second_far = onward(second_sum, far_of, "far_sum")
+    last_sum = together(far_work, own, pair, far_got[2], (second_sum,))
+    last_far = onward(last_sum, far_of, "far_sum")
 
     column = jnp.where(k == z, mine, column)
     row_scale = 1.0 / jnp.sqrt(variance)
@@ -403,9 +416,14 @@
         ]
         return lax.switch(flags[0], [lambda case=case: base(flags, case, scales) for case in cases])
 
+    def last_work(fars, scales, result):
+        tiles = [(*tile, folded(tile[1], far_of, "far_fold")) for tile in fars]
+        return finish(flags, tiles, scales, result, far[1][0])
+
     near = own_sum, own_far, pair_sum, pair_far, pair_fold
     result = together(base_work, near, (mid_sum, mid_far), (first_sum, first_far), scales)
-    return finish(flags, (last_sum, *last_far), scales, result, far[1][0])
+    fars = (second_sum, second_far), (last_sum, last_far)
+    return together(last_work, fars, scales, result)
 
 
 def on_a_ring(expression):

time: 255 us -> 246 us (0.965)
  waiting for transfers between devices: 96.6 us -> 75.8 us
  Pallas kernels: 101 us -> 111 us
  starting transfers between devices: 38.1 us -> 44.3 us
    ppermute x16 -> x19, waiting for transfers between devices: 87.9 us -> 75.1 us  [between(): lax.ppermute(part, BOTH, [(a * 4 + b, c * 4 + d) for (a, b), (c, d) in pa...]
    pallas_call x6 -> x8, Pallas kernels: 88.7 us -> 97.7 us  [the longest x7 92.1 us: gram(): call(functools.partial(gram_kernel, roles, cores, turned, adds), scalars=...]
    ppermute x4 -> x5, waiting for transfers between devices: 8.63 us -> 0.69 us  [along(): return lax.ppermute(part, 'blocks', pairs)]
    ppermute x4 -> x5, starting transfers between devices: 10.6 us -> 15.5 us  [along(): return lax.ppermute(part, 'blocks', pairs)]
    ppermute x16 -> x19, starting transfers between devices: 27.4 us -> 28.8 us  [between(): lax.ppermute(part, BOTH, [(a * 4 + b, c * 4 + d) for (a, b), (c, d) in pa...]
    unnamed x6 -> x4, local copies, waits for them, and re-layouts: 5.14 us -> 3.78 us
  transfers between devices with their start and end apart: 20 -> 24, of which waited for: 10 -> 11; matrix products, arithmetic and copies ran while one was open for 2% -> 1% of each run, Pallas kernels for 36% -> 41%
where the time goes in v5:
time: 246 us; the launch traced here: 245 us
  Pallas kernels  111 us (45%)
  waiting for transfers between devices  75.8 us (31%)
  starting transfers between devices  44.3 us (18%)
  local copies, waits for them, and re-layouts  6.86 us (3%)
  blocking collectives  6.24 us (3%)
    pallas_call x7, Pallas kernels, gram(): call(functools.partial(gram_kernel, roles, cores, turned, adds), scalars=...  92.1 us
    ppermute x19, waiting for transfers between devices, between(): lax.ppermute(part, BOTH, [(a * 4 + b, c * 4 + d) for (a, b), (c, d) in pa...  75.1 us
    ppermute x19, starting transfers between devices, between(): lax.ppermute(part, BOTH, [(a * 4 + b, c * 4 + d) for (a, b), (c, d) in pa...  28.8 us
    ppermute x5, starting transfers between devices, along(): return lax.ppermute(part, 'blocks', pairs)  15.5 us
    all_gather x1, blocking collectives, statistics(): shards = lax.all_gather(jnp.stack([mean, spread]), 'cells')  6.24 us
    pallas_call x1, Pallas kernels, base(): call(functools.partial(base_kernel, [(start, len(parts) == 4) for start,...  5.93 us
    pallas_call x1, Pallas kernels, finish(): call(finish_kernel, scalars=1, grid=(width // TILE,), in_specs=in_specs +...  5.62 us
  transfers between devices with their start and end apart: 24, of which 11 were waited for; matrix products, arithmetic and copies ran while one was open for 1% of the time, Pallas kernels for 41%

profile of v5, /device:TPU:5, one launch (start us, length us, event | category | flops | bytes accessed | tf_op | source)
XLA Modules:
  0.0 245.3 jit_solution(10382830628558884967)
XLA Ops:
  1.6 4.3 %shard_map.19 = (f32[1024,1024]{1,0:T(8,128)}, f32[1024,1024]{1,0:T(8,128)}, f32[1,1024]{1,0:T(1,128)S(1)}, f32[1,1024]{1,0:T(1,128)S(1)}) custom-call(bf16[1024,1024]{1,0:T(8,128)(2,1)S(1)} %copy-done.2), custom_call_target="tpu_custom_call" | custom-call | flops 1 | bytes 1 | tf_op jit(solution)/shard_map/pallas_call | solution.py:58
  16.1 6.2 %all-gather.1 = f32[4,2,1024]{2,1,0:T(2,128)S(1)} all-gather(f32[1,2,1024]{2,1,0:T(2,128)S(1)} %maximum_bitcast_fusion), channel_id=2, replica_groups=mesh['groups'=2,'cells'=4,'blocks'=4] {'cells'}, dimensions={0}, use_global_device_ids=true | all-gather | bytes 40960 | tf_op jit(solution)/shard_map/all_gather | solution.py:300
  22.5 28.9 %conditional.8 = (f32[1024,1024]{1,0:T(8,128)}, f32[1024,1024]{1,0:T(8,128)}) conditional(s32[]{:T(128)} %convert_element_type.9, () %tuple.76, (f32[1024,1024]{1,0:T(8,128)}, s32[2]{0:T(128)S(1)}, f32[16,1024]{1,0:T(8,128)S(1)}, f32[1040,512]{1,0:T(8,128)}, f32[1040,256]{1,0:T(8,128)}, /*index=5*/f32[1088,256]{1,0:T(8,128)S(1)}) %tuple.77), branch_computations={%region_3.4_spmd, %region_4.5_spmd} | conditional | flops 1 | bytes 16777272 | solution.py:164
  22.8 7.3 %collective-permute-done.refs_1_.refs_3_ = f32[1024,1024]{1,0:T(8,128)} collective-permute-done((f32[1024,1024]{1,0:T(8,128)}, f32[1024,1024]{1,0:T(8,128)}, u32[]{:S(2)}, u32[]{:S(2)}) %collective-permute-start) | collective-permute-done | bytes 4194336 | tf_op jit(solution)/shard_map/cond/branch_1_fun/own_other/ppermute | solution.py:323
  30.1 21.3 %branch_1_fun.9 = f32[1024,1024]{1,0:T(8,128)} custom-call(s32[2]{0:T(128)S(1)} %get-tuple-element.234.role_ref, f32[1024,1024]{1,0:T(8,128)} %get-tuple-element.235.refs_0_.refs_2_, f32[1024,1024]{1,0:T(8,128)} %collective-permute-done.refs_1_.refs_3_, f32[1024,1024]{1,0:T(8,128)} %get-tuple-element.235.refs_0_.refs_2_, ...), custom_call_target="tpu_custom_call" | custom-call | flops 1 | bytes 1 | tf_op jit(solution)/shard_map/cond/branch_1_fun/pallas_call | solution.py:147
  57.1 47.1 %collective-permute-done.14.refs_3_ = f32[16,1024]{1,0:T(8,128)S(1)} collective-permute-done((f32[16,1024]{1,0:T(8,128)S(1)}, f32[16,1024]{1,0:T(8,128)S(1)}, u32[]{:S(2)}, u32[]{:S(2)}) %collective-permute-start.14) | collective-permute-done | bytes 65568 | tf_op jit(solution)/shard_map/moments/ppermute | solution.py:323
  107.7 27.3 %conditional.9 = (f32[1024,1024]{1,0:T(8,128)}, f32[1024,1024]{1,0:T(8,128)}) conditional(s32[]{:T(128)} %convert_element_type.9, () %tuple.78, (f32[1024,1024]{1,0:T(8,128)}, f32[1024,1024]{1,0:T(8,128)}, s32[2]{0:T(128)S(1)}, f32[1024,1024]{1,0:T(8,128)}, f32[1024,1024]{1,0:T(8,128)}, /*index=5*/f32[1024,1024]{1,0:T(8,128)}) %tuple.79), branch_computations={%region_5.6_spmd, %region_6.7_spmd} | conditional | flops 2 | bytes 50331772 | solution.py:164
  108.9 12.0 %branch_1_fun.10.refs_3_ = f32[1024,1024]{1,0:T(8,128)S(1)} custom-call(s32[2]{0:T(128)S(1)} %get-tuple-element.240.role_ref, f32[1024,1024]{1,0:T(8,128)} %get-tuple-element.257.refs_0_, f32[1024,1024]{1,0:T(8,128)} %get-tuple-element.254.refs_1_, f32[1024,1024]{1,0:T(8,128)} %get-tuple-element.256.refs_2_, f32[1024,1024]{1,0:T(8,128)} %get-tuple-element.258.refs_3_), custom_call_target="tpu_custom_call" | custom-call | flops 1 | bytes 1 | tf_op jit(solution)/shard_map/cond/branch_1_fun/pallas_call | solution.py:147
  122.9 12.1 %branch_1_fun.11 = f32[1024,1024]{1,0:T(8,128)} custom-call(s32[2]{0:T(128)S(1)} %get-tuple-element.240.role_ref, f32[1024,1024]{1,0:T(8,128)} %get-tuple-element.252.refs_0_, f32[1024,1024]{1,0:T(8,128)} %collective-permute-done.1.refs_1_, f32[1024,1024]{1,0:T(8,128)S(1)} %collective-permute-done.2.refs_2_, f32[1024,1024]{1,0:T(8,128)} %copy-done.1), custom_call_target="tpu_custom_call" | custom-call | flops 1 | bytes 1 | tf_op jit(solution)/shard_map/cond/branch_1_fun/pallas_call | solution.py:147
  136.4 5.2 %collective-permute-start.15 = (f32[1040,256]{1,0:T(8,128)}, f32[1040,256]{1,0:T(8,128)}, u32[]{:S(2)}, u32[]{:S(2)}) collective-permute-start(f32[1040,256]{1,0:T(8,128)} %shard_map.21), channel_id=1, source_target_pairs={{0,2},{3,1},{4,6},{7,5},{8,10},{11,9},{12,14},{15,13},{16,18},{19,... | collective-permute-start | bytes 3194888 | tf_op jit(solution)/shard_map/far_block/ppermute | solution.py:327
  143.9 13.0 %shard_map.25 = f32[528,1024]{1,0:T(8,128)S(1)} custom-call(s32[2]{0:T(128)S(1)} %pad_add_fusion.2.role_ref, f32[1024,1024]{1,0:T(8,128)} %get-tuple-element.369.refs_0_, f32[1024,1024]{1,0:T(8,128)} %get-tuple-element.372.refs_1_, f32[1024,1024]{1,0:T(8,128)} %collective-permute-done.12.refs_1_.refs_2_, f32[1024,1024]{1,0:T(8,128)} %get-tuple-element.374.refs_3_, ...), custom_call_target="tpu_custom_call" | custom-call | flops 1 | bytes 1 | tf_op jit(solution)/shard_map/pallas_call | solution.py:147
  160.5 21.1 %conditional.10 = (f32[1040,512]{1,0:T(8,128)}, f32[528,1024]{1,0:T(8,128)}) conditional(s32[]{:T(128)} %convert_element_type.9, () %tuple.80, (f32[1040,512]{1,0:T(8,128)}, s32[2]{0:T(128)S(1)}, f32[1024,1024]{1,0:T(8,128)}, f32[1024,1024]{1,0:T(8,128)}, f32[1024,1024]{1,0:T(8,128)}, /*index=5*/f32[1024,1024]{1,0:T(8,128)}, ...), branch_computations={%region_7.8_spmd, %region_8.9_spmd} | conditional | flops 2 | bytes 21495906 | solution.py:164
  167.9 13.7 %branch_1_fun.12 = f32[1040,512]{1,0:T(8,128)} custom-call(s32[2]{0:T(128)S(1)} %get-tuple-element.259.role_ref, f32[1024,1024]{1,0:T(8,128)} %get-tuple-element.260.refs_0_, f32[1024,1024]{1,0:T(8,128)} %get-tuple-element.261.refs_1_, f32[1024,1024]{1,0:T(8,128)} %get-tuple-element.262.refs_2_, f32[1024,1024]{1,0:T(8,128)} %get-tuple-element.263.refs_3_, ...), custom_call_target="tpu_custom_call" | custom-call | flops 1 | bytes 1 | tf_op jit(solution)/shard_map/cond/branch_1_fun/pallas_call | solution.py:147
  183.0 12.9 %conditional.11 = (f32[1040,256]{1,0:T(8,128)}) conditional(s32[]{:T(128)} %convert_element_type.9, () %tuple.75, (f32[1040,256]{1,0:T(8,128)}, s32[2]{0:T(128)S(1)}, f32[1024,1024]{1,0:T(8,128)}, f32[1024,1024]{1,0:T(8,128)}, f32[1024,1024]{1,0:T(8,128)}, /*index=5*/f32[1024,1024]{1,0:T(8,128)}, f32[1040,512]{1,0:T(8,128)}) %tuple.82), branch_computations={%region_9.10_spmd, %region_10.11_spmd} | conditional | flops 1 | bytes 4259889 | solution.py:164
  185.9 10.0 %branch_1_fun.14 = f32[1040,256]{1,0:T(8,128)} custom-call(s32[2]{0:T(128)S(1)} %get-tuple-element.266.role_ref, f32[1024,1024]{1,0:T(8,128)} %get-tuple-element.267.refs_0_, f32[1024,1024]{1,0:T(8,128)} %get-tuple-element.268.refs_1_, f32[1024,1024]{1,0:T(8,128)} %get-tuple-element.269.refs_2_, f32[1024,1024]{1,0:T(8,128)} %get-tuple-element.270.refs_3_, ...), custom_call_target="tpu_custom_call" | custom-call | flops 1 | bytes 1 | tf_op jit(solution)/shard_map/cond/branch_1_fun/pallas_call | solution.py:147
  197.9 14.4 %conditional.12 = (f32[1040,256]{1,0:T(8,128)}) conditional(s32[]{:T(128)} %convert_element_type.9, () %tuple.83, (f32[1088,256]{1,0:T(8,128)}, s32[2]{0:T(128)S(1)}, f32[1024,1024]{1,0:T(8,128)}, f32[1024,1024]{1,0:T(8,128)}, f32[1024,1024]{1,0:T(8,128)}, /*index=5*/f32[1024,1024]{1,0:T(8,128)}, f32[1040,256]{1,0:T(8,128)}) %tuple.84), branch_computations={%region_11.12_spmd, %region_12.13_spmd} | conditional | flops 1 | bytes 4456497 | solution.py:164
  202.3 10.0 %branch_1_fun.15 = f32[1040,256]{1,0:T(8,128)} custom-call(s32[2]{0:T(128)S(1)} %get-tuple-element.273.role_ref, f32[1024,1024]{1,0:T(8,128)} %get-tuple-element.274.refs_0_, f32[1024,1024]{1,0:T(8,128)} %get-tuple-element.275.refs_1_, f32[1024,1024]{1,0:T(8,128)} %get-tuple-element.276.refs_2_, f32[1024,1024]{1,0:T(8,128)} %get-tuple-element.277.refs_3_, ...), custom_call_target="tpu_custom_call" | custom-call | flops 1 | bytes 1 | tf_op jit(solution)/shard_map/cond/branch_1_fun/pallas_call | solution.py:147
  213.8 18.1 %conditional.13 = (f32[1024,1024]{1,0:T(8,128)}) conditional(s32[]{:T(128)} %convert_element_type.9, () %tuple.85, (s32[]{:T(128)}, f32[528,1024]{1,0:T(8,128)}, f32[1024,1024]{1,0:T(8,128)}, f32[1040,512]{1,0:T(8,128)}, s32[2]{0:T(128)S(1)}, /*index=5*/f32[1024,1024]{1,0:T(8,128)}, f32[1024,1024]{1,0:T(8,128)}, f32[1024,1]{0,1:T(1,128)S(1)}, ...), branch_computations={%region_13.14_spmd, %region_14.22_spmd} | conditional | flops 2 | bytes 34021944 | solution.py:164
  213.8 3.9 %collective-permute-start.8 = (f32[1024,1024]{1,0:T(8,128)}, f32[1024,1024]{1,0:T(8,128)}, u32[]{:S(2)}, u32[]{:S(2)}) collective-permute-start(f32[1024,1024]{1,0:T(8,128)} %get-tuple-element.345), channel_id=1, source_target_pairs={{12,8},{3,7},{28,24},{19,23}} | collective-permute-start | bytes 12582920 | tf_op jit(solution)/shard_map/cond/branch_1_fun/mid_fold/ppermute | solution.py:323
  219.5 5.9 %collective-permute-done.9 = f32[1040,512]{1,0:T(8,128)} collective-permute-done((f32[1040,512]{1,0:T(8,128)}, f32[1040,512]{1,0:T(8,128)}, u32[]{:S(2)}, u32[]{:S(2)}) %collective-permute-start.9) | collective-permute-done | bytes 2129952 | tf_op jit(solution)/shard_map/cond/branch_1_fun/far_fold/ppermute | solution.py:323
  226.0 5.9 %conditional = (f32[1024,1024]{1,0:T(8,128)}) conditional(s32[]{:T(128)} %clamp.2, (s32[2]{0:T(128)S(1)}, f32[1024,1024]{1,0:T(8,128)}, f32[1024,1024]{1,0:T(8,128)}, f32[1024,1]{1,0:T(8,128)S(1)}, f32[1,1024]{1,0:T(1,128)S(1)}, /*index=5*/f32[1024,8]{1,0:T(8,128)S(1)}, f32[8,1024]{1,0:T(8,128)S(1)}) %tuple.53, ...), branch_computations={%region_15.15_spmd, %region_16.16_spmd, %region_17.17_spmd, %regio... | conditional | flops 1 | bytes 9 | solution.py:417
  226.0 5.9 %branch_6_fun.1 = f32[1024,1024]{1,0:T(8,128)} custom-call(s32[2]{0:T(128)S(1)} %get-tuple-element.326.flags, f32[1040,512]{1,0:T(8,128)} %get-tuple-element.327.refs_0_, f32[1040,512]{1,0:T(8,128)} %get-tuple-element.328.refs_1_, f32[1024,1]{1,0:T(8,128)S(1)} %get-tuple-element.329.refs_2_, f32[1,1024]{1,0:T(1,128)S(1)} %get-tuple-element.330.refs_3_, ...), custom_call_target="tpu_custom_call" | custom-call | flops 1 | bytes 1 | tf_op jit(solution)/shard_map/cond/branch_1_fun/cond/branch_6_fun/pallas_call | solution.py:222
  233.4 11.9 %conditional.14 = (f32[1024,1024]{1,0:T(8,128)}) conditional(s32[]{:T(128)} %convert_element_type.9, () %tuple.74, (f32[1040,256]{1,0:T(8,128)}, f32[1040,256]{1,0:T(8,128)}, s32[2]{0:T(128)S(1)}, f32[1040,256]{1,0:T(8,128)}, f32[1040,256]{1,0:T(8,128)}, /*index=5*/f32[1024,1]{0,1:T(1,128)S(1)}, f32[1,1024]{1,0:T(1,128)S(1)}, ...), branch_computations={%region_22.23_spmd, %region_23.24_spmd} | conditional | flops 1 | bytes 8593497 | solution.py:164
  239.7 5.6 %branch_1_fun.17 = f32[1024,1024]{1,0:T(8,128)} custom-call(s32[2]{0:T(128)S(1)} %get-tuple-element.348.flags, f32[1040,256]{1,0:T(8,128)} %get-tuple-element.349.refs_0_, f32[1040,256]{1,0:T(8,128)} %get-tuple-element.350.refs_1_, f32[1040,256]{1,0:T(8,128)S(1)} %collective-permute-done.10.refs_2_, ...), custom_call_target="tpu_custom_call", output_to_operand_aliasing={{}: (11, {})} | custom-call | flops 1 | bytes 1 | tf_op jit(solution)/shard_map/cond/branch_1_fun/pallas_call | solution.py:266
  (79 shorter events, 61.3 us)
Async XLA Ops:
  5.9 98.4 %collective-permute-start.13 = (f32[1024,1024]{1,0:T(8,128)}, f32[1024,1024]{1,0:T(8,128)}, u32[]{:S(2)}, u32[]{:S(2)}) collective-permute-start(f32[1024,1024]{1,0:T(8,128)} %get-tuple-element.368.from_ref), channel_id=1, source_target_pairs={{1,2},{2,1},{5,6},{6,5},{9,10},{10,9},{13,14},{14,13},{17,18},{18,... | collective-permute-start | bytes 12582920 | tf_op jit(solution)/shard_map/mid_block/ppermute | solution.py:327
  8.5 95.7 %collective-permute-start.12 = (f32[1024,1024]{1,0:T(8,128)}, f32[1024,1024]{1,0:T(8,128)}, u32[]{:S(2)}, u32[]{:S(2)}) collective-permute-start(f32[1024,1024]{1,0:T(8,128)} %get-tuple-element.369.refs_0_), channel_id=1, source_target_pairs={{0,1},{1,0},{2,3},{3,2},{4,5},{5,4},{6,7},{7,6},{8,9},{9,8},{10,11... | collective-permute-start | bytes 12582920 | tf_op jit(solution)/shard_map/pair_block/ppermute | solution.py:327
  22.5 7.5 %collective-permute-start = (f32[1024,1024]{1,0:T(8,128)}, f32[1024,1024]{1,0:T(8,128)}, u32[]{:S(2)}, u32[]{:S(2)}) collective-permute-start(f32[1024,1024]{1,0:T(8,128)} %get-tuple-element.235.refs_0_.refs_2_), channel_id=1, source_target_pairs={{0,4},{1,5},{2,6},{3,7},{4,0},{5,1},{6,2},{7,3},{8,12},{9,13},{10,... | collective-permute-start | bytes 12582920 | tf_op jit(solution)/shard_map/cond/branch_1_fun/own_other/ppermute | solution.py:323
  51.4 92.5 %collective-permute-start.17 = (f32[1024,1024]{1,0:T(8,128)}, f32[1024,1024]{1,0:T(8,128)}, u32[]{:S(2)}, u32[]{:S(2)}) collective-permute-start(f32[1024,1024]{1,0:T(8,128)} %get-tuple-element.373), channel_id=1, source_target_pairs={{8,0},{13,5},{2,10},{7,15},{24,16},{29,21},{18,26},{23,31}} | collective-permute-start | bytes 12582920 | tf_op jit(solution)/shard_map/own_lane/ppermute | solution.py:323
  54.1 50.1 %collective-permute-start.14 = (f32[16,1024]{1,0:T(8,128)S(1)}, f32[16,1024]{1,0:T(8,128)S(1)}, u32[]{:S(2)}, u32[]{:S(2)}) collective-permute-start(f32[16,1024]{1,0:T(8,128)S(1)} %maximum_maximum_fusion), channel_id=1, source_target_pairs={{1,4},{2,8},{3,12},{4,1},{6,9},{7,13},{8,2},{9,6},{11,14},{12,3},{... | collective-permute-start | bytes 196616 | tf_op jit(solution)/shard_map/moments/ppermute | solution.py:323
  104.2 56.3 %collective-permute-start.16 = (f32[1040,512]{1,0:T(8,128)}, f32[1040,512]{1,0:T(8,128)}, u32[]{:S(2)}, u32[]{:S(2)}) collective-permute-start(f32[1040,512]{1,0:T(8,128)} %shard_map.24), channel_id=1, source_target_pairs={{0,2},{3,1},{4,6},{7,5},{8,10},{11,9},{12,14},{15,13},{16,18},{19,... | collective-permute-start | bytes 6389768 | tf_op jit(solution)/shard_map/far_block/ppermute | solution.py:327
  107.7 15.2 %collective-permute-start.1 = (f32[1024,1024]{1,0:T(8,128)}, f32[1024,1024]{1,0:T(8,128)}, u32[]{:S(2)}, u32[]{:S(2)}) collective-permute-start(f32[1024,1024]{1,0:T(8,128)} %get-tuple-element.254.refs_1_), channel_id=1, source_target_pairs={{0,4},{1,5},{2,6},{3,7},{4,0},{5,1},{6,2},{7,3},{8,12},{9,13},{10,... | collective-permute-start | bytes 12582920 | tf_op jit(solution)/shard_map/cond/branch_1_fun/pair_other/ppermute | solution.py:323
  108.9 14.0 %collective-permute-start.2 = (f32[1024,1024]{1,0:T(8,128)}, f32[1024,1024]{1,0:T(8,128)S(1)}, u32[]{:S(2)}, u32[]{:S(2)}) collective-permute-start(f32[1024,1024]{1,0:T(8,128)} %get-tuple-element.256.refs_2_), channel_id=1, source_target_pairs={{0,4},{1,5},{2,6},{3,7},{4,0},{5,1},{6,2},{7,3},{8,12},{9,13},{10,... | collective-permute-start | bytes 12582920 | tf_op jit(solution)/shard_map/cond/branch_1_fun/mid_other/ppermute | solution.py:323
  135.0 78.8 %collective-permute-start.22 = (f32[1024,1024]{1,0:T(8,128)}, f32[1024,1024]{1,0:T(8,128)}, u32[]{:S(2)}, u32[]{:S(2)}) collective-permute-start(f32[1024,1024]{1,0:T(8,128)} %get-tuple-element.375.refs_4_), channel_id=1, source_target_pairs={{1,9},{14,6},{5,8},{10,7},{13,12},{2,3},{17,25},{30,22},{21,24},{2... | collective-permute-start | bytes 12582920 | tf_op jit(solution)/shard_map/mid_sum/ppermute | solution.py:323
  136.4 46.6 %collective-permute-start.15 = (f32[1040,256]{1,0:T(8,128)}, f32[1040,256]{1,0:T(8,128)}, u32[]{:S(2)}, u32[]{:S(2)}) collective-permute-start(f32[1040,256]{1,0:T(8,128)} %shard_map.21), channel_id=1, source_target_pairs={{0,2},{3,1},{4,6},{7,5},{8,10},{11,9},{12,14},{15,13},{16,18},{19,... | collective-permute-start | bytes 3194888 | tf_op jit(solution)/shard_map/far_block/ppermute | solution.py:327
  141.6 56.3 %collective-permute-start.19 = (f32[1088,256]{1,0:T(8,128)S(1)}, f32[1088,256]{1,0:T(8,128)}, u32[]{:S(2)}, u32[]{:S(2)}) collective-permute-start(f32[1088,256]{1,0:T(8,128)S(1)} %shard_map.26), channel_id=1, source_target_pairs={{0,2},{3,1},{4,6},{7,5},{8,10},{11,9},{12,14},{15,13},{16,18},{19,... | collective-permute-start | bytes 3342344 | tf_op jit(solution)/shard_map/far_block/ppermute | solution.py:327
  156.9 56.9 %collective-permute-start.21 = (f32[528,1024]{1,0:T(8,128)S(1)}, f32[528,1024]{1,0:T(8,128)}, u32[]{:S(2)}, u32[]{:S(2)}) collective-permute-start(f32[528,1024]{1,0:T(8,128)S(1)} %shard_map.25), channel_id=1, source_target_pairs={{12,4},{8,0},{9,1},{13,5},{6,14},{2,10},{3,11},{7,15},{28,20},{24,... | collective-permute-start | bytes 6488072 | tf_op jit(solution)/shard_map/pair_lane/ppermute | solution.py:323
  160.5 7.0 %collective-permute-start.3 = (f32[1040,512]{1,0:T(8,128)}, f32[1040,512]{1,0:T(8,128)S(1)}, u32[]{:S(2)}, u32[]{:S(2)}) collective-permute-start(f32[1040,512]{1,0:T(8,128)} %get-tuple-element.264.refs_4_), channel_id=1, source_target_pairs={{0,4},{1,5},{2,6},{3,7},{4,0},{5,1},{6,2},{7,3},{8,12},{9,13},{10,... | collective-permute-start | bytes 6389768 | tf_op jit(solution)/shard_map/cond/branch_1_fun/far_other/ppermute | solution.py:323
  167.6 14.0 %collective-permute-start.4 = (f32[528,1024]{1,0:T(8,128)S(1)}, f32[528,1024]{1,0:T(8,128)}, u32[]{:S(2)}, u32[]{:S(2)}) collective-permute-start(f32[528,1024]{1,0:T(8,128)S(1)} %branch_1_fun.13), channel_id=1, source_target_pairs={{0,4},{1,5},{2,6},{3,7},{4,0},{5,1},{6,2},{7,3},{8,12},{9,13},{10,... | collective-permute-start | bytes 6488072 | tf_op jit(solution)/shard_map/cond/branch_1_fun/pair_fold/ppermute | solution.py:323
  181.6 32.2 %collective-permute-start.23 = (f32[1040,512]{1,0:T(8,128)}, f32[1040,512]{1,0:T(8,128)}, u32[]{:S(2)}, u32[]{:S(2)}) collective-permute-start(f32[1040,512]{1,0:T(8,128)} %get-tuple-element.376), channel_id=1, source_target_pairs={{5,13},{10,2},{1,12},{14,3},{9,8},{6,7},{21,29},{26,18},{17,28},{3... | collective-permute-start | bytes 6389768 | tf_op jit(solution)/shard_map/far_sum/ppermute | solution.py:323
  183.0 3.0 %collective-permute-start.5 = (f32[1040,256]{1,0:T(8,128)}, f32[1040,256]{1,0:T(8,128)S(1)}, u32[]{:S(2)}, u32[]{:S(2)}) collective-permute-start(f32[1040,256]{1,0:T(8,128)} %get-tuple-element.271.refs_4_), channel_id=1, source_target_pairs={{0,4},{1,5},{2,6},{3,7},{4,0},{5,1},{6,2},{7,3},{8,12},{9,13},{10,... | collective-permute-start | bytes 3194888 | tf_op jit(solution)/shard_map/cond/branch_1_fun/far_other/ppermute | solution.py:323
  195.9 37.5 %collective-permute-start.18 = (f32[1040,256]{1,0:T(8,128)}, f32[1040,256]{1,0:T(8,128)}, u32[]{:S(2)}, u32[]{:S(2)}) collective-permute-start(f32[1040,256]{1,0:T(8,128)} %get-tuple-element.476), channel_id=1, source_target_pairs={{5,13},{10,2},{1,12},{14,3},{9,8},{6,7},{21,29},{26,18},{17,28},{3... | collective-permute-start | bytes 3194888 | tf_op jit(solution)/shard_map/far_sum/ppermute | solution.py:323
  197.9 4.4 %collective-permute-start.6 = (f32[1088,256]{1,0:T(8,128)}, f32[1088,256]{1,0:T(8,128)S(1)}, u32[]{:S(2)}, u32[]{:S(2)}) collective-permute-start(f32[1088,256]{1,0:T(8,128)} %get-tuple-element.278.refs_4_), channel_id=1, source_target_pairs={{0,4},{1,5},{2,6},{3,7},{4,0},{5,1},{6,2},{7,3},{8,12},{9,13},{10,... | collective-permute-start | bytes 3342344 | tf_op jit(solution)/shard_map/cond/branch_1_fun/far_other/ppermute | solution.py:323
  212.3 21.1 %collective-permute-start.20 = (f32[1040,256]{1,0:T(8,128)}, f32[1040,256]{1,0:T(8,128)}, u32[]{:S(2)}, u32[]{:S(2)}) collective-permute-start(f32[1040,256]{1,0:T(8,128)} %get-tuple-element.477), channel_id=1, source_target_pairs={{5,13},{10,2},{1,12},{14,3},{9,8},{6,7},{21,29},{26,18},{17,28},{3... | collective-permute-start | bytes 3194888 | tf_op jit(solution)/shard_map/far_sum/ppermute | solution.py:323
  213.8 12.2 %collective-permute-start.8 = (f32[1024,1024]{1,0:T(8,128)}, f32[1024,1024]{1,0:T(8,128)}, u32[]{:S(2)}, u32[]{:S(2)}) collective-permute-start(f32[1024,1024]{1,0:T(8,128)} %get-tuple-element.345), channel_id=1, source_target_pairs={{12,8},{3,7},{28,24},{19,23}} | collective-permute-start | bytes 12582920 | tf_op jit(solution)/shard_map/cond/branch_1_fun/mid_fold/ppermute | solution.py:323
  217.8 8.2 %collective-permute-start.7 = (f32[528,1024]{1,0:T(8,128)}, f32[528,1024]{1,0:T(8,128)}, u32[]{:S(2)}, u32[]{:S(2)}) collective-permute-start(f32[528,1024]{1,0:T(8,128)} %get-tuple-element.342), channel_id=1, source_target_pairs={{0,4},{1,5},{2,6},{3,7},{4,0},{5,1},{6,2},{7,3},{8,12},{9,13},{10,... | collective-permute-start | bytes 6488072 | tf_op jit(solution)/shard_map/cond/branch_1_fun/pair_fold/ppermute | solution.py:323
  217.8 7.6 %collective-permute-start.9 = (f32[1040,512]{1,0:T(8,128)}, f32[1040,512]{1,0:T(8,128)}, u32[]{:S(2)}, u32[]{:S(2)}) collective-permute-start(f32[1040,512]{1,0:T(8,128)} %get-tuple-element.347), channel_id=1, source_target_pairs={{8,12},{7,3},{24,28},{23,19}} | collective-permute-start | bytes 6389768 | tf_op jit(solution)/shard_map/cond/branch_1_fun/far_fold/ppermute | solution.py:323
  233.4 4.8 %collective-permute-start.11 = (f32[1040,256]{1,0:T(8,128)}, f32[1040,256]{1,0:T(8,128)S(1)}, u32[]{:S(2)}, u32[]{:S(2)}) collective-permute-start(f32[1040,256]{1,0:T(8,128)} %get-tuple-element.352.refs_4_), channel_id=1, source_target_pairs={{8,12},{7,3},{24,28},{23,19}} | collective-permute-start | bytes 3194888 | tf_op jit(solution)/shard_map/cond/branch_1_fun/far_fold/ppermute | solution.py:323
  234.7 5.0 %collective-permute-start.10 = (f32[1040,256]{1,0:T(8,128)}, f32[1040,256]{1,0:T(8,128)S(1)}, u32[]{:S(2)}, u32[]{:S(2)}) collective-permute-start(f32[1040,256]{1,0:T(8,128)} %get-tuple-element.350.refs_1_), channel_id=1, source_target_pairs={{8,12},{7,3},{24,28},{23,19}} | collective-permute-start | bytes 3194888 | tf_op jit(solution)/shard_map/cond/branch_1_fun/far_fold/ppermute | solution.py:323
  (3 other events, 5.8 us)

commit v6 on v5

--- a/solution.py
+++ b/solution.py
@@ -9,13 +9,14 @@
 
 BOTH = ("cells", "blocks")
 TILE = 256
+WIDE = 512
 FAR_WIDTHS = (2, 1, 1)
 PAD = 16
 f32, bf16 = jnp.float32, jnp.bfloat16
 ANYWHERE = pl.BlockSpec(memory_space=pl.ANY)
 
 
-def call(kernel, *, grid, in_specs, out_specs, out_shape, scratch=(), scalars=0, aliases=None, flops=1):
+def call(kernel, *, grid, in_specs, out_specs, out_shape, scratch=(), scalars=0, aliases=None, vmem=40, flops=1):
     return pl.pallas_call(
         kernel,
         grid_spec=pltpu.PrefetchScalarGridSpec(
@@ -28,7 +29,7 @@
         out_shape=out_shape,
         input_output_aliases=aliases or {},
         cost_estimate=pl.CostEstimate(flops=flops, bytes_accessed=1, transcendentals=0),
-        compiler_params=pltpu.CompilerParams(vmem_limit_bytes=48 << 20),
+        compiler_params=pltpu.CompilerParams(vmem_limit_bytes=vmem << 20),
     )
 
 
@@ -61,6 +62,7 @@
         in_specs=[column],
         out_specs=[column, pl.BlockSpec((TILE, rows), lambda g: (g, 0)), line, line],
         out_shape=[shape(rows, width), shape(width, rows), shape(1, width), shape(1, width)],
+        vmem=60,
     )(expression)
 
 
@@ -192,9 +194,9 @@
 
 def scale_specs(size, column):
     return [
-        pl.BlockSpec((TILE, 1), lambda i, flags: (i, 0)),
+        pl.BlockSpec((WIDE, 1), lambda i, flags: (i, 0)),
         pl.BlockSpec((1, size), lambda i, flags: (0, column)),
-        pl.BlockSpec((TILE, 8), lambda i, flags: (i, 0)),
+        pl.BlockSpec((WIDE, 8), lambda i, flags: (i, 0)),
         pl.BlockSpec((8, size), lambda i, flags: (0, column)),
     ]
 
@@ -216,15 +218,15 @@
     arrays = [array for _, *parts in pieces for array in parts]
 
     def spec(array):
-        steps = array.shape[0] // TILE
-        return pl.BlockSpec((TILE, array.shape[1]), lambda i, flags: (i % steps, 0))
+        steps = array.shape[0] // WIDE
+        return pl.BlockSpec((WIDE, array.shape[1]), lambda i, flags: (i % steps, 0))
 
     return call(
         functools.partial(base_kernel, [(start, len(parts) == 4) for start, *parts in pieces]),
         scalars=1,
-        grid=(width // TILE,),
+        grid=(width // WIDE,),
         in_specs=[spec(array) for array in arrays] + scale_specs(width, 0),
-        out_specs=pl.BlockSpec((TILE, width), lambda i, flags: (i, 0)),
+        out_specs=pl.BlockSpec((WIDE, width), lambda i, flags: (i, 0)),
         out_shape=shape(width, width),
     )(flags, *arrays, *scales)
 
@@ -250,14 +252,14 @@
 
 def finish(flags, tiles, scales, before, start):
     width, size = before.shape[0], sum(tile[0].shape[1] for tile in tiles)
-    here = pl.BlockSpec((TILE, size), lambda i, flags: (i, start // size))
+    here = pl.BlockSpec((WIDE, size), lambda i, flags: (i, start // size))
 
     def spec(size, *kinds, column=0):
         def index(i, flags):
             used = functools.reduce(jnp.logical_or, [flags[1] == kind for kind in kinds])
             return jnp.where(used, i, 0), column
 
-        return pl.BlockSpec((TILE, size), index)
+        return pl.BlockSpec((WIDE, size), index)
 
     operands = [flags, *(array for tile in tiles for array in tile), *scales, before]
     in_specs = []
@@ -266,7 +268,7 @@
     return call(
         finish_kernel,
         scalars=1,
-        grid=(width // TILE,),
+        grid=(width // WIDE,),
         in_specs=in_specs + scale_specs(size, start // size) + [spec(size, 0, column=start // size)],
         out_specs=here,
         out_shape=shape(width, width),

time: 246 us -> 244 us (level)
  local copies, waits for them, and re-layouts: 6.86 us -> 3.28 us
  waiting for transfers between devices: 75.8 us -> 78.4 us
  transfers between devices with their start and end apart: 24 -> 24, of which waited for: 11 -> 12; matrix products, arithmetic and copies ran while one was open for 1% -> 1% of each run, Pallas kernels for 41% -> 40%
where the time goes in v6:
time: 244 us
  Pallas kernels  110 us (45%)
  waiting for transfers between devices  78.4 us (32%)
  starting transfers between devices  45.1 us (18%)
  blocking collectives  6.24 us (3%)
  local copies, waits for them, and re-layouts  3.28 us (1%)
    pallas_call x7, Pallas kernels, gram(): call(functools.partial(gram_kernel, roles, cores, turned, adds), scalars=...  90.3 us
    ppermute x19, waiting for transfers between devices, between(): lax.ppermute(part, BOTH, [(a * 4 + b, c * 4 + d) for (a, b), (c, d) in pa...  75.7 us
    ppermute x19, starting transfers between devices, between(): lax.ppermute(part, BOTH, [(a * 4 + b, c * 4 + d) for (a, b), (c, d) in pa...  29.5 us
    ppermute x5, starting transfers between devices, along(): return lax.ppermute(part, 'blocks', pairs)  15.6 us
    all_gather x1, blocking collectives, statistics(): shards = lax.all_gather(jnp.stack([mean, spread]), 'cells')  6.24 us
    pallas_call x1, Pallas kernels, centre(): call(centre_kernel, grid=(width // TILE,), in_specs=[column], out_specs=[...  5.82 us
    pallas_call x1, Pallas kernels, finish(): call(finish_kernel, scalars=1, grid=(width // WIDE,), in_specs=in_specs +...  5.43 us
    pallas_call x1, Pallas kernels, base(): call(functools.partial(base_kernel, [(start, len(parts) == 4) for start,...  4.97 us
  transfers between devices with their start and end apart: 24, of which 12 were waited for; matrix products, arithmetic and copies ran while one was open for 1% of the time, Pallas kernels for 40%

profile of v6, /device:TPU:5, one launch (start us, length us, event | category | flops | bytes accessed | tf_op | source)
XLA Modules:
  0.0 243.7 jit_solution(2013972625606021470)
XLA Ops:
  0.0 5.8 %shard_map.19 = (f32[1024,1024]{1,0:T(8,128)}, f32[1024,1024]{1,0:T(8,128)}, f32[1,1024]{1,0:T(1,128)}, f32[1,1024]{1,0:T(1,128)}) custom-call(bf16[1024,1024]{1,0:T(8,128)(2,1)} %x_ref.1), custom_call_target="tpu_custom_call" | custom-call | flops 1 | bytes 1 | tf_op jit(solution)/shard_map/pallas_call | solution.py:59
  16.0 6.2 %all-gather.1 = f32[4,2,1024]{2,1,0:T(2,128)S(1)} all-gather(f32[1,2,1024]{2,1,0:T(2,128)S(1)} %maximum_bitcast_fusion), channel_id=2, replica_groups=mesh['groups'=2,'cells'=4,'blocks'=4] {'cells'}, dimensions={0}, use_global_device_ids=true | all-gather | bytes 40960 | tf_op jit(solution)/shard_map/all_gather | solution.py:302
  22.5 28.8 %conditional.8 = (f32[1024,1024]{1,0:T(8,128)}, f32[1024,1024]{1,0:T(8,128)}) conditional(s32[]{:T(128)} %convert_element_type.9, () %tuple.76, (f32[1024,1024]{1,0:T(8,128)}, s32[2]{0:T(128)S(1)}, f32[16,1024]{1,0:T(8,128)S(1)}, f32[1040,512]{1,0:T(8,128)}, f32[1040,256]{1,0:T(8,128)}, /*index=5*/f32[1088,256]{1,0:T(8,128)S(1)}) %tuple.77), branch_computations={%region_3.4_spmd, %region_4.5_spmd} | conditional | flops 1 | bytes 16777272 | solution.py:166
  22.7 7.3 %collective-permute-done.refs_1_.refs_3_ = f32[1024,1024]{1,0:T(8,128)} collective-permute-done((f32[1024,1024]{1,0:T(8,128)}, f32[1024,1024]{1,0:T(8,128)}, u32[]{:S(2)}, u32[]{:S(2)}) %collective-permute-start) | collective-permute-done | bytes 4194336 | tf_op jit(solution)/shard_map/cond/branch_1_fun/own_other/ppermute | solution.py:325
  30.1 21.3 %branch_1_fun.9 = f32[1024,1024]{1,0:T(8,128)} custom-call(s32[2]{0:T(128)S(1)} %get-tuple-element.234.role_ref, f32[1024,1024]{1,0:T(8,128)} %get-tuple-element.235.refs_0_.refs_2_, f32[1024,1024]{1,0:T(8,128)} %collective-permute-done.refs_1_.refs_3_, f32[1024,1024]{1,0:T(8,128)} %get-tuple-element.235.refs_0_.refs_2_, ...), custom_call_target="tpu_custom_call" | custom-call | flops 1 | bytes 1 | tf_op jit(solution)/shard_map/cond/branch_1_fun/pallas_call | solution.py:149
  57.1 47.0 %collective-permute-done.14.refs_3_ = f32[16,1024]{1,0:T(8,128)S(1)} collective-permute-done((f32[16,1024]{1,0:T(8,128)S(1)}, f32[16,1024]{1,0:T(8,128)S(1)}, u32[]{:S(2)}, u32[]{:S(2)}) %collective-permute-start.14) | collective-permute-done | bytes 65568 | tf_op jit(solution)/shard_map/moments/ppermute | solution.py:325
  107.6 26.0 %conditional.9 = (f32[1024,1024]{1,0:T(8,128)}, f32[1024,1024]{1,0:T(8,128)}) conditional(s32[]{:T(128)} %convert_element_type.9, () %tuple.78, (f32[1024,1024]{1,0:T(8,128)}, f32[1024,1024]{1,0:T(8,128)}, s32[2]{0:T(128)S(1)}, f32[1024,1024]{1,0:T(8,128)S(1)}, f32[1024,1024]{1,0:T(8,128)}, /*index=5*/f32[1024,1024]{1,0:T(8,128)}) %tuple.121), branch_computations={%region_5.6_spmd, %region_6.7_spmd} | conditional | flops 2 | bytes 33554528 | solution.py:166
  108.8 11.6 %branch_1_fun.10.refs_3_ = f32[1024,1024]{1,0:T(8,128)S(1)} custom-call(s32[2]{0:T(128)S(1)} %get-tuple-element.240.role_ref, f32[1024,1024]{1,0:T(8,128)S(1)} %get-tuple-element.257.refs_0_, f32[1024,1024]{1,0:T(8,128)} %get-tuple-element.254.refs_1_, f32[1024,1024]{1,0:T(8,128)} %get-tuple-element.256.refs_2_, f32[1024,1024]{1,0:T(8,128)} %get-tuple-element.258.refs_3_), custom_call_target="tpu_custom_call" | custom-call | flops 1 | bytes 1 | tf_op jit(solution)/shard_map/cond/branch_1_fun/pallas_call | solution.py:149
  121.9 11.7 %branch_1_fun.11 = f32[1024,1024]{1,0:T(8,128)} custom-call(s32[2]{0:T(128)S(1)} %get-tuple-element.240.role_ref, f32[1024,1024]{1,0:T(8,128)} %get-tuple-element.252.refs_0_, f32[1024,1024]{1,0:T(8,128)} %collective-permute-done.1.refs_1_, f32[1024,1024]{1,0:T(8,128)S(1)} %collective-permute-done.2.refs_2_, f32[1024,1024]{1,0:T(8,128)S(1)} %branch_1_fun.10.refs_3_), custom_call_target="tpu_custom_call" | custom-call | flops 1 | bytes 1 | tf_op jit(solution)/shard_map/cond/branch_1_fun/pallas_call | solution.py:149
  135.0 5.1 %collective-permute-start.15 = (f32[1040,256]{1,0:T(8,128)}, f32[1040,256]{1,0:T(8,128)}, u32[]{:S(2)}, u32[]{:S(2)}) collective-permute-start(f32[1040,256]{1,0:T(8,128)} %shard_map.21), channel_id=1, source_target_pairs={{0,2},{3,1},{4,6},{7,5},{8,10},{11,9},{12,14},{15,13},{16,18},{19,... | collective-permute-start | bytes 3194888 | tf_op jit(solution)/shard_map/far_block/ppermute | solution.py:329
  142.6 12.7 %shard_map.25 = f32[528,1024]{1,0:T(8,128)S(1)} custom-call(s32[2]{0:T(128)S(1)} %pad_add_fusion.2.role_ref, f32[1024,1024]{1,0:T(8,128)S(1)} %copy-done.2, f32[1024,1024]{1,0:T(8,128)} %get-tuple-element.372.refs_1_, f32[1024,1024]{1,0:T(8,128)} %collective-permute-done.12.refs_1_.refs_2_, f32[1024,1024]{1,0:T(8,128)} %get-tuple-element.374.refs_3_, ...), custom_call_target="tpu_custom_call" | custom-call | flops 1 | bytes 1 | tf_op jit(solution)/shard_map/pallas_call | solution.py:149
  159.2 20.3 %conditional.10 = (f32[1040,512]{1,0:T(8,128)}, f32[528,1024]{1,0:T(8,128)}) conditional(s32[]{:T(128)} %convert_element_type.9, () %tuple.80, (f32[1040,512]{1,0:T(8,128)}, s32[2]{0:T(128)S(1)}, f32[1024,1024]{1,0:T(8,128)S(1)}, f32[1024,1024]{1,0:T(8,128)}, f32[1024,1024]{1,0:T(8,128)}, /*index=5*/f32[1024,1024]{1,0:T(8,128)}, ...), branch_computations={%region_7.8_spmd, %region_8.9_spmd} | conditional | flops 2 | bytes 21495906 | solution.py:166
  166.5 13.0 %branch_1_fun.12 = f32[1040,512]{1,0:T(8,128)} custom-call(s32[2]{0:T(128)S(1)} %get-tuple-element.259.role_ref, f32[1024,1024]{1,0:T(8,128)S(1)} %get-tuple-element.260.refs_0_, f32[1024,1024]{1,0:T(8,128)} %get-tuple-element.261.refs_1_, f32[1024,1024]{1,0:T(8,128)} %get-tuple-element.262.refs_2_, f32[1024,1024]{1,0:T(8,128)} %get-tuple-element.263.refs_3_, ...), custom_call_target="tpu_custom_call" | custom-call | flops 1 | bytes 1 | tf_op jit(solution)/shard_map/cond/branch_1_fun/pallas_call | solution.py:149
  180.8 13.0 %conditional.11 = (f32[1040,256]{1,0:T(8,128)}) conditional(s32[]{:T(128)} %convert_element_type.9, () %tuple.75, (f32[1040,256]{1,0:T(8,128)}, s32[2]{0:T(128)S(1)}, f32[1024,1024]{1,0:T(8,128)}, f32[1024,1024]{1,0:T(8,128)}, f32[1024,1024]{1,0:T(8,128)}, /*index=5*/f32[1024,1024]{1,0:T(8,128)}, f32[1040,512]{1,0:T(8,128)}) %tuple.82), branch_computations={%region_9.10_spmd, %region_10.11_spmd} | conditional | flops 1 | bytes 4259889 | solution.py:166
  183.8 10.0 %branch_1_fun.14 = f32[1040,256]{1,0:T(8,128)} custom-call(s32[2]{0:T(128)S(1)} %get-tuple-element.266.role_ref, f32[1024,1024]{1,0:T(8,128)} %get-tuple-element.267.refs_0_, f32[1024,1024]{1,0:T(8,128)} %get-tuple-element.268.refs_1_, f32[1024,1024]{1,0:T(8,128)} %get-tuple-element.269.refs_2_, f32[1024,1024]{1,0:T(8,128)} %get-tuple-element.270.refs_3_, ...), custom_call_target="tpu_custom_call" | custom-call | flops 1 | bytes 1 | tf_op jit(solution)/shard_map/cond/branch_1_fun/pallas_call | solution.py:149
  197.8 14.4 %conditional.12 = (f32[1040,256]{1,0:T(8,128)}) conditional(s32[]{:T(128)} %convert_element_type.9, () %tuple.83, (f32[1088,256]{1,0:T(8,128)}, s32[2]{0:T(128)S(1)}, f32[1024,1024]{1,0:T(8,128)}, f32[1024,1024]{1,0:T(8,128)}, f32[1024,1024]{1,0:T(8,128)}, /*index=5*/f32[1024,1024]{1,0:T(8,128)}, f32[1040,256]{1,0:T(8,128)}) %tuple.84), branch_computations={%region_11.12_spmd, %region_12.13_spmd} | conditional | flops 1 | bytes 4456497 | solution.py:166
  202.3 10.0 %branch_1_fun.15 = f32[1040,256]{1,0:T(8,128)} custom-call(s32[2]{0:T(128)S(1)} %get-tuple-element.273.role_ref, f32[1024,1024]{1,0:T(8,128)} %get-tuple-element.274.refs_0_, f32[1024,1024]{1,0:T(8,128)} %get-tuple-element.275.refs_1_, f32[1024,1024]{1,0:T(8,128)} %get-tuple-element.276.refs_2_, f32[1024,1024]{1,0:T(8,128)} %get-tuple-element.277.refs_3_, ...), custom_call_target="tpu_custom_call" | custom-call | flops 1 | bytes 1 | tf_op jit(solution)/shard_map/cond/branch_1_fun/pallas_call | solution.py:149
  213.8 17.1 %conditional.13 = (f32[1024,1024]{1,0:T(8,128)}) conditional(s32[]{:T(128)} %convert_element_type.9, () %tuple.85, (s32[]{:T(128)}, f32[528,1024]{1,0:T(8,128)}, f32[1024,1024]{1,0:T(8,128)}, f32[1040,512]{1,0:T(8,128)}, s32[2]{0:T(128)S(1)}, /*index=5*/f32[1024,1024]{1,0:T(8,128)}, f32[1024,1024]{1,0:T(8,128)}, f32[1024,1]{0,1:T(1,128)S(1)}, ...), branch_computations={%region_13.14_spmd, %region_14.22_spmd} | conditional | flops 2 | bytes 34021944 | solution.py:166
  213.8 3.9 %collective-permute-start.8 = (f32[1024,1024]{1,0:T(8,128)}, f32[1024,1024]{1,0:T(8,128)}, u32[]{:S(2)}, u32[]{:S(2)}) collective-permute-start(f32[1024,1024]{1,0:T(8,128)} %get-tuple-element.345), channel_id=1, source_target_pairs={{12,8},{3,7},{28,24},{19,23}} | collective-permute-start | bytes 12582920 | tf_op jit(solution)/shard_map/cond/branch_1_fun/mid_fold/ppermute | solution.py:325
  219.4 5.9 %collective-permute-done.9 = f32[1040,512]{1,0:T(8,128)} collective-permute-done((f32[1040,512]{1,0:T(8,128)}, f32[1040,512]{1,0:T(8,128)}, u32[]{:S(2)}, u32[]{:S(2)}) %collective-permute-start.9) | collective-permute-done | bytes 2129952 | tf_op jit(solution)/shard_map/cond/branch_1_fun/far_fold/ppermute | solution.py:325
  225.9 5.0 %conditional = (f32[1024,1024]{1,0:T(8,128)}) conditional(s32[]{:T(128)} %clamp.2, (s32[2]{0:T(128)S(1)}, f32[1024,1024]{1,0:T(8,128)}, f32[1024,1024]{1,0:T(8,128)}, f32[1024,1]{1,0:T(8,128)S(1)}, f32[1,1024]{1,0:T(1,128)S(1)}, /*index=5*/f32[1024,8]{1,0:T(8,128)S(1)}, f32[8,1024]{1,0:T(8,128)S(1)}) %tuple.53, ...), branch_computations={%region_15.15_spmd, %region_16.16_spmd, %region_17.17_spmd, %regio... | conditional | flops 1 | bytes 9 | solution.py:419
  225.9 5.0 %branch_6_fun.1 = f32[1024,1024]{1,0:T(8,128)} custom-call(s32[2]{0:T(128)S(1)} %get-tuple-element.326.flags, f32[1040,512]{1,0:T(8,128)} %get-tuple-element.327.refs_0_, f32[1040,512]{1,0:T(8,128)} %get-tuple-element.328.refs_1_, f32[1024,1]{1,0:T(8,128)S(1)} %get-tuple-element.329.refs_2_, f32[1,1024]{1,0:T(1,128)S(1)} %get-tuple-element.330.refs_3_, ...), custom_call_target="tpu_custom_call" | custom-call | flops 1 | bytes 1 | tf_op jit(solution)/shard_map/cond/branch_1_fun/cond/branch_6_fun/pallas_call | solution.py:224
  231.2 12.5 %conditional.14 = (f32[1024,1024]{1,0:T(8,128)}) conditional(s32[]{:T(128)} %convert_element_type.9, () %tuple.74, (f32[1040,256]{1,0:T(8,128)}, f32[1040,256]{1,0:T(8,128)}, s32[2]{0:T(128)S(1)}, f32[1040,256]{1,0:T(8,128)}, f32[1040,256]{1,0:T(8,128)}, /*index=5*/f32[1024,1]{0,1:T(1,128)S(1)}, f32[1,1024]{1,0:T(1,128)S(1)}, ...), branch_computations={%region_22.23_spmd, %region_23.24_spmd} | conditional | flops 1 | bytes 8593497 | solution.py:166
  238.3 5.4 %branch_1_fun.17 = f32[1024,1024]{1,0:T(8,128)} custom-call(s32[2]{0:T(128)S(1)} %get-tuple-element.348.flags, f32[1040,256]{1,0:T(8,128)} %get-tuple-element.349.refs_0_, f32[1040,256]{1,0:T(8,128)} %get-tuple-element.350.refs_1_, f32[1040,256]{1,0:T(8,128)S(1)} %collective-permute-done.10.refs_2_, ...), custom_call_target="tpu_custom_call", output_to_operand_aliasing={{}: (11, {})} | custom-call | flops 1 | bytes 1 | tf_op jit(solution)/shard_map/cond/branch_1_fun/pallas_call | solution.py:268
  (83 shorter events, 61.4 us)
Async XLA Ops:
  5.8 98.3 %collective-permute-start.13 = (f32[1024,1024]{1,0:T(8,128)}, f32[1024,1024]{1,0:T(8,128)}, u32[]{:S(2)}, u32[]{:S(2)}) collective-permute-start(f32[1024,1024]{1,0:T(8,128)} %get-tuple-element.368.from_ref), channel_id=1, source_target_pairs={{1,2},{2,1},{5,6},{6,5},{9,10},{10,9},{13,14},{14,13},{17,18},{18,... | collective-permute-start | bytes 12582920 | tf_op jit(solution)/shard_map/mid_block/ppermute | solution.py:329
  8.5 95.7 %collective-permute-start.12 = (f32[1024,1024]{1,0:T(8,128)}, f32[1024,1024]{1,0:T(8,128)}, u32[]{:S(2)}, u32[]{:S(2)}) collective-permute-start(f32[1024,1024]{1,0:T(8,128)} %get-tuple-element.369.refs_0_), channel_id=1, source_target_pairs={{0,1},{1,0},{2,3},{3,2},{4,5},{5,4},{6,7},{7,6},{8,9},{9,8},{10,11... | collective-permute-start | bytes 12582920 | tf_op jit(solution)/shard_map/pair_block/ppermute | solution.py:329
  22.5 7.5 %collective-permute-start = (f32[1024,1024]{1,0:T(8,128)}, f32[1024,1024]{1,0:T(8,128)}, u32[]{:S(2)}, u32[]{:S(2)}) collective-permute-start(f32[1024,1024]{1,0:T(8,128)} %get-tuple-element.235.refs_0_.refs_2_), channel_id=1, source_target_pairs={{0,4},{1,5},{2,6},{3,7},{4,0},{5,1},{6,2},{7,3},{8,12},{9,13},{10,... | collective-permute-start | bytes 12582920 | tf_op jit(solution)/shard_map/cond/branch_1_fun/own_other/ppermute | solution.py:325
  51.3 91.3 %collective-permute-start.17 = (f32[1024,1024]{1,0:T(8,128)}, f32[1024,1024]{1,0:T(8,128)}, u32[]{:S(2)}, u32[]{:S(2)}) collective-permute-start(f32[1024,1024]{1,0:T(8,128)} %get-tuple-element.373), channel_id=1, source_target_pairs={{8,0},{13,5},{2,10},{7,15},{24,16},{29,21},{18,26},{23,31}} | collective-permute-start | bytes 12582920 | tf_op jit(solution)/shard_map/own_lane/ppermute | solution.py:325
  54.2 50.0 %collective-permute-start.14 = (f32[16,1024]{1,0:T(8,128)S(1)}, f32[16,1024]{1,0:T(8,128)S(1)}, u32[]{:S(2)}, u32[]{:S(2)}) collective-permute-start(f32[16,1024]{1,0:T(8,128)S(1)} %maximum_maximum_fusion), channel_id=1, source_target_pairs={{1,4},{2,8},{3,12},{4,1},{6,9},{7,13},{8,2},{9,6},{11,14},{12,3},{... | collective-permute-start | bytes 196616 | tf_op jit(solution)/shard_map/moments/ppermute | solution.py:325
  104.2 55.0 %collective-permute-start.16 = (f32[1040,512]{1,0:T(8,128)}, f32[1040,512]{1,0:T(8,128)}, u32[]{:S(2)}, u32[]{:S(2)}) collective-permute-start(f32[1040,512]{1,0:T(8,128)} %shard_map.24), channel_id=1, source_target_pairs={{0,2},{3,1},{4,6},{7,5},{8,10},{11,9},{12,14},{15,13},{16,18},{19,... | collective-permute-start | bytes 6389768 | tf_op jit(solution)/shard_map/far_block/ppermute | solution.py:329
  107.6 14.3 %collective-permute-start.1 = (f32[1024,1024]{1,0:T(8,128)}, f32[1024,1024]{1,0:T(8,128)}, u32[]{:S(2)}, u32[]{:S(2)}) collective-permute-start(f32[1024,1024]{1,0:T(8,128)} %get-tuple-element.254.refs_1_), channel_id=1, source_target_pairs={{0,4},{1,5},{2,6},{3,7},{4,0},{5,1},{6,2},{7,3},{8,12},{9,13},{10,... | collective-permute-start | bytes 12582920 | tf_op jit(solution)/shard_map/cond/branch_1_fun/pair_other/ppermute | solution.py:325
  108.8 13.1 %collective-permute-start.2 = (f32[1024,1024]{1,0:T(8,128)}, f32[1024,1024]{1,0:T(8,128)S(1)}, u32[]{:S(2)}, u32[]{:S(2)}) collective-permute-start(f32[1024,1024]{1,0:T(8,128)} %get-tuple-element.256.refs_2_), channel_id=1, source_target_pairs={{0,4},{1,5},{2,6},{3,7},{4,0},{5,1},{6,2},{7,3},{8,12},{9,13},{10,... | collective-permute-start | bytes 12582920 | tf_op jit(solution)/shard_map/cond/branch_1_fun/mid_other/ppermute | solution.py:325
  133.6 80.1 %collective-permute-start.22 = (f32[1024,1024]{1,0:T(8,128)}, f32[1024,1024]{1,0:T(8,128)}, u32[]{:S(2)}, u32[]{:S(2)}) collective-permute-start(f32[1024,1024]{1,0:T(8,128)} %get-tuple-element.375.refs_4_), channel_id=1, source_target_pairs={{1,9},{14,6},{5,8},{10,7},{13,12},{2,3},{17,25},{30,22},{21,24},{2... | collective-permute-start | bytes 12582920 | tf_op jit(solution)/shard_map/mid_sum/ppermute | solution.py:325
  135.0 45.8 %collective-permute-start.15 = (f32[1040,256]{1,0:T(8,128)}, f32[1040,256]{1,0:T(8,128)}, u32[]{:S(2)}, u32[]{:S(2)}) collective-permute-start(f32[1040,256]{1,0:T(8,128)} %shard_map.21), channel_id=1, source_target_pairs={{0,2},{3,1},{4,6},{7,5},{8,10},{11,9},{12,14},{15,13},{16,18},{19,... | collective-permute-start | bytes 3194888 | tf_op jit(solution)/shard_map/far_block/ppermute | solution.py:329
  140.1 57.7 %collective-permute-start.19 = (f32[1088,256]{1,0:T(8,128)S(1)}, f32[1088,256]{1,0:T(8,128)}, u32[]{:S(2)}, u32[]{:S(2)}) collective-permute-start(f32[1088,256]{1,0:T(8,128)S(1)} %shard_map.26), channel_id=1, source_target_pairs={{0,2},{3,1},{4,6},{7,5},{8,10},{11,9},{12,14},{15,13},{16,18},{19,... | collective-permute-start | bytes 3342344 | tf_op jit(solution)/shard_map/far_block/ppermute | solution.py:329
  155.4 58.3 %collective-permute-start.21 = (f32[528,1024]{1,0:T(8,128)S(1)}, f32[528,1024]{1,0:T(8,128)}, u32[]{:S(2)}, u32[]{:S(2)}) collective-permute-start(f32[528,1024]{1,0:T(8,128)S(1)} %shard_map.25), channel_id=1, source_target_pairs={{12,4},{8,0},{9,1},{13,5},{6,14},{2,10},{3,11},{7,15},{28,20},{24,... | collective-permute-start | bytes 6488072 | tf_op jit(solution)/shard_map/pair_lane/ppermute | solution.py:325
  159.2 6.9 %collective-permute-start.3 = (f32[1040,512]{1,0:T(8,128)}, f32[1040,512]{1,0:T(8,128)S(1)}, u32[]{:S(2)}, u32[]{:S(2)}) collective-permute-start(f32[1040,512]{1,0:T(8,128)} %get-tuple-element.264.refs_4_), channel_id=1, source_target_pairs={{0,4},{1,5},{2,6},{3,7},{4,0},{5,1},{6,2},{7,3},{8,12},{9,13},{10,... | collective-permute-start | bytes 6389768 | tf_op jit(solution)/shard_map/cond/branch_1_fun/far_other/ppermute | solution.py:325
  166.1 13.4 %collective-permute-start.4 = (f32[528,1024]{1,0:T(8,128)S(1)}, f32[528,1024]{1,0:T(8,128)}, u32[]{:S(2)}, u32[]{:S(2)}) collective-permute-start(f32[528,1024]{1,0:T(8,128)S(1)} %branch_1_fun.13), channel_id=1, source_target_pairs={{0,4},{1,5},{2,6},{3,7},{4,0},{5,1},{6,2},{7,3},{8,12},{9,13},{10,... | collective-permute-start | bytes 6488072 | tf_op jit(solution)/shard_map/cond/branch_1_fun/pair_fold/ppermute | solution.py:325
  179.5 34.3 %collective-permute-start.23 = (f32[1040,512]{1,0:T(8,128)}, f32[1040,512]{1,0:T(8,128)}, u32[]{:S(2)}, u32[]{:S(2)}) collective-permute-start(f32[1040,512]{1,0:T(8,128)} %get-tuple-element.376), channel_id=1, source_target_pairs={{5,13},{10,2},{1,12},{14,3},{9,8},{6,7},{21,29},{26,18},{17,28},{3... | collective-permute-start | bytes 6389768 | tf_op jit(solution)/shard_map/far_sum/ppermute | solution.py:325
  180.8 3.0 %collective-permute-start.5 = (f32[1040,256]{1,0:T(8,128)}, f32[1040,256]{1,0:T(8,128)S(1)}, u32[]{:S(2)}, u32[]{:S(2)}) collective-permute-start(f32[1040,256]{1,0:T(8,128)} %get-tuple-element.271.refs_4_), channel_id=1, source_target_pairs={{0,4},{1,5},{2,6},{3,7},{4,0},{5,1},{6,2},{7,3},{8,12},{9,13},{10,... | collective-permute-start | bytes 3194888 | tf_op jit(solution)/shard_map/cond/branch_1_fun/far_other/ppermute | solution.py:325
  193.8 37.4 %collective-permute-start.18 = (f32[1040,256]{1,0:T(8,128)}, f32[1040,256]{1,0:T(8,128)}, u32[]{:S(2)}, u32[]{:S(2)}) collective-permute-start(f32[1040,256]{1,0:T(8,128)} %get-tuple-element.476), channel_id=1, source_target_pairs={{5,13},{10,2},{1,12},{14,3},{9,8},{6,7},{21,29},{26,18},{17,28},{3... | collective-permute-start | bytes 3194888 | tf_op jit(solution)/shard_map/far_sum/ppermute | solution.py:325
  197.8 4.4 %collective-permute-start.6 = (f32[1088,256]{1,0:T(8,128)}, f32[1088,256]{1,0:T(8,128)S(1)}, u32[]{:S(2)}, u32[]{:S(2)}) collective-permute-start(f32[1088,256]{1,0:T(8,128)} %get-tuple-element.278.refs_4_), channel_id=1, source_target_pairs={{0,4},{1,5},{2,6},{3,7},{4,0},{5,1},{6,2},{7,3},{8,12},{9,13},{10,... | collective-permute-start | bytes 3342344 | tf_op jit(solution)/shard_map/cond/branch_1_fun/far_other/ppermute | solution.py:325
  212.2 19.0 %collective-permute-start.20 = (f32[1040,256]{1,0:T(8,128)}, f32[1040,256]{1,0:T(8,128)}, u32[]{:S(2)}, u32[]{:S(2)}) collective-permute-start(f32[1040,256]{1,0:T(8,128)} %get-tuple-element.477), channel_id=1, source_target_pairs={{5,13},{10,2},{1,12},{14,3},{9,8},{6,7},{21,29},{26,18},{17,28},{3... | collective-permute-start | bytes 3194888 | tf_op jit(solution)/shard_map/far_sum/ppermute | solution.py:325
  213.8 12.2 %collective-permute-start.8 = (f32[1024,1024]{1,0:T(8,128)}, f32[1024,1024]{1,0:T(8,128)}, u32[]{:S(2)}, u32[]{:S(2)}) collective-permute-start(f32[1024,1024]{1,0:T(8,128)} %get-tuple-element.345), channel_id=1, source_target_pairs={{12,8},{3,7},{28,24},{19,23}} | collective-permute-start | bytes 12582920 | tf_op jit(solution)/shard_map/cond/branch_1_fun/mid_fold/ppermute | solution.py:325
  217.7 8.2 %collective-permute-start.7 = (f32[528,1024]{1,0:T(8,128)}, f32[528,1024]{1,0:T(8,128)}, u32[]{:S(2)}, u32[]{:S(2)}) collective-permute-start(f32[528,1024]{1,0:T(8,128)} %get-tuple-element.342), channel_id=1, source_target_pairs={{0,4},{1,5},{2,6},{3,7},{4,0},{5,1},{6,2},{7,3},{8,12},{9,13},{10,... | collective-permute-start | bytes 6488072 | tf_op jit(solution)/shard_map/cond/branch_1_fun/pair_fold/ppermute | solution.py:325
  217.7 7.6 %collective-permute-start.9 = (f32[1040,512]{1,0:T(8,128)}, f32[1040,512]{1,0:T(8,128)}, u32[]{:S(2)}, u32[]{:S(2)}) collective-permute-start(f32[1040,512]{1,0:T(8,128)} %get-tuple-element.347), channel_id=1, source_target_pairs={{8,12},{7,3},{24,28},{23,19}} | collective-permute-start | bytes 6389768 | tf_op jit(solution)/shard_map/cond/branch_1_fun/far_fold/ppermute | solution.py:325
  231.2 5.6 %collective-permute-start.11 = (f32[1040,256]{1,0:T(8,128)}, f32[1040,256]{1,0:T(8,128)S(1)}, u32[]{:S(2)}, u32[]{:S(2)}) collective-permute-start(f32[1040,256]{1,0:T(8,128)} %get-tuple-element.352.refs_4_), channel_id=1, source_target_pairs={{8,12},{7,3},{24,28},{23,19}} | collective-permute-start | bytes 3194888 | tf_op jit(solution)/shard_map/cond/branch_1_fun/far_fold/ppermute | solution.py:325
  232.5 5.8 %collective-permute-start.10 = (f32[1040,256]{1,0:T(8,128)}, f32[1040,256]{1,0:T(8,128)S(1)}, u32[]{:S(2)}, u32[]{:S(2)}) collective-permute-start(f32[1040,256]{1,0:T(8,128)} %get-tuple-element.350.refs_1_), channel_id=1, source_target_pairs={{8,12},{7,3},{24,28},{23,19}} | collective-permute-start | bytes 3194888 | tf_op jit(solution)/shard_map/cond/branch_1_fun/far_fold/ppermute | solution.py:325
  (5 other events, 64.5 us)

commit v7 on v6

--- a/solution.py
+++ b/solution.py
@@ -130,7 +130,7 @@
         out_ref[:, span] = before_ref[:, span] + total if adds else total
 
 
-def gram(role, lefts, rights, turned, earlier, rows=None, pad=0, before=None):
+def gram(role, lefts, rights, turned, earlier, rows=None, pad=0, before=None, vmem=40):
     width, cells = lefts[0].shape
     cores, adds = len(rights), before is not None
     roles, rows = len(lefts) // cores, rows or width
@@ -157,6 +157,7 @@
         out_specs=out,
         out_shape=shape(rows + pad, size),
         scratch=[pltpu.VMEM((TILE, cores * cells), bf16)] * 2 + [pltpu.VMEM(right_shape, bf16)] * 2,
+        vmem=vmem,
     )(role, *lefts, *rights, *([before] if adds else []), *earlier)
 
 
@@ -348,7 +349,7 @@
     mid_got = along(centred, [(1, 2), (2, 1)], "mid_block")
     pair_got = along(turned, [(0, 1), (1, 0), (2, 3), (3, 2)], "pair_block")
     far = pieces(width, FAR_WIDTHS)
-    far_parts = [columns(centred, *piece, pad) for piece, pad in zip(far, (PAD, PAD, 4 * PAD))]
+    far_parts = [columns(centred, *piece, pad) for piece, pad in zip(far, (PAD, PAD, 2 * PAD))]
     away, variance = statistics(rows, mean[0], spread[0])
     mine = jnp.concatenate([away, variance[None, :], jnp.zeros((11, width), f32)])
 
@@ -357,7 +358,7 @@
         return gram(mid_role, own, own, True, earlier), own[1]
 
     def in_turn(role, own, pair, got, got_other, earlier, pad=0):
-        mine = gram(role, (own[0], pair[0]), (got,), False, earlier)
+        mine = gram(role, (own[0], pair[0]), (got,), False, earlier, vmem=60)
         return gram(role, (own[1], pair[1]), (got_other,), False, (), pad=pad, before=mine)
 
     def mid_work(own, pair_got, mid_got, earlier):

time: 244 us -> 247 us (1.012)
  Pallas kernels: 110 us -> 113 us
    ppermute x5, waiting for transfers between devices: 2.73 us -> 0.01 us  [along(): return lax.ppermute(part, 'blocks', pairs)]
    pallas_call x7, Pallas kernels: 90.3 us -> 93 us  [gram(): call(functools.partial(gram_kernel, roles, cores, turned, adds), scalars=...]
  transfers between devices with their start and end apart: 24 -> 24, of which waited for: 12 -> 11; matrix products, arithmetic and copies ran while one was open for 1% -> 1% of each run, Pallas kernels for 40% -> 41%
where the time goes in v7:
time: 247 us; the launch traced here: 246 us
  Pallas kernels  113 us (46%)
  waiting for transfers between devices  78.1 us (32%)
  starting transfers between devices  43.3 us (18%)
  blocking collectives  6.24 us (3%)
  local copies, waits for them, and re-layouts  5.46 us (2%)
    pallas_call x7, Pallas kernels, gram(): call(functools.partial(gram_kernel, roles, cores, turned, adds), scalars=...  93 us
    ppermute x19, waiting for transfers between devices, between(): lax.ppermute(part, BOTH, [(a * 4 + b, c * 4 + d) for (a, b), (c, d) in pa...  78 us
    ppermute x19, starting transfers between devices, between(): lax.ppermute(part, BOTH, [(a * 4 + b, c * 4 + d) for (a, b), (c, d) in pa...  27.6 us
    ppermute x5, starting transfers between devices, along(): return lax.ppermute(part, 'blocks', pairs)  15.7 us
    all_gather x1, blocking collectives, statistics(): shards = lax.all_gather(jnp.stack([mean, spread]), 'cells')  6.24 us
    pallas_call x1, Pallas kernels, centre(): call(centre_kernel, grid=(width // TILE,), in_specs=[column], out_specs=[...  5.82 us
    pallas_call x1, Pallas kernels, finish(): call(finish_kernel, scalars=1, grid=(width // WIDE,), in_specs=in_specs +...  5.43 us
    pallas_call x1, Pallas kernels, base(): call(functools.partial(base_kernel, [(start, len(parts) == 4) for start,...  4.97 us
  transfers between devices with their start and end apart: 24, of which 11 were waited for; matrix products, arithmetic and copies ran while one was open for 1% of the time, Pallas kernels for 41%

profile of v7, /device:TPU:5, one launch (start us, length us, event | category | flops | bytes accessed | tf_op | source)
XLA Modules:
  0.0 246.5 jit_solution(2067835089117525071)
XLA Ops:
  0.0 5.8 %shard_map.19 = (f32[1024,1024]{1,0:T(8,128)}, f32[1024,1024]{1,0:T(8,128)}, f32[1,1024]{1,0:T(1,128)}, f32[1,1024]{1,0:T(1,128)}) custom-call(bf16[1024,1024]{1,0:T(8,128)(2,1)} %x_ref.1), custom_call_target="tpu_custom_call" | custom-call | flops 1 | bytes 1 | tf_op jit(solution)/shard_map/pallas_call | solution.py:59
  16.0 6.2 %all-gather.1 = f32[4,2,1024]{2,1,0:T(2,128)S(1)} all-gather(f32[1,2,1024]{2,1,0:T(2,128)S(1)} %maximum_bitcast_fusion), channel_id=2, replica_groups=mesh['groups'=2,'cells'=4,'blocks'=4] {'cells'}, dimensions={0}, use_global_device_ids=true | all-gather | bytes 40960 | tf_op jit(solution)/shard_map/all_gather | solution.py:303
  22.5 28.8 %conditional.8 = (f32[1024,1024]{1,0:T(8,128)}, f32[1024,1024]{1,0:T(8,128)}) conditional(s32[]{:T(128)} %convert_element_type.9, () %tuple.76, (f32[1024,1024]{1,0:T(8,128)}, s32[2]{0:T(128)S(1)}, f32[16,1024]{1,0:T(8,128)S(1)}, f32[1040,512]{1,0:T(8,128)}, f32[1040,256]{1,0:T(8,128)}, /*index=5*/f32[1056,256]{1,0:T(8,128)S(1)}) %tuple.77), branch_computations={%region_3.4_spmd, %region_4.5_spmd} | conditional | flops 1 | bytes 16777272 | solution.py:167
  22.7 7.3 %collective-permute-done.refs_1_.refs_3_ = f32[1024,1024]{1,0:T(8,128)} collective-permute-done((f32[1024,1024]{1,0:T(8,128)}, f32[1024,1024]{1,0:T(8,128)}, u32[]{:S(2)}, u32[]{:S(2)}) %collective-permute-start) | collective-permute-done | bytes 4194336 | tf_op jit(solution)/shard_map/cond/branch_1_fun/own_other/ppermute | solution.py:326
  30.1 21.3 %branch_1_fun.9 = f32[1024,1024]{1,0:T(8,128)} custom-call(s32[2]{0:T(128)S(1)} %get-tuple-element.234.role_ref, f32[1024,1024]{1,0:T(8,128)} %get-tuple-element.235.refs_0_.refs_2_, f32[1024,1024]{1,0:T(8,128)} %collective-permute-done.refs_1_.refs_3_, f32[1024,1024]{1,0:T(8,128)} %get-tuple-element.235.refs_0_.refs_2_, ...), custom_call_target="tpu_custom_call" | custom-call | flops 1 | bytes 1 | tf_op jit(solution)/shard_map/cond/branch_1_fun/pallas_call | solution.py:149
  57.0 47.2 %collective-permute-done.14.refs_3_ = f32[16,1024]{1,0:T(8,128)S(1)} collective-permute-done((f32[16,1024]{1,0:T(8,128)S(1)}, f32[16,1024]{1,0:T(8,128)S(1)}, u32[]{:S(2)}, u32[]{:S(2)}) %collective-permute-start.14) | collective-permute-done | bytes 65568 | tf_op jit(solution)/shard_map/moments/ppermute | solution.py:326
  107.6 29.6 %conditional.9 = (f32[1024,1024]{1,0:T(8,128)}, f32[1024,1024]{1,0:T(8,128)}) conditional(s32[]{:T(128)} %convert_element_type.9, () %tuple.78, (f32[1024,1024]{1,0:T(8,128)}, f32[1024,1024]{1,0:T(8,128)}, s32[2]{0:T(128)S(1)}, f32[1024,1024]{1,0:T(8,128)}, f32[1024,1024]{1,0:T(8,128)}, /*index=5*/f32[1024,1024]{1,0:T(8,128)}) %tuple.79), branch_computations={%region_5.6_spmd, %region_6.7_spmd} | conditional | flops 2 | bytes 50331772 | solution.py:167
  108.8 13.0 %branch_1_fun.10.refs_3_ = f32[1024,1024]{1,0:T(8,128)} custom-call(s32[2]{0:T(128)S(1)} %get-tuple-element.240.role_ref, f32[1024,1024]{1,0:T(8,128)} %get-tuple-element.257.refs_0_, f32[1024,1024]{1,0:T(8,128)} %get-tuple-element.254.refs_1_, f32[1024,1024]{1,0:T(8,128)} %get-tuple-element.256.refs_2_, f32[1024,1024]{1,0:T(8,128)} %get-tuple-element.258.refs_3_), custom_call_target="tpu_custom_call" | custom-call | flops 1 | bytes 1 | tf_op jit(solution)/shard_map/cond/branch_1_fun/pallas_call | solution.py:149
  124.1 13.1 %branch_1_fun.11 = f32[1024,1024]{1,0:T(8,128)} custom-call(s32[2]{0:T(128)S(1)} %get-tuple-element.240.role_ref, f32[1024,1024]{1,0:T(8,128)} %get-tuple-element.252.refs_0_, f32[1024,1024]{1,0:T(8,128)} %collective-permute-done.1.refs_1_, f32[1024,1024]{1,0:T(8,128)} %collective-permute-done.2.refs_2_, f32[1024,1024]{1,0:T(8,128)S(1)} %copy-done.1), custom_call_target="tpu_custom_call" | custom-call | flops 1 | bytes 1 | tf_op jit(solution)/shard_map/cond/branch_1_fun/pallas_call | solution.py:149
  138.6 5.2 %collective-permute-start.15 = (f32[1040,256]{1,0:T(8,128)}, f32[1040,256]{1,0:T(8,128)}, u32[]{:S(2)}, u32[]{:S(2)}) collective-permute-start(f32[1040,256]{1,0:T(8,128)} %shard_map.21), channel_id=1, source_target_pairs={{0,2},{3,1},{4,6},{7,5},{8,10},{11,9},{12,14},{15,13},{16,18},{19,... | collective-permute-start | bytes 3194888 | tf_op jit(solution)/shard_map/far_block/ppermute | solution.py:330
  146.3 12.7 %shard_map.25 = f32[528,1024]{1,0:T(8,128)S(1)} custom-call(s32[2]{0:T(128)S(1)} %pad_add_fusion.2.role_ref, f32[1024,1024]{1,0:T(8,128)S(1)} %copy-done.2, f32[1024,1024]{1,0:T(8,128)} %get-tuple-element.372.refs_1_, f32[1024,1024]{1,0:T(8,128)} %collective-permute-done.12.refs_1_.refs_2_, f32[1024,1024]{1,0:T(8,128)} %get-tuple-element.374.refs_3_, ...), custom_call_target="tpu_custom_call" | custom-call | flops 1 | bytes 1 | tf_op jit(solution)/shard_map/pallas_call | solution.py:149
  162.7 20.3 %conditional.10 = (f32[1040,512]{1,0:T(8,128)}, f32[528,1024]{1,0:T(8,128)}) conditional(s32[]{:T(128)} %convert_element_type.9, () %tuple.80, (f32[1040,512]{1,0:T(8,128)}, s32[2]{0:T(128)S(1)}, f32[1024,1024]{1,0:T(8,128)S(1)}, f32[1024,1024]{1,0:T(8,128)}, f32[1024,1024]{1,0:T(8,128)}, /*index=5*/f32[1024,1024]{1,0:T(8,128)}, ...), branch_computations={%region_7.8_spmd, %region_8.9_spmd} | conditional | flops 2 | bytes 21495906 | solution.py:167
  170.0 13.0 %branch_1_fun.12 = f32[1040,512]{1,0:T(8,128)} custom-call(s32[2]{0:T(128)S(1)} %get-tuple-element.259.role_ref, f32[1024,1024]{1,0:T(8,128)S(1)} %get-tuple-element.260.refs_0_, f32[1024,1024]{1,0:T(8,128)} %get-tuple-element.261.refs_1_, f32[1024,1024]{1,0:T(8,128)} %get-tuple-element.262.refs_2_, f32[1024,1024]{1,0:T(8,128)} %get-tuple-element.263.refs_3_, ...), custom_call_target="tpu_custom_call" | custom-call | flops 1 | bytes 1 | tf_op jit(solution)/shard_map/cond/branch_1_fun/pallas_call | solution.py:149
  184.3 13.0 %conditional.11 = (f32[1040,256]{1,0:T(8,128)}) conditional(s32[]{:T(128)} %convert_element_type.9, () %tuple.75, (f32[1040,256]{1,0:T(8,128)}, s32[2]{0:T(128)S(1)}, f32[1024,1024]{1,0:T(8,128)}, f32[1024,1024]{1,0:T(8,128)}, f32[1024,1024]{1,0:T(8,128)}, /*index=5*/f32[1024,1024]{1,0:T(8,128)}, f32[1040,512]{1,0:T(8,128)}) %tuple.82), branch_computations={%region_9.10_spmd, %region_10.11_spmd} | conditional | flops 1 | bytes 4259889 | solution.py:167
  187.4 10.0 %branch_1_fun.14 = f32[1040,256]{1,0:T(8,128)} custom-call(s32[2]{0:T(128)S(1)} %get-tuple-element.266.role_ref, f32[1024,1024]{1,0:T(8,128)} %get-tuple-element.267.refs_0_, f32[1024,1024]{1,0:T(8,128)} %get-tuple-element.268.refs_1_, f32[1024,1024]{1,0:T(8,128)} %get-tuple-element.269.refs_2_, f32[1024,1024]{1,0:T(8,128)} %get-tuple-element.270.refs_3_, ...), custom_call_target="tpu_custom_call" | custom-call | flops 1 | bytes 1 | tf_op jit(solution)/shard_map/cond/branch_1_fun/pallas_call | solution.py:149
  198.6 13.0 %conditional.12 = (f32[1040,256]{1,0:T(8,128)}) conditional(s32[]{:T(128)} %convert_element_type.9, () %tuple.83, (f32[1056,256]{1,0:T(8,128)}, s32[2]{0:T(128)S(1)}, f32[1024,1024]{1,0:T(8,128)}, f32[1024,1024]{1,0:T(8,128)}, f32[1024,1024]{1,0:T(8,128)}, /*index=5*/f32[1024,1024]{1,0:T(8,128)}, f32[1040,256]{1,0:T(8,128)}) %tuple.84), branch_computations={%region_11.12_spmd, %region_12.13_spmd} | conditional | flops 1 | bytes 4325425 | solution.py:167
  201.6 10.0 %branch_1_fun.15 = f32[1040,256]{1,0:T(8,128)} custom-call(s32[2]{0:T(128)S(1)} %get-tuple-element.273.role_ref, f32[1024,1024]{1,0:T(8,128)} %get-tuple-element.274.refs_0_, f32[1024,1024]{1,0:T(8,128)} %get-tuple-element.275.refs_1_, f32[1024,1024]{1,0:T(8,128)} %get-tuple-element.276.refs_2_, f32[1024,1024]{1,0:T(8,128)} %get-tuple-element.277.refs_3_, ...), custom_call_target="tpu_custom_call" | custom-call | flops 1 | bytes 1 | tf_op jit(solution)/shard_map/cond/branch_1_fun/pallas_call | solution.py:149
  213.1 17.0 %conditional.13 = (f32[1024,1024]{1,0:T(8,128)}) conditional(s32[]{:T(128)} %convert_element_type.9, () %tuple.85, (s32[]{:T(128)}, f32[528,1024]{1,0:T(8,128)}, f32[1024,1024]{1,0:T(8,128)}, f32[1040,512]{1,0:T(8,128)}, s32[2]{0:T(128)S(1)}, /*index=5*/f32[1024,1024]{1,0:T(8,128)}, f32[1024,1024]{1,0:T(8,128)}, f32[1024,1]{0,1:T(1,128)S(1)}, ...), branch_computations={%region_13.14_spmd, %region_14.22_spmd} | conditional | flops 2 | bytes 34021944 | solution.py:167
  218.7 5.9 %collective-permute-done.9 = f32[1040,512]{1,0:T(8,128)} collective-permute-done((f32[1040,512]{1,0:T(8,128)}, f32[1040,512]{1,0:T(8,128)}, u32[]{:S(2)}, u32[]{:S(2)}) %collective-permute-start.9) | collective-permute-done | bytes 2129952 | tf_op jit(solution)/shard_map/cond/branch_1_fun/far_fold/ppermute | solution.py:326
  225.2 5.0 %conditional = (f32[1024,1024]{1,0:T(8,128)}) conditional(s32[]{:T(128)} %clamp.2, (s32[2]{0:T(128)S(1)}, f32[1024,1024]{1,0:T(8,128)}, f32[1024,1024]{1,0:T(8,128)}, f32[1024,1]{1,0:T(8,128)S(1)}, f32[1,1024]{1,0:T(1,128)S(1)}, /*index=5*/f32[1024,8]{1,0:T(8,128)S(1)}, f32[8,1024]{1,0:T(8,128)S(1)}) %tuple.53, ...), branch_computations={%region_15.15_spmd, %region_16.16_spmd, %region_17.17_spmd, %regio... | conditional | flops 1 | bytes 9 | solution.py:420
  225.2 5.0 %branch_6_fun.1 = f32[1024,1024]{1,0:T(8,128)} custom-call(s32[2]{0:T(128)S(1)} %get-tuple-element.326.flags, f32[1040,512]{1,0:T(8,128)} %get-tuple-element.327.refs_0_, f32[1040,512]{1,0:T(8,128)} %get-tuple-element.328.refs_1_, f32[1024,1]{1,0:T(8,128)S(1)} %get-tuple-element.329.refs_2_, f32[1,1024]{1,0:T(1,128)S(1)} %get-tuple-element.330.refs_3_, ...), custom_call_target="tpu_custom_call" | custom-call | flops 1 | bytes 1 | tf_op jit(solution)/shard_map/cond/branch_1_fun/cond/branch_6_fun/pallas_call | solution.py:225
  230.2 4.6 %collective-permute-done.20 = f32[1040,256]{1,0:T(8,128)} collective-permute-done((f32[1040,256]{1,0:T(8,128)}, f32[1040,256]{1,0:T(8,128)}, u32[]{:S(2)}, u32[]{:S(2)}) %collective-permute-start.20) | collective-permute-done | bytes 1064992 | tf_op jit(solution)/shard_map/far_sum/ppermute | solution.py:326
  234.7 11.7 %conditional.14 = (f32[1024,1024]{1,0:T(8,128)}) conditional(s32[]{:T(128)} %convert_element_type.9, () %tuple.74, (f32[1040,256]{1,0:T(8,128)}, f32[1040,256]{1,0:T(8,128)}, s32[2]{0:T(128)S(1)}, f32[1040,256]{1,0:T(8,128)}, f32[1040,256]{1,0:T(8,128)}, /*index=5*/f32[1024,1]{0,1:T(1,128)S(1)}, f32[1,1024]{1,0:T(1,128)S(1)}, ...), branch_computations={%region_22.23_spmd, %region_23.24_spmd} | conditional | flops 1 | bytes 8593497 | solution.py:167
  241.0 5.4 %branch_1_fun.17 = f32[1024,1024]{1,0:T(8,128)} custom-call(s32[2]{0:T(128)S(1)} %get-tuple-element.348.flags, f32[1040,256]{1,0:T(8,128)} %get-tuple-element.349.refs_0_, f32[1040,256]{1,0:T(8,128)} %get-tuple-element.350.refs_1_, f32[1040,256]{1,0:T(8,128)S(1)} %collective-permute-done.10.refs_2_, ...), custom_call_target="tpu_custom_call", output_to_operand_aliasing={{}: (11, {})} | custom-call | flops 1 | bytes 1 | tf_op jit(solution)/shard_map/cond/branch_1_fun/pallas_call | solution.py:269
  (83 shorter events, 60.6 us)
Async XLA Ops:
  5.8 98.3 %collective-permute-start.13 = (f32[1024,1024]{1,0:T(8,128)}, f32[1024,1024]{1,0:T(8,128)}, u32[]{:S(2)}, u32[]{:S(2)}) collective-permute-start(f32[1024,1024]{1,0:T(8,128)} %get-tuple-element.368.from_ref), channel_id=1, source_target_pairs={{1,2},{2,1},{5,6},{6,5},{9,10},{10,9},{13,14},{14,13},{17,18},{18,... | collective-permute-start | bytes 12582920 | tf_op jit(solution)/shard_map/mid_block/ppermute | solution.py:330
  8.5 95.7 %collective-permute-start.12 = (f32[1024,1024]{1,0:T(8,128)}, f32[1024,1024]{1,0:T(8,128)}, u32[]{:S(2)}, u32[]{:S(2)}) collective-permute-start(f32[1024,1024]{1,0:T(8,128)} %get-tuple-element.369.refs_0_), channel_id=1, source_target_pairs={{0,1},{1,0},{2,3},{3,2},{4,5},{5,4},{6,7},{7,6},{8,9},{9,8},{10,11... | collective-permute-start | bytes 12582920 | tf_op jit(solution)/shard_map/pair_block/ppermute | solution.py:330
  22.5 7.5 %collective-permute-start = (f32[1024,1024]{1,0:T(8,128)}, f32[1024,1024]{1,0:T(8,128)}, u32[]{:S(2)}, u32[]{:S(2)}) collective-permute-start(f32[1024,1024]{1,0:T(8,128)} %get-tuple-element.235.refs_0_.refs_2_), channel_id=1, source_target_pairs={{0,4},{1,5},{2,6},{3,7},{4,0},{5,1},{6,2},{7,3},{8,12},{9,13},{10,... | collective-permute-start | bytes 12582920 | tf_op jit(solution)/shard_map/cond/branch_1_fun/own_other/ppermute | solution.py:326
  51.3 94.9 %collective-permute-start.17 = (f32[1024,1024]{1,0:T(8,128)}, f32[1024,1024]{1,0:T(8,128)}, u32[]{:S(2)}, u32[]{:S(2)}) collective-permute-start(f32[1024,1024]{1,0:T(8,128)} %get-tuple-element.373), channel_id=1, source_target_pairs={{8,0},{13,5},{2,10},{7,15},{24,16},{29,21},{18,26},{23,31}} | collective-permute-start | bytes 12582920 | tf_op jit(solution)/shard_map/own_lane/ppermute | solution.py:326
  54.0 50.1 %collective-permute-start.14 = (f32[16,1024]{1,0:T(8,128)S(1)}, f32[16,1024]{1,0:T(8,128)S(1)}, u32[]{:S(2)}, u32[]{:S(2)}) collective-permute-start(f32[16,1024]{1,0:T(8,128)S(1)} %maximum_maximum_fusion), channel_id=1, source_target_pairs={{1,4},{2,8},{3,12},{4,1},{6,9},{7,13},{8,2},{9,6},{11,14},{12,3},{... | collective-permute-start | bytes 196616 | tf_op jit(solution)/shard_map/moments/ppermute | solution.py:326
  104.2 58.5 %collective-permute-start.16 = (f32[1040,512]{1,0:T(8,128)}, f32[1040,512]{1,0:T(8,128)}, u32[]{:S(2)}, u32[]{:S(2)}) collective-permute-start(f32[1040,512]{1,0:T(8,128)} %shard_map.24), channel_id=1, source_target_pairs={{0,2},{3,1},{4,6},{7,5},{8,10},{11,9},{12,14},{15,13},{16,18},{19,... | collective-permute-start | bytes 6389768 | tf_op jit(solution)/shard_map/far_block/ppermute | solution.py:330
  107.6 14.2 %collective-permute-start.1 = (f32[1024,1024]{1,0:T(8,128)}, f32[1024,1024]{1,0:T(8,128)}, u32[]{:S(2)}, u32[]{:S(2)}) collective-permute-start(f32[1024,1024]{1,0:T(8,128)} %get-tuple-element.254.refs_1_), channel_id=1, source_target_pairs={{0,4},{1,5},{2,6},{3,7},{4,0},{5,1},{6,2},{7,3},{8,12},{9,13},{10,... | collective-permute-start | bytes 12582920 | tf_op jit(solution)/shard_map/cond/branch_1_fun/pair_other/ppermute | solution.py:326
  108.8 13.1 %collective-permute-start.2 = (f32[1024,1024]{1,0:T(8,128)}, f32[1024,1024]{1,0:T(8,128)}, u32[]{:S(2)}, u32[]{:S(2)}) collective-permute-start(f32[1024,1024]{1,0:T(8,128)} %get-tuple-element.256.refs_2_), channel_id=1, source_target_pairs={{0,4},{1,5},{2,6},{3,7},{4,0},{5,1},{6,2},{7,3},{8,12},{9,13},{10,... | collective-permute-start | bytes 12582920 | tf_op jit(solution)/shard_map/cond/branch_1_fun/mid_other/ppermute | solution.py:326
  137.2 75.9 %collective-permute-start.22 = (f32[1024,1024]{1,0:T(8,128)}, f32[1024,1024]{1,0:T(8,128)}, u32[]{:S(2)}, u32[]{:S(2)}) collective-permute-start(f32[1024,1024]{1,0:T(8,128)} %get-tuple-element.375.refs_4_), channel_id=1, source_target_pairs={{1,9},{14,6},{5,8},{10,7},{13,12},{2,3},{17,25},{30,22},{21,24},{2... | collective-permute-start | bytes 12582920 | tf_op jit(solution)/shard_map/mid_sum/ppermute | solution.py:326
  138.6 45.7 %collective-permute-start.15 = (f32[1040,256]{1,0:T(8,128)}, f32[1040,256]{1,0:T(8,128)}, u32[]{:S(2)}, u32[]{:S(2)}) collective-permute-start(f32[1040,256]{1,0:T(8,128)} %shard_map.21), channel_id=1, source_target_pairs={{0,2},{3,1},{4,6},{7,5},{8,10},{11,9},{12,14},{15,13},{16,18},{19,... | collective-permute-start | bytes 3194888 | tf_op jit(solution)/shard_map/far_block/ppermute | solution.py:330
  143.7 54.9 %collective-permute-start.19 = (f32[1056,256]{1,0:T(8,128)S(1)}, f32[1056,256]{1,0:T(8,128)}, u32[]{:S(2)}, u32[]{:S(2)}) collective-permute-start(f32[1056,256]{1,0:T(8,128)S(1)} %shard_map.26), channel_id=1, source_target_pairs={{0,2},{3,1},{4,6},{7,5},{8,10},{11,9},{12,14},{15,13},{16,18},{19,... | collective-permute-start | bytes 3244040 | tf_op jit(solution)/shard_map/far_block/ppermute | solution.py:330
  159.0 54.1 %collective-permute-start.21 = (f32[528,1024]{1,0:T(8,128)S(1)}, f32[528,1024]{1,0:T(8,128)}, u32[]{:S(2)}, u32[]{:S(2)}) collective-permute-start(f32[528,1024]{1,0:T(8,128)S(1)} %shard_map.25), channel_id=1, source_target_pairs={{12,4},{8,0},{9,1},{13,5},{6,14},{2,10},{3,11},{7,15},{28,20},{24,... | collective-permute-start | bytes 6488072 | tf_op jit(solution)/shard_map/pair_lane/ppermute | solution.py:326
  162.7 6.9 %collective-permute-start.3 = (f32[1040,512]{1,0:T(8,128)}, f32[1040,512]{1,0:T(8,128)S(1)}, u32[]{:S(2)}, u32[]{:S(2)}) collective-permute-start(f32[1040,512]{1,0:T(8,128)} %get-tuple-element.264.refs_4_), channel_id=1, source_target_pairs={{0,4},{1,5},{2,6},{3,7},{4,0},{5,1},{6,2},{7,3},{8,12},{9,13},{10,... | collective-permute-start | bytes 6389768 | tf_op jit(solution)/shard_map/cond/branch_1_fun/far_other/ppermute | solution.py:326
  169.6 13.4 %collective-permute-start.4 = (f32[528,1024]{1,0:T(8,128)S(1)}, f32[528,1024]{1,0:T(8,128)}, u32[]{:S(2)}, u32[]{:S(2)}) collective-permute-start(f32[528,1024]{1,0:T(8,128)S(1)} %branch_1_fun.13), channel_id=1, source_target_pairs={{0,4},{1,5},{2,6},{3,7},{4,0},{5,1},{6,2},{7,3},{8,12},{9,13},{10,... | collective-permute-start | bytes 6488072 | tf_op jit(solution)/shard_map/cond/branch_1_fun/pair_fold/ppermute | solution.py:326
  183.0 30.1 %collective-permute-start.23 = (f32[1040,512]{1,0:T(8,128)}, f32[1040,512]{1,0:T(8,128)}, u32[]{:S(2)}, u32[]{:S(2)}) collective-permute-start(f32[1040,512]{1,0:T(8,128)} %get-tuple-element.376), channel_id=1, source_target_pairs={{5,13},{10,2},{1,12},{14,3},{9,8},{6,7},{21,29},{26,18},{17,28},{3... | collective-permute-start | bytes 6389768 | tf_op jit(solution)/shard_map/far_sum/ppermute | solution.py:326
  184.3 3.0 %collective-permute-start.5 = (f32[1040,256]{1,0:T(8,128)}, f32[1040,256]{1,0:T(8,128)S(1)}, u32[]{:S(2)}, u32[]{:S(2)}) collective-permute-start(f32[1040,256]{1,0:T(8,128)} %get-tuple-element.271.refs_4_), channel_id=1, source_target_pairs={{0,4},{1,5},{2,6},{3,7},{4,0},{5,1},{6,2},{7,3},{8,12},{9,13},{10,... | collective-permute-start | bytes 3194888 | tf_op jit(solution)/shard_map/cond/branch_1_fun/far_other/ppermute | solution.py:326
  197.3 37.4 %collective-permute-start.18 = (f32[1040,256]{1,0:T(8,128)}, f32[1040,256]{1,0:T(8,128)}, u32[]{:S(2)}, u32[]{:S(2)}) collective-permute-start(f32[1040,256]{1,0:T(8,128)} %get-tuple-element.476), channel_id=1, source_target_pairs={{5,13},{10,2},{1,12},{14,3},{9,8},{6,7},{21,29},{26,18},{17,28},{3... | collective-permute-start | bytes 3194888 | tf_op jit(solution)/shard_map/far_sum/ppermute | solution.py:326
  198.6 3.0 %collective-permute-start.6 = (f32[1056,256]{1,0:T(8,128)}, f32[1056,256]{1,0:T(8,128)S(1)}, u32[]{:S(2)}, u32[]{:S(2)}) collective-permute-start(f32[1056,256]{1,0:T(8,128)} %get-tuple-element.278.refs_4_), channel_id=1, source_target_pairs={{0,4},{1,5},{2,6},{3,7},{4,0},{5,1},{6,2},{7,3},{8,12},{9,13},{10,... | collective-permute-start | bytes 3244040 | tf_op jit(solution)/shard_map/cond/branch_1_fun/far_other/ppermute | solution.py:326
  211.6 23.1 %collective-permute-start.20 = (f32[1040,256]{1,0:T(8,128)}, f32[1040,256]{1,0:T(8,128)}, u32[]{:S(2)}, u32[]{:S(2)}) collective-permute-start(f32[1040,256]{1,0:T(8,128)} %get-tuple-element.477), channel_id=1, source_target_pairs={{5,13},{10,2},{1,12},{14,3},{9,8},{6,7},{21,29},{26,18},{17,28},{3... | collective-permute-start | bytes 3194888 | tf_op jit(solution)/shard_map/far_sum/ppermute | solution.py:326
  213.1 12.1 %collective-permute-start.8 = (f32[1024,1024]{1,0:T(8,128)}, f32[1024,1024]{1,0:T(8,128)}, u32[]{:S(2)}, u32[]{:S(2)}) collective-permute-start(f32[1024,1024]{1,0:T(8,128)} %get-tuple-element.345), channel_id=1, source_target_pairs={{12,8},{3,7},{28,24},{19,23}} | collective-permute-start | bytes 12582920 | tf_op jit(solution)/shard_map/cond/branch_1_fun/mid_fold/ppermute | solution.py:326
  217.0 8.2 %collective-permute-start.7 = (f32[528,1024]{1,0:T(8,128)}, f32[528,1024]{1,0:T(8,128)}, u32[]{:S(2)}, u32[]{:S(2)}) collective-permute-start(f32[528,1024]{1,0:T(8,128)} %get-tuple-element.342), channel_id=1, source_target_pairs={{0,4},{1,5},{2,6},{3,7},{4,0},{5,1},{6,2},{7,3},{8,12},{9,13},{10,... | collective-permute-start | bytes 6488072 | tf_op jit(solution)/shard_map/cond/branch_1_fun/pair_fold/ppermute | solution.py:326
  217.0 7.6 %collective-permute-start.9 = (f32[1040,512]{1,0:T(8,128)}, f32[1040,512]{1,0:T(8,128)}, u32[]{:S(2)}, u32[]{:S(2)}) collective-permute-start(f32[1040,512]{1,0:T(8,128)} %get-tuple-element.347), channel_id=1, source_target_pairs={{8,12},{7,3},{24,28},{23,19}} | collective-permute-start | bytes 6389768 | tf_op jit(solution)/shard_map/cond/branch_1_fun/far_fold/ppermute | solution.py:326
  234.7 4.8 %collective-permute-start.11 = (f32[1040,256]{1,0:T(8,128)}, f32[1040,256]{1,0:T(8,128)S(1)}, u32[]{:S(2)}, u32[]{:S(2)}) collective-permute-start(f32[1040,256]{1,0:T(8,128)} %get-tuple-element.352.refs_4_), channel_id=1, source_target_pairs={{8,12},{7,3},{24,28},{23,19}} | collective-permute-start | bytes 3194888 | tf_op jit(solution)/shard_map/cond/branch_1_fun/far_fold/ppermute | solution.py:326
  236.0 5.0 %collective-permute-start.10 = (f32[1040,256]{1,0:T(8,128)}, f32[1040,256]{1,0:T(8,128)S(1)}, u32[]{:S(2)}, u32[]{:S(2)}) collective-permute-start(f32[1040,256]{1,0:T(8,128)} %get-tuple-element.350.refs_1_), channel_id=1, source_target_pairs={{8,12},{7,3},{24,28},{23,19}} | collective-permute-start | bytes 3194888 | tf_op jit(solution)/shard_map/cond/branch_1_fun/far_fold/ppermute | solution.py:326
  (5 other events, 10.4 us)
